TPU v7x, 128 devices: a whole 4x4x4 slice. The times are simulated.
128 devices in a mesh: leaf: 64 (over x, y, z), rhs: 2 (over core).
Axes of the slice: x: 4, y: 4, z: 4, core: 2. Of those that a mesh axis runs over, the one named last changes fastest.
Arguments:
- points: bfloat16 [8192, 8, 256], P('leaf'), may hold values from -5 to 5
- values: bfloat16 [8192, 16, 256], P('leaf', 'rhs'), parts along dimension 1, may hold values from -6 to 6
- counts: int32 [8192], P('leaf'), may hold values from 128 to 256
- leaf_basis: bfloat16 [8192, 64, 256], P('leaf'), may hold values from -0.375 to 0.375
- transfer: bfloat16 [8192, 64, 64], P('leaf'), may hold values from -0.5 to 0.5
- leaf_skeleton: bfloat16 [8192, 8, 64], P('leaf'), may hold values from -5 to 5
- upper_skeleton: bfloat16 [4096, 8, 64], P('leaf'), may hold values from -5 to 5
- near_list: int32 [8192, 6], P('leaf'), may hold values from 0 to 8191, as said below
- far_owner: int32 [8192, 8], P('leaf'), may hold values from 0 to 63, all different within a row; in each aligned block of 128 rows (0 to 127, 128 to 255, ...) at most 32 rows name the same one
- far_local: int32 [8192, 8], P('leaf'), may hold values from 0 to 127
- upper_owner: int32 [4096, 8], P('leaf'), may hold values from 0 to 63, all different within a row; in each aligned block of 64 rows (0 to 63, 64 to 127, ...) at most 16 rows name the same one
- upper_local: int32 [4096, 8], P('leaf'), may hold values from 0 to 63
Outputs:
- product: float32 [8192, 16, 256], P('leaf', 'rhs'), parts along dimension 1
There are 2 independent parts, one for each index of `rhs`. A program takes and returns all parts, laid end to end along the dimension named above; an argument that names none is the same for every part. Nothing has to cross between parts.
Inputs may be any that keep to these rules, and one draw needn't show every extreme that they name: `near_list`: entry 0 of leaf l's list is l itself; every entry lies within 4 leaves of the block of 128 leaves that holds l, and some lists reach both ends of that range where the grid of leaves allows. `far_owner`: A row's 8 owners are different; among the rows of one device (aligned blocks of 128 rows) no owner is named by more than 32 entries, and some owner by exactly that many. `upper_owner`: A row's 8 owners are different; among the rows of one device (aligned blocks of 64 rows) no owner is named by more than 16 entries, and some owner by exactly that many.
All inputs are finite; a program needn't handle non-finite values.
Results may differ from a plain program's by a relative error of at most 0.0032.
Values may be sent and summed in bfloat16 or wider, within the bound.
No kernel may reach another device: no remote copies, remote signals or barrier semaphores. Data moves between devices by JAX's collectives and lax.ppermute only.
A program may use at most 128 MiB of HBM per device.

v0:
```python
import math

import jax
import jax.numpy as jnp
from jax import lax
from jax.sharding import PartitionSpec as P

DIM = 8
HALO = 4


SQRT_THREE = 1.7320508075688772
LENGTH_SCALE = 1.5


def with_halo(cells, sides, width):
    for axis, dim in sides:
        count = lax.axis_size(axis)
        ends = count - 1
        head = lax.slice_in_dim(cells, 0, width, axis=dim)
        tail = lax.slice_in_dim(cells, cells.shape[dim] - width, cells.shape[dim], axis=dim)
        cells = jnp.concatenate(
            [
                lax.ppermute(tail, axis, [(i, (i + 1) % count) for i in range(ends)]),
                cells,
                lax.ppermute(head, axis, [((i + 1) % count, i) for i in range(ends)]),
            ],
            axis=dim,
        )
    return cells


def matern(targets, sources):
    square = 0.0
    for coord in range(targets.shape[-2]):
        offset = targets[..., coord, :, None] - sources[..., coord, None, :]
        square = square + offset * offset
    scaled = SQRT_THREE / LENGTH_SCALE * jnp.sqrt(square)
    return (1.0 + scaled) * jnp.exp(-scaled)


def far_sum(target_skel, source_skel, source_coef):
    kernel = matern(
        target_skel.astype(jnp.float32)[:, None], source_skel.astype(jnp.float32)
    ).astype(jnp.bfloat16)
    return jnp.einsum("nfcb,nfab->nca", source_coef, kernel, preferred_element_type=jnp.float32)


def slot_table(owner, local, owners, capacity):
    flat_owner = owner.reshape(-1)
    flat_local = local.reshape(-1)
    owner_hits = (flat_owner[:, None] == jnp.arange(owners, dtype=jnp.int32)[None, :]).astype(
        jnp.int32
    )
    before = jnp.cumsum(owner_hits, axis=0) - owner_hits
    slot_index = jnp.sum(before * owner_hits, axis=1)
    wanted = jnp.zeros((owners, capacity), jnp.int32).at[flat_owner, slot_index].set(flat_local)
    return (wanted, flat_owner, slot_index)


def body(
    points,
    values,
    counts,
    leaf_basis,
    transfer,
    leaf_skeleton,
    upper_skeleton,
    near_list,
    far_owner,
    far_local,
    upper_owner,
    upper_local,
):
    leaf_dev = points.shape[0]
    leaf_size = points.shape[2]
    columns = values.shape[1]
    rank = leaf_basis.shape[1]
    far_count = far_owner.shape[1]
    par_dev = leaf_dev // 2
    owners = lax.axis_size("leaf")
    point_live = lax.broadcasted_iota(jnp.int32, (leaf_dev, leaf_size), 1) < counts[:, None]
    masked = jnp.where(point_live[:, None, :], values, jnp.zeros_like(values))
    leaf_coef = jnp.einsum(
        "lcp,lkp->lck", masked, leaf_basis, preferred_element_type=jnp.float32
    ).astype(jnp.bfloat16)
    child_coef = leaf_coef.reshape(par_dev, 2, columns, rank)
    child_transfer = transfer.reshape(par_dev, 2, rank, rank)
    upper_coef = jnp.einsum(
        "pjck,pjkm->pcm", child_coef, child_transfer, preferred_element_type=jnp.float32
    ).astype(jnp.bfloat16)
    bundle = jnp.concatenate([points, masked], axis=1)
    extended = with_halo(bundle, (("leaf", 0),), HALO)
    first_leaf = lax.axis_index("leaf") * leaf_dev - HALO
    near_count = near_list.shape[1]
    group_size = math.gcd(leaf_dev, 8)
    turns = leaf_dev // group_size
    local_ids = (near_list - first_leaf).reshape(turns, group_size, near_count)

    def near_block(pieces):
        target_points, chosen = pieces
        source_rows = extended[chosen]
        kernel = matern(
            target_points.astype(jnp.float32)[:, None], source_rows[:, :, :DIM].astype(jnp.float32)
        ).astype(jnp.bfloat16)
        return jnp.einsum(
            "gjcs,gjts->gct", source_rows[:, :, DIM:], kernel, preferred_element_type=jnp.float32
        )

    near_part = lax.map(near_block, (points.reshape(turns, group_size, DIM, leaf_size), local_ids))
    near_part = near_part.reshape(leaf_dev, columns, leaf_size)
    leaf_rows = leaf_coef.reshape(leaf_dev, columns * rank)
    leaf_skel_rows = leaf_skeleton.reshape(leaf_dev, DIM * rank)
    capacity = max(2, 2 * leaf_dev * far_count // owners)
    wanted, flat_owner, slot_index = slot_table(far_owner, far_local, owners, capacity)
    asked = lax.all_to_all(wanted, "leaf", split_axis=0, concat_axis=0, tiled=True)
    got_coef = lax.all_to_all(leaf_rows[asked], "leaf", split_axis=0, concat_axis=0, tiled=True)
    got_skel = lax.all_to_all(
        leaf_skel_rows[asked], "leaf", split_axis=0, concat_axis=0, tiled=True
    )
    picked_coef = got_coef[flat_owner, slot_index]
    picked_skel = got_skel[flat_owner, slot_index]
    leaf_far = far_sum(
        leaf_skeleton,
        picked_skel.reshape(leaf_dev, far_count, DIM, rank),
        picked_coef.reshape(leaf_dev, far_count, columns, rank),
    )
    upper_rows = upper_coef.reshape(par_dev, columns * rank)
    upper_skel_rows = upper_skeleton.reshape(par_dev, DIM * rank)
    upper_capacity = max(2, 2 * par_dev * far_count // owners)
    upper_wanted, upper_flat, upper_slot = slot_table(
        upper_owner, upper_local, owners, upper_capacity
    )
    asked = lax.all_to_all(upper_wanted, "leaf", split_axis=0, concat_axis=0, tiled=True)
    got_upper = lax.all_to_all(upper_rows[asked], "leaf", split_axis=0, concat_axis=0, tiled=True)
    got_upper_skel = lax.all_to_all(
        upper_skel_rows[asked], "leaf", split_axis=0, concat_axis=0, tiled=True
    )
    chosen_coef = got_upper[upper_flat, upper_slot]
    chosen_skel = got_upper_skel[upper_flat, upper_slot]
    upper_field = far_sum(
        upper_skeleton,
        chosen_skel.reshape(par_dev, far_count, DIM, rank),
        chosen_coef.reshape(par_dev, far_count, columns, rank),
    ).astype(jnp.bfloat16)
    spread = jnp.repeat(upper_field, 2, axis=0)
    leaf_field = (
        leaf_far + jnp.einsum("lcm,lkm->lck", spread, transfer, preferred_element_type=jnp.float32)
    ).astype(jnp.bfloat16)
    far_part = jnp.einsum(
        "lck,lkp->lcp", leaf_field, leaf_basis, preferred_element_type=jnp.float32
    )
    return jnp.where(point_live[:, None, :], far_part + near_part, 0.0)


def solution(mesh):
    return jax.shard_map(
        body,
        mesh=mesh,
        in_specs=(
            P("leaf", None, None),
            P("leaf", "rhs", None),
            P("leaf"),
            P("leaf", None, None),
            P("leaf", None, None),
            P("leaf", None, None),
            P("leaf", None, None),
            P("leaf", None),
            P("leaf", None),
            P("leaf", None),
            P("leaf", None),
            P("leaf", None),
        ),
        out_specs=P("leaf", "rhs", None),
        check_vma=False,
    )
```

profile of v0, /device:TPU:1, one launch (start us, length us, event | category | flops | bytes accessed | tf_op | source)
XLA Modules:
  0.0 652.2 jit_solution(9136574727650140852)
XLA Ops:
  4.3 25.2 %scatter_fusion = s32[64,16]{0,1:T(8,128)S(1)} fusion(s32[64,16]{0,1:T(8,128)S(1)} %broadcast.187, s32[512]{0:T(512)S(1)} %bitcast.214, s32[512]{0:T(512)S(1)} %reshape.402), kind=kCustom, calls=%fused_computation.9 | custom fusion | bytes 10240 | tf_op jit(solution)/shard_map/scatter | solution.py:57
  30.2 12.0 %all-to-all-start.3 = ((s32[64,1,16]{2,1,0:T(1,128)}), s32[64,1,16]{2,1,0:T(1,128)S(1)}, u32[]{:S(2)}, u32[]{:S(2)}) async-start(s32[64,1,16]{2,1,0:T(1,128)} %copy.151), calls=%async_computation.3 | async-start | bytes 65536 | tf_op jit(solution)/shard_map/all_to_all | solution.py:134
  43.1 3.5 collective-permute-start
  48.3 18.0 %reduce-window.14 = s32[64,8,128]{2,1,0:T(8,128)S(1)} reduce-window(s32[64,8,128]{2,1,0:T(8,128)S(1)} %fusion.18, s32[]{:T(128)} %copy.202), window={size=1x1x128 pad=0_0x0_0x127_0}, to_apply=%region_0.1 | reduce-window | flops 8323072 | bytes 524292 | tf_op jit(solution)/shard_map/reduce-window
  68.1 4.3 scatter_custom_fusion.1
  73.2 10.3 %all-to-all-start = ((s32[64,1,32]{2,1,0:T(1,128)}), s32[64,1,32]{2,1,0:T(1,128)S(1)}, u32[]{:S(2)}, u32[]{:S(2)}) async-start(s32[64,1,32]{2,1,0:T(1,128)} %copy.134), calls=%async_computation | async-start | bytes 65536 | tf_op jit(solution)/shard_map/all_to_all | solution.py:116
  83.6 5.1 gather_fusion.7
  88.7 3.1 all-to-all-done
  92.4 6.7 %all-to-all-start.5 = ((bf16[64,16,512]{2,1,0:T(8,128)(2,1)}), bf16[64,16,512]{2,1,0:T(8,128)(2,1)S(1)}, u32[]{:S(2)}, u32[]{:S(2)}) async-start(bf16[64,16,512]{2,1,0:T(8,128)(2,1)} %bitcast.75), calls=%async_computation.5 | async-start | bytes 2097152 | tf_op jit(solution)/shard_map/all_to_all | solution.py:136
  99.1 4.1 convolution_convert_fusion
  103.2 4.0 copy.145
  107.2 2.0 copy.127
  124.8 5.1 gather_fusion.5
  129.9 10.0 %all-to-all-start.4 = ((bf16[64,16,512]{2,1,0:T(8,128)(2,1)}), bf16[64,16,512]{2,1,0:T(8,128)(2,1)S(1)}, u32[]{:S(2)}, u32[]{:S(2)}) async-start(bf16[64,16,512]{2,1,0:T(8,128)(2,1)} %bitcast.220), calls=%async_computation.4 | async-start | bytes 2097152 | tf_op jit(solution)/shard_map/all_to_all | solution.py:135
  141.8 9.2 %gather_fusion.3 = bf16[2048,512]{1,0:T(8,128)(2,1)} fusion(bf16[128,512]{1,0:T(8,128)(2,1)S(1)} %copy.137, s32[2048]{0:T(1024)S(1)} %broadcast_clamp_fusion), kind=kCustom, calls=%fused_computation.3 | custom fusion | bytes 4202496 | tf_op jit(solution)/shard_map/gather | solution.py:119
  151.0 9.2 %gather_fusion.1 = bf16[2048,512]{1,0:T(8,128)(2,1)} fusion(bf16[128,512]{1,0:T(8,128)(2,1)S(1)} %copy.135, s32[2048]{0:T(1024)S(1)} %broadcast_clamp_fusion), kind=kCustom, calls=%fused_computation.1 | custom fusion | bytes 4202496 | tf_op jit(solution)/shard_map/gather | solution.py:117
  160.2 1.9 pad_maximum_fusion
  162.2 9.9 %all-to-all-start.2 = ((bf16[64,32,512]{2,1,0:T(8,128)(2,1)}), bf16[64,32,512]{2,1,0:T(8,128)(2,1)}, u32[]{:S(2)}, u32[]{:S(2)}) async-start(bf16[64,32,512]{2,1,0:T(8,128)(2,1)} %bitcast.219), calls=%async_computation.2 | async-start | bytes 4194304 | tf_op jit(solution)/shard_map/all_to_all | solution.py:118
  172.1 330.8 %while.10 = (s32[]{:T(128)}, f32[16,8,8,256]{3,2,1,0:T(8,128)}, s32[16,8,6]{1,0,2:T(8,128)}, bf16[136,16,256]{2,1,0:T(8,128)(2,1)}, bf16[16,8,8,256]{3,2,1,0:T(8,128)(2,1)S(1)}, /*index=5*/s32[]{:T(128)}) while((s32[]{:T(128)}, f32[16,8,8,256]{3,2,1,0:T(8,128)}, s32[16,8,6]{1,0,2:T(8,128)}, bf16[136,16,256]{2,1,0:T(8,128)(2,1)}, ...), condition=%wide.region_9.10_spmd, body=%wide.region_8.9_spmd.sunk | while | flops 138527888 | bytes 4102221 | solution.py:110
  175.4 17.4 %fusion.52 = f32[16,8,8,256]{3,2,1,0:T(8,128)} fusion(f32[16,8,8,256]{3,2,1,0:T(8,128)} %get-tuple-element.207, s32[]{:T(128)} %get-tuple-element.206, f32[8,6,256]{2,1,0:T(8,128)S(1)} %get-tuple-element.178, f32[8,256]{1,0:T(8,128)S(1)} %get-tuple-element.179, f32[8,6,256]{2,1,0:T(8,128)S(1)} %get-tuple-element.180, ...), kind=kOutput, calls=%fused_computation.14.clone.1 | convolution fusion | flops 138412032 | bytes 852480 | tf_op jit(solution)/shard_map/while/body/eval_jaxpr/gjcs,gjts->gct/dot_general | solution.py:106
  193.8 1.8 gather_fusion
  196.1 17.4 %fusion.52 = f32[16,8,8,256]{3,2,1,0:T(8,128)} fusion(f32[16,8,8,256]{3,2,1,0:T(8,128)} %get-tuple-element.207, s32[]{:T(128)} %get-tuple-element.206, f32[8,6,256]{2,1,0:T(8,128)S(1)} %get-tuple-element.178, f32[8,256]{1,0:T(8,128)S(1)} %get-tuple-element.179, f32[8,6,256]{2,1,0:T(8,128)S(1)} %get-tuple-element.180, ...), kind=kOutput, calls=%fused_computation.14.clone.1 | convolution fusion | flops 138412032 | bytes 852480 | tf_op jit(solution)/shard_map/while/body/eval_jaxpr/gjcs,gjts->gct/dot_general | solution.py:106
  216.7 17.4 %fusion.52 = f32[16,8,8,256]{3,2,1,0:T(8,128)} fusion(f32[16,8,8,256]{3,2,1,0:T(8,128)} %get-tuple-element.207, s32[]{:T(128)} %get-tuple-element.206, f32[8,6,256]{2,1,0:T(8,128)S(1)} %get-tuple-element.178, f32[8,256]{1,0:T(8,128)S(1)} %get-tuple-element.179, f32[8,6,256]{2,1,0:T(8,128)S(1)} %get-tuple-element.180, ...), kind=kOutput, calls=%fused_computation.14.clone.1 | convolution fusion | flops 138412032 | bytes 852480 | tf_op jit(solution)/shard_map/while/body/eval_jaxpr/gjcs,gjts->gct/dot_general | solution.py:106
  237.4 17.4 %fusion.52 = f32[16,8,8,256]{3,2,1,0:T(8,128)} fusion(f32[16,8,8,256]{3,2,1,0:T(8,128)} %get-tuple-element.207, s32[]{:T(128)} %get-tuple-element.206, f32[8,6,256]{2,1,0:T(8,128)S(1)} %get-tuple-element.178, f32[8,256]{1,0:T(8,128)S(1)} %get-tuple-element.179, f32[8,6,256]{2,1,0:T(8,128)S(1)} %get-tuple-element.180, ...), kind=kOutput, calls=%fused_computation.14.clone.1 | convolution fusion | flops 138412032 | bytes 852480 | tf_op jit(solution)/shard_map/while/body/eval_jaxpr/gjcs,gjts->gct/dot_general | solution.py:106
  258.1 17.4 %fusion.52 = f32[16,8,8,256]{3,2,1,0:T(8,128)} fusion(f32[16,8,8,256]{3,2,1,0:T(8,128)} %get-tuple-element.207, s32[]{:T(128)} %get-tuple-element.206, f32[8,6,256]{2,1,0:T(8,128)S(1)} %get-tuple-element.178, f32[8,256]{1,0:T(8,128)S(1)} %get-tuple-element.179, f32[8,6,256]{2,1,0:T(8,128)S(1)} %get-tuple-element.180, ...), kind=kOutput, calls=%fused_computation.14.clone.1 | convolution fusion | flops 138412032 | bytes 852480 | tf_op jit(solution)/shard_map/while/body/eval_jaxpr/gjcs,gjts->gct/dot_general | solution.py:106
  278.7 17.4 %fusion.52 = f32[16,8,8,256]{3,2,1,0:T(8,128)} fusion(f32[16,8,8,256]{3,2,1,0:T(8,128)} %get-tuple-element.207, s32[]{:T(128)} %get-tuple-element.206, f32[8,6,256]{2,1,0:T(8,128)S(1)} %get-tuple-element.178, f32[8,256]{1,0:T(8,128)S(1)} %get-tuple-element.179, f32[8,6,256]{2,1,0:T(8,128)S(1)} %get-tuple-element.180, ...), kind=kOutput, calls=%fused_computation.14.clone.1 | convolution fusion | flops 138412032 | bytes 852480 | tf_op jit(solution)/shard_map/while/body/eval_jaxpr/gjcs,gjts->gct/dot_general | solution.py:106
  299.4 17.4 %fusion.52 = f32[16,8,8,256]{3,2,1,0:T(8,128)} fusion(f32[16,8,8,256]{3,2,1,0:T(8,128)} %get-tuple-element.207, s32[]{:T(128)} %get-tuple-element.206, f32[8,6,256]{2,1,0:T(8,128)S(1)} %get-tuple-element.178, f32[8,256]{1,0:T(8,128)S(1)} %get-tuple-element.179, f32[8,6,256]{2,1,0:T(8,128)S(1)} %get-tuple-element.180, ...), kind=kOutput, calls=%fused_computation.14.clone.1 | convolution fusion | flops 138412032 | bytes 852480 | tf_op jit(solution)/shard_map/while/body/eval_jaxpr/gjcs,gjts->gct/dot_general | solution.py:106
  320.1 17.4 %fusion.52 = f32[16,8,8,256]{3,2,1,0:T(8,128)} fusion(f32[16,8,8,256]{3,2,1,0:T(8,128)} %get-tuple-element.207, s32[]{:T(128)} %get-tuple-element.206, f32[8,6,256]{2,1,0:T(8,128)S(1)} %get-tuple-element.178, f32[8,256]{1,0:T(8,128)S(1)} %get-tuple-element.179, f32[8,6,256]{2,1,0:T(8,128)S(1)} %get-tuple-element.180, ...), kind=kOutput, calls=%fused_computation.14.clone.1 | convolution fusion | flops 138412032 | bytes 852480 | tf_op jit(solution)/shard_map/while/body/eval_jaxpr/gjcs,gjts->gct/dot_general | solution.py:106
  340.7 17.4 %fusion.52 = f32[16,8,8,256]{3,2,1,0:T(8,128)} fusion(f32[16,8,8,256]{3,2,1,0:T(8,128)} %get-tuple-element.207, s32[]{:T(128)} %get-tuple-element.206, f32[8,6,256]{2,1,0:T(8,128)S(1)} %get-tuple-element.178, f32[8,256]{1,0:T(8,128)S(1)} %get-tuple-element.179, f32[8,6,256]{2,1,0:T(8,128)S(1)} %get-tuple-element.180, ...), kind=kOutput, calls=%fused_computation.14.clone.1 | convolution fusion | flops 138412032 | bytes 852480 | tf_op jit(solution)/shard_map/while/body/eval_jaxpr/gjcs,gjts->gct/dot_general | solution.py:106
  361.4 17.4 %fusion.52 = f32[16,8,8,256]{3,2,1,0:T(8,128)} fusion(f32[16,8,8,256]{3,2,1,0:T(8,128)} %get-tuple-element.207, s32[]{:T(128)} %get-tuple-element.206, f32[8,6,256]{2,1,0:T(8,128)S(1)} %get-tuple-element.178, f32[8,256]{1,0:T(8,128)S(1)} %get-tuple-element.179, f32[8,6,256]{2,1,0:T(8,128)S(1)} %get-tuple-element.180, ...), kind=kOutput, calls=%fused_computation.14.clone.1 | convolution fusion | flops 138412032 | bytes 852480 | tf_op jit(solution)/shard_map/while/body/eval_jaxpr/gjcs,gjts->gct/dot_general | solution.py:106
  382.1 17.4 %fusion.52 = f32[16,8,8,256]{3,2,1,0:T(8,128)} fusion(f32[16,8,8,256]{3,2,1,0:T(8,128)} %get-tuple-element.207, s32[]{:T(128)} %get-tuple-element.206, f32[8,6,256]{2,1,0:T(8,128)S(1)} %get-tuple-element.178, f32[8,256]{1,0:T(8,128)S(1)} %get-tuple-element.179, f32[8,6,256]{2,1,0:T(8,128)S(1)} %get-tuple-element.180, ...), kind=kOutput, calls=%fused_computation.14.clone.1 | convolution fusion | flops 138412032 | bytes 852480 | tf_op jit(solution)/shard_map/while/body/eval_jaxpr/gjcs,gjts->gct/dot_general | solution.py:106
  402.8 17.4 %fusion.52 = f32[16,8,8,256]{3,2,1,0:T(8,128)} fusion(f32[16,8,8,256]{3,2,1,0:T(8,128)} %get-tuple-element.207, s32[]{:T(128)} %get-tuple-element.206, f32[8,6,256]{2,1,0:T(8,128)S(1)} %get-tuple-element.178, f32[8,256]{1,0:T(8,128)S(1)} %get-tuple-element.179, f32[8,6,256]{2,1,0:T(8,128)S(1)} %get-tuple-element.180, ...), kind=kOutput, calls=%fused_computation.14.clone.1 | convolution fusion | flops 138412032 | bytes 852480 | tf_op jit(solution)/shard_map/while/body/eval_jaxpr/gjcs,gjts->gct/dot_general | solution.py:106
  423.4 17.4 %fusion.52 = f32[16,8,8,256]{3,2,1,0:T(8,128)} fusion(f32[16,8,8,256]{3,2,1,0:T(8,128)} %get-tuple-element.207, s32[]{:T(128)} %get-tuple-element.206, f32[8,6,256]{2,1,0:T(8,128)S(1)} %get-tuple-element.178, f32[8,256]{1,0:T(8,128)S(1)} %get-tuple-element.179, f32[8,6,256]{2,1,0:T(8,128)S(1)} %get-tuple-element.180, ...), kind=kOutput, calls=%fused_computation.14.clone.1 | convolution fusion | flops 138412032 | bytes 852480 | tf_op jit(solution)/shard_map/while/body/eval_jaxpr/gjcs,gjts->gct/dot_general | solution.py:106
  444.1 17.4 %fusion.52 = f32[16,8,8,256]{3,2,1,0:T(8,128)} fusion(f32[16,8,8,256]{3,2,1,0:T(8,128)} %get-tuple-element.207, s32[]{:T(128)} %get-tuple-element.206, f32[8,6,256]{2,1,0:T(8,128)S(1)} %get-tuple-element.178, f32[8,256]{1,0:T(8,128)S(1)} %get-tuple-element.179, f32[8,6,256]{2,1,0:T(8,128)S(1)} %get-tuple-element.180, ...), kind=kOutput, calls=%fused_computation.14.clone.1 | convolution fusion | flops 138412032 | bytes 852480 | tf_op jit(solution)/shard_map/while/body/eval_jaxpr/gjcs,gjts->gct/dot_general | solution.py:106
  464.8 17.4 %fusion.52 = f32[16,8,8,256]{3,2,1,0:T(8,128)} fusion(f32[16,8,8,256]{3,2,1,0:T(8,128)} %get-tuple-element.207, s32[]{:T(128)} %get-tuple-element.206, f32[8,6,256]{2,1,0:T(8,128)S(1)} %get-tuple-element.178, f32[8,256]{1,0:T(8,128)S(1)} %get-tuple-element.179, f32[8,6,256]{2,1,0:T(8,128)S(1)} %get-tuple-element.180, ...), kind=kOutput, calls=%fused_computation.14.clone.1 | convolution fusion | flops 138412032 | bytes 852480 | tf_op jit(solution)/shard_map/while/body/eval_jaxpr/gjcs,gjts->gct/dot_general | solution.py:106
  485.4 17.4 %fusion.52 = f32[16,8,8,256]{3,2,1,0:T(8,128)} fusion(f32[16,8,8,256]{3,2,1,0:T(8,128)} %get-tuple-element.207, s32[]{:T(128)} %get-tuple-element.206, f32[8,6,256]{2,1,0:T(8,128)S(1)} %get-tuple-element.178, f32[8,256]{1,0:T(8,128)S(1)} %get-tuple-element.179, f32[8,6,256]{2,1,0:T(8,128)S(1)} %get-tuple-element.180, ...), kind=kOutput, calls=%fused_computation.14.clone.1 | convolution fusion | flops 138412032 | bytes 852480 | tf_op jit(solution)/shard_map/while/body/eval_jaxpr/gjcs,gjts->gct/dot_general | solution.py:106
  502.9 3.9 gather_fusion.8
  508.6 3.9 gather_fusion.6
  513.1 10.3 %fusion.33 = (f32[64,8,1,64]{3,2,1,0:T(1,128)S(1)}, f32[64,8,1,64]{3,2,1,0:T(1,128)}, f32[64,8,1,64]{3,2,1,0:T(1,128)}, f32[64,8,1,64]{3,2,1,0:T(1,128)}, f32[64...) fusion(f32[64,8,8,64]{3,2,1,0:T(8,128)} %reshape.335), kind=kLoop, calls=%fused_computation.112 | loop fusion | bytes 2097152 | tf_op jit(solution)/shard_map/slice | solution.py:36
  523.4 9.9 %all-to-all-start.1 = ((bf16[64,32,512]{2,1,0:T(8,128)(2,1)}), bf16[64,32,512]{2,1,0:T(8,128)(2,1)S(1)}, u32[]{:S(2)}, u32[]{:S(2)}) async-start(bf16[64,32,512]{2,1,0:T(8,128)(2,1)} %bitcast.218), calls=%async_computation.1 | async-start | bytes 4194304 | tf_op jit(solution)/shard_map/all_to_all | solution.py:117
  533.4 25.4 %fusion.14 = bf16[64,8,64]{2,1,0:T(8,128)(2,1)} fusion(bf16[64,8,8,64]{3,2,1,0:T(8,128)(2,1)S(1)} %reshape.321, f32[64,8,64]{2,1,0:T(8,128)} %bitcast.237, f32[64,64]{1,0:T(8,128)S(1)} %bitcast.248, f32[64,8,64]{2,1,0:T(8,128)} %bitcast.238, f32[64,64]{1,0:T(8,128)S(1)} %bitcast.249, f32[64,8,64]{2,1,0:T(8,128)} %bitcast.239, f32[64,64]{1,0:T(8,128)S(1)} %bitcast.250, ...), kind=kOutput, calls=%fused_computation.53 | convolution fusion | flops 92307456 | bytes 1769472 | tf_op jit(solution)/shard_map/nfcb,nfab->nca/dot_general | solution.py:46
  558.8 13.5 %gather_fusion.4 = bf16[1024,512]{1,0:T(8,128)(2,1)S(1)} fusion(bf16[64,32,512]{2,1,0:T(8,128)(2,1)} %all-to-all-done.2, s32[1024]{0:T(1024)S(1)} %bitcast.210), kind=kCustom, calls=%fused_computation.4 | custom fusion | bytes 2105344 | tf_op jit(solution)/shard_map/gather | solution.py:122
  572.3 2.4 reshape.333
  574.7 17.3 %fusion.32 = (f32[128,8,1,64]{3,2,1,0:T(1,128)}, f32[128,8,1,64]{3,2,1,0:T(1,128)}, f32[128,8,1,64]{3,2,1,0:T(1,128)}, f32[128,8,1,64]{3,2,1,0:T(1,128)}, f32[12...) fusion(f32[128,8,8,64]{3,2,1,0:T(8,128)} %reshape.333), kind=kLoop, calls=%fused_computation.111 | loop fusion | bytes 4194304 | tf_op jit(solution)/shard_map/slice | solution.py:36
  592.1 7.3 %gather_fusion.2 = bf16[1024,512]{1,0:T(8,128)(2,1)S(1)} fusion(bf16[64,32,512]{2,1,0:T(8,128)(2,1)S(1)} %all-to-all-done.1, s32[1024]{0:T(1024)S(1)} %bitcast.211), kind=kCustom, calls=%fused_computation.2 | custom fusion | bytes 2105344 | tf_op jit(solution)/shard_map/gather | solution.py:121
  599.4 2.1 reshape.313
  601.5 45.6 %fusion.10 = f32[128,8,64]{2,1,0:T(8,128)} fusion(bf16[128,8,8,64]{3,2,1,0:T(8,128)(2,1)} %reshape.313, f32[128,8,64]{2,1,0:T(8,128)} %bitcast.227, f32[128,64]{1,0:T(8,128)} %copy.144, f32[128,8,64]{2,1,0:T(8,128)} %bitcast.228, f32[128,64]{1,0:T(8,128)} %copy.143, f32[128,8,64]{2,1,0:T(8,128)} %bitcast.229, f32[128,64]{1,0:T(8,128)} %copy.142, ...), kind=kOutput, calls=%fused_computation.47 | convolution fusion | flops 184549376 | bytes 3670016 | tf_op jit(solution)/shard_map/nfcb,nfab->nca/dot_general | solution.py:46
  647.2 5.1 fusion.9
  (368 shorter events, 79.3 us)
Async XLA Ops:
  0.0 42.1 %copy-start.32 = (s32[128]{0:T(128)S(1)}, s32[128]{0:T(128)}, u32[]{:S(2)}) copy-start(s32[128]{0:T(128)} %param.16) | copy-start | bytes 1540
  0.0 42.2 %copy-start.15 = (bf16[128,8,256]{2,1,0:T(8,128)(2,1)S(1)}, bf16[128,8,256]{2,1,0:T(8,128)(2,1)}, u32[]{:S(2)}) copy-start(bf16[128,8,256]{2,1,0:T(8,128)(2,1)} %param.15) | copy-start | bytes 1572868
  0.0 42.4 %copy-start.10 = (bf16[128,8,256]{2,1,0:T(8,128)(2,1)S(1)}, bf16[128,8,256]{2,1,0:T(8,128)(2,1)}, u32[]{:S(2)}) copy-start(bf16[128,8,256]{2,1,0:T(8,128)(2,1)} %param.14) | copy-start | bytes 1572868
  0.0 47.9 %copy-start.29 = (s32[128,8]{0,1:T(8,128)S(1)}, s32[128,8]{0,1:T(8,128)}, u32[]{:S(2)}) copy-start(s32[128,8]{0,1:T(8,128)} %param.22) | copy-start | bytes 12292
  4.2 63.3 %copy-start.34 = (s32[2]{0:T(128)S(1)}, s32[2]{0:T(128)}, u32[]{:S(2)}) copy-start(s32[2]{0:T(128)} %constant.38) | copy-start | bytes 28
  4.3 63.4 %copy-start.33 = (s32[2]{0:T(128)S(1)}, s32[2]{0:T(128)}, u32[]{:S(2)}) copy-start(s32[2]{0:T(128)} %constant.66) | copy-start | bytes 28
  4.3 63.5 %copy-start.14 = (bf16[64,8,64]{2,1,0:T(8,128)(2,1)S(1)}, bf16[64,8,64]{2,1,0:T(8,128)(2,1)}, u32[]{:S(2)}) copy-start(bf16[64,8,64]{2,1,0:T(8,128)(2,1)} %param.20) | copy-start | bytes 196612
  4.3 63.7 %copy-start.30 = (s32[128,8]{0,1:T(8,128)S(1)}, s32[128,8]{0,1:T(8,128)}, u32[]{:S(2)}) copy-start(s32[128,8]{0,1:T(8,128)} %param.23) | copy-start | bytes 12292
  30.2 43.1 %all-to-all-start.3 = ((s32[64,1,16]{2,1,0:T(1,128)}), s32[64,1,16]{2,1,0:T(1,128)S(1)}, u32[]{:S(2)}, u32[]{:S(2)}) async-start(s32[64,1,16]{2,1,0:T(1,128)} %copy.151), calls=%async_computation.3 | async-start | bytes 65536 | tf_op jit(solution)/shard_map/all_to_all | solution.py:134
  42.2 46.5 %copy-start.16 = (pred[128,256]{1,0:T(8,128)(4,1)}, pred[128,256]{1,0:T(8,128)(4,1)S(1)}, u32[]{:S(2)}) copy-start(pred[128,256]{1,0:T(8,128)(4,1)S(1)} %iota_compare_fusion.4) | copy-start | bytes 98308
  42.4 56.7 %copy-start.8 = (bf16[128,8,256]{2,1,0:T(8,128)(2,1)}, bf16[128,8,256]{2,1,0:T(8,128)(2,1)S(1)}, u32[]{:S(2)}) copy-start(bf16[128,8,256]{2,1,0:T(8,128)(2,1)S(1)} %broadcast_select_fusion) | copy-start | bytes 1572868
  43.1 117.1 %collective-permute-start = (bf16[4,16,256]{2,1,0:T(8,128)(2,1)}, bf16[4,16,256]{2,1,0:T(8,128)(2,1)}, u32[]{:S(2)}, u32[]{:S(2)}) collective-permute-start(bf16[4,16,256]{2,1,0:T(8,128)(2,1)} %get-tuple-element.100), channel_id=1, source_target_pairs={{0,2},{2,4},{4,6},{6,8},{8,10},{10,12},{12,14},{14,16},{16,18},{18... | collective-permute-start | bytes 98312 | tf_op jit(solution)/shard_map/ppermute | solution.py:24
  46.6 113.6 %collective-permute-start.1 = (bf16[4,16,256]{2,1,0:T(8,128)(2,1)}, bf16[4,16,256]{2,1,0:T(8,128)(2,1)}, u32[]{:S(2)}, u32[]{:S(2)}) collective-permute-start(bf16[4,16,256]{2,1,0:T(8,128)(2,1)} %get-tuple-element.101), channel_id=1, source_target_pairs={{2,0},{4,2},{6,4},{8,6},{10,8},{12,10},{14,12},{16,14},{18,16},{20... | collective-permute-start | bytes 98312 | tf_op jit(solution)/shard_map/ppermute | solution.py:26
  73.2 18.6 %all-to-all-start = ((s32[64,1,32]{2,1,0:T(1,128)}), s32[64,1,32]{2,1,0:T(1,128)S(1)}, u32[]{:S(2)}, u32[]{:S(2)}) async-start(s32[64,1,32]{2,1,0:T(1,128)} %copy.134), calls=%async_computation | async-start | bytes 65536 | tf_op jit(solution)/shard_map/all_to_all | solution.py:116
  91.8 0.6 copy-start.19
  92.4 37.5 %all-to-all-start.5 = ((bf16[64,16,512]{2,1,0:T(8,128)(2,1)}), bf16[64,16,512]{2,1,0:T(8,128)(2,1)S(1)}, u32[]{:S(2)}, u32[]{:S(2)}) async-start(bf16[64,16,512]{2,1,0:T(8,128)(2,1)} %bitcast.75), calls=%async_computation.5 | async-start | bytes 2097152 | tf_op jit(solution)/shard_map/all_to_all | solution.py:136
  103.2 7.8 %copy-start.13 = (bf16[128,8,64]{0,2,1:T(8,128)(2,1)S(1)}, bf16[128,8,64]{0,2,1:T(8,128)(2,1)}, u32[]{:S(2)}) copy-start(bf16[128,8,64]{0,2,1:T(8,128)(2,1)} %param.19) | copy-start | bytes 393220
  103.2 20.9 %copy-start.31 = (s32[128,6]{0,1:T(8,128)S(1)}, s32[128,6]{0,1:T(8,128)}, u32[]{:S(2)}) copy-start(s32[128,6]{0,1:T(8,128)} %param.21) | copy-start | bytes 9220
  107.2 22.7 %copy-start.6 = (bf16[128,64,64]{2,1,0:T(8,128)(2,1)}, bf16[128,64,64]{2,1,0:T(8,128)(2,1)S(1)}, u32[]{:S(2)}) copy-start(bf16[128,64,64]{2,1,0:T(8,128)(2,1)S(1)} %copy.145) | copy-start | bytes 3145732
  124.8 16.9 %copy-start.20 = (s32[64,1,32]{2,1,0:T(1,128)S(1)}, s32[64,1,32]{2,1,0:T(1,128)}, u32[]{:S(2)}) copy-start(s32[64,1,32]{2,1,0:T(1,128)} %copy-done.19) | copy-start | bytes 24580
  129.9 21.1 %copy-start.2 = (bf16[64,16,512]{2,1,0:T(8,128)(2,1)}, bf16[64,16,512]{2,1,0:T(8,128)(2,1)S(1)}, u32[]{:S(2)}) copy-start(bf16[64,16,512]{2,1,0:T(8,128)(2,1)S(1)} %all-to-all-done.5) | copy-start | bytes 3145732
  129.9 32.3 %all-to-all-start.4 = ((bf16[64,16,512]{2,1,0:T(8,128)(2,1)}), bf16[64,16,512]{2,1,0:T(8,128)(2,1)S(1)}, u32[]{:S(2)}, u32[]{:S(2)}) async-start(bf16[64,16,512]{2,1,0:T(8,128)(2,1)} %bitcast.220), calls=%async_computation.4 | async-start | bytes 2097152 | tf_op jit(solution)/shard_map/all_to_all | solution.py:135
  151.0 9.2 %copy-start.9 = (bf16[128,8,256]{2,1,0:T(8,128)(2,1)S(1)}, bf16[128,8,256]{2,1,0:T(8,128)(2,1)}, u32[]{:S(2)}) copy-start(bf16[128,8,256]{2,1,0:T(8,128)(2,1)} %copy-done.8) | copy-start | bytes 1572868
  151.0 9.2 %copy-start.11 = (bf16[128,8,256]{2,1,0:T(8,128)(2,1)S(1)}, bf16[128,8,256]{2,1,0:T(8,128)(2,1)}, u32[]{:S(2)}) copy-start(bf16[128,8,256]{2,1,0:T(8,128)(2,1)} %param.14) | copy-start | bytes 1572868
  162.2 9.9 %copy-start.4 = (bf16[64,16,512]{2,1,0:T(8,128)(2,1)}, bf16[64,16,512]{2,1,0:T(8,128)(2,1)S(1)}, u32[]{:S(2)}) copy-start(bf16[64,16,512]{2,1,0:T(8,128)(2,1)S(1)} %all-to-all-done.4) | copy-start | bytes 3145732
  162.2 361.2 %all-to-all-start.2 = ((bf16[64,32,512]{2,1,0:T(8,128)(2,1)}), bf16[64,32,512]{2,1,0:T(8,128)(2,1)}, u32[]{:S(2)}, u32[]{:S(2)}) async-start(bf16[64,32,512]{2,1,0:T(8,128)(2,1)} %bitcast.219), calls=%async_computation.2 | async-start | bytes 4194304 | tf_op jit(solution)/shard_map/all_to_all | solution.py:118
  172.0 330.8 %copy-start.1 = (s32[512,1]{0,1:T(1,128)S(1)}, s32[512,1]{0,1:T(1,128)}, u32[]{:S(2)}) copy-start(s32[512,1]{0,1:T(1,128)} %get-tuple-element.59) | copy-start | bytes 6148
  172.0 330.8 %copy-start.3 = (bf16[64,16,512]{2,1,0:T(8,128)(2,1)S(1)}, bf16[64,16,512]{2,1,0:T(8,128)(2,1)}, u32[]{:S(2)}) copy-start(bf16[64,16,512]{2,1,0:T(8,128)(2,1)} %copy-done.2) | copy-start | bytes 3145732
  502.9 5.7 copy-start.5
  513.1 20.3 %copy-start.25 = (f32[64,1,1,64]{3,2,0,1:T(1,128)S(1)}, f32[64,1,1,64]{3,2,0,1:T(1,128)}, u32[]{:S(2)}) copy-start(f32[64,1,1,64]{3,2,0,1:T(1,128)} %get-tuple-element.102) | copy-start | bytes 49156
  513.1 20.3 %copy-start.26 = (f32[64,1,1,64]{3,2,0,1:T(1,128)S(1)}, f32[64,1,1,64]{3,2,0,1:T(1,128)}, u32[]{:S(2)}) copy-start(f32[64,1,1,64]{3,2,0,1:T(1,128)} %get-tuple-element.103) | copy-start | bytes 49156
  513.1 20.3 %copy-start.27 = (f32[64,1,1,64]{3,2,0,1:T(1,128)S(1)}, f32[64,1,1,64]{3,2,0,1:T(1,128)}, u32[]{:S(2)}) copy-start(f32[64,1,1,64]{3,2,0,1:T(1,128)} %get-tuple-element.104) | copy-start | bytes 49156
  513.1 20.3 %copy-start.28 = (f32[64,1,1,64]{3,2,0,1:T(1,128)S(1)}, f32[64,1,1,64]{3,2,0,1:T(1,128)}, u32[]{:S(2)}) copy-start(f32[64,1,1,64]{3,2,0,1:T(1,128)} %get-tuple-element.105) | copy-start | bytes 49156
  523.4 68.6 %all-to-all-start.1 = ((bf16[64,32,512]{2,1,0:T(8,128)(2,1)}), bf16[64,32,512]{2,1,0:T(8,128)(2,1)S(1)}, u32[]{:S(2)}, u32[]{:S(2)}) async-start(bf16[64,32,512]{2,1,0:T(8,128)(2,1)} %bitcast.218), calls=%async_computation.1 | async-start | bytes 4194304 | tf_op jit(solution)/shard_map/all_to_all | solution.py:117
  533.4 25.4 %copy-start = (s32[1024,1]{0,1:T(1,128)S(1)}, s32[1024,1]{0,1:T(1,128)}, u32[]{:S(2)}) copy-start(s32[1024,1]{0,1:T(1,128)} %get-tuple-element.118) | copy-start | bytes 12292
  592.0 9.4 %copy-start.21 = (f32[128,64]{1,0:T(8,128)S(1)}, f32[128,64]{1,0:T(8,128)}, u32[]{:S(2)}) copy-start(f32[128,64]{1,0:T(8,128)} %copy.136) | copy-start | bytes 98308
  592.0 9.4 %copy-start.22 = (f32[128,64]{1,0:T(8,128)S(1)}, f32[128,64]{1,0:T(8,128)}, u32[]{:S(2)}) copy-start(f32[128,64]{1,0:T(8,128)} %copy.138) | copy-start | bytes 98308
  592.0 9.4 %copy-start.23 = (f32[128,64]{1,0:T(8,128)S(1)}, f32[128,64]{1,0:T(8,128)}, u32[]{:S(2)}) copy-start(f32[128,64]{1,0:T(8,128)} %copy.139) | copy-start | bytes 98308
  592.0 9.4 %copy-start.24 = (f32[128,64]{1,0:T(8,128)S(1)}, f32[128,64]{1,0:T(8,128)}, u32[]{:S(2)}) copy-start(f32[128,64]{1,0:T(8,128)} %copy.140) | copy-start | bytes 98308
  601.5 45.6 %copy-start.18 = (bf16[64,8,64]{2,1,0:T(8,128)(2,1)S(1)}, bf16[64,8,64]{2,1,0:T(8,128)(2,1)}, u32[]{:S(2)}) copy-start(bf16[64,8,64]{2,1,0:T(8,128)(2,1)} %fusion.14) | copy-start | bytes 196612
  601.5 45.7 %copy-start.7 = (bf16[128,64,64]{2,1,0:T(8,128)(2,1)S(1)}, bf16[128,64,64]{2,1,0:T(8,128)(2,1)}, u32[]{:S(2)}) copy-start(bf16[128,64,64]{2,1,0:T(8,128)(2,1)} %copy-done.6) | copy-start | bytes 3145732
  601.5 45.7 %copy-start.12 = (f32[16,8,8,256]{3,2,1,0:T(8,128)S(1)}, f32[16,8,8,256]{3,2,1,0:T(8,128)}, u32[]{:S(2)}) copy-start(f32[16,8,8,256]{3,2,1,0:T(8,128)} %get-tuple-element.32) | copy-start | bytes 3145732
  601.5 45.7 %copy-start.17 = (pred[128,256]{1,0:T(8,128)(4,1)S(1)}, pred[128,256]{1,0:T(8,128)(4,1)}, u32[]{:S(2)}) copy-start(pred[128,256]{1,0:T(8,128)(4,1)} %copy-done.16) | copy-start | bytes 98308
where the time goes:
time: 658 us; the launch traced here: 652 us
  matrix products  361 us (55%)
  local copies, waits for them, and re-layouts  184 us (28%)
  starting transfers between devices  63.4 us (10%)
  other arithmetic  38.5 us (6%)
    dot_general x16, matrix products, near_block(): jnp.einsum('gjcs,gjts->gct', source_rows[:, :, DIM:], kernel, preferred_e...  279 us
    dot_general x2, matrix products, far_sum(): jnp.einsum('nfcb,nfab->nca', source_coef, kernel, preferred_element_type=...  71 us
    slice x19, local copies, waits for them, and re-layouts, matern(): offset = targets[..., coord, :, None] - sources[..., coord, None, :]  32.7 us
    gather x16, local copies, waits for them, and re-layouts, near_block(): source_rows = extended[chosen]  29.3 us
    scatter x1, local copies, waits for them, and re-layouts, slot_table(): jnp.zeros((owners, capacity), jnp.int32).at[flat_owner, slot_index]  25.2 us
    another operation x5, other arithmetic  19.4 us
    gather x1, local copies, waits for them, and re-layouts, body(): picked_skel = got_skel[flat_owner, slot_index]  13.5 us
  transfers between devices with their start and end apart: 8, of which 1 were waited for; matrix products, arithmetic and copies ran while one was open for 76% of the time, Pallas kernels for 0%

commit v1 on v0

--- a/solution.py
+++ b/solution.py
@@ -1,8 +1,11 @@
+import functools
 import math
 
 import jax
 import jax.numpy as jnp
 from jax import lax
+from jax.experimental import pallas as pl
+from jax.experimental.pallas import tpu as pltpu
 from jax.sharding import PartitionSpec as P
 
 DIM = 8
@@ -11,6 +14,104 @@
 
 SQRT_THREE = 1.7320508075688772
 LENGTH_SCALE = 1.5
+
+
+RATE = SQRT_THREE / LENGTH_SCALE
+RATE_TWO = RATE * math.log2(math.e)
+BF16 = jnp.bfloat16
+F32 = jnp.float32
+
+
+def matern_of_square(square):
+    square = jnp.maximum(square, 1e-30)
+    radius = square * lax.rsqrt(square)
+    return ((1.0 + RATE * radius) * jnp.exp2(-RATE_TWO * radius)).astype(BF16)
+
+
+def norm_rows(coords):
+    norm = jnp.sum(coords * coords, axis=0, keepdims=True)
+    high = norm.astype(BF16).astype(F32)
+    middle = (norm - high).astype(BF16).astype(F32)
+    low = norm - high - middle
+    row = lax.broadcasted_iota(jnp.int32, coords.shape, 0)
+    return row, high, middle, low
+
+
+def source_form(coords):
+    row, high, middle, low = norm_rows(coords)
+    tail = jnp.where(row == 0, high, jnp.where(row == 1, middle, jnp.where(row == 2, low, 1.0)))
+    return jnp.concatenate([coords, jnp.where(row < 6, tail, 0.0)], axis=0)
+
+
+def target_form(coords):
+    row, high, middle, low = norm_rows(coords)
+    tail = jnp.where(row == 3, high, jnp.where(row == 4, middle, jnp.where(row == 5, low, 1.0)))
+    return jnp.concatenate([-2.0 * coords, jnp.where(row < 6, tail, 0.0)], axis=0)
+
+
+def near_kernel(near, leaves, ids, pts, cols, out, rows, mine, even, odd):
+    half = out.shape[0]
+    size = pts.shape[2]
+    base = ids[half * near]
+
+    def stage(q, carry):
+        rows[q] = source_form(pts[q].astype(F32)).T.astype(BF16)
+        return carry
+
+    lax.fori_loop(0, leaves, stage, 0)
+
+    def stage_target(i, carry):
+        mine[i] = target_form(pts[base + i].astype(F32)).astype(BF16)
+        return carry
+
+    lax.fori_loop(0, half, stage_target, 0)
+
+    def values(i, j, store):
+        square = jnp.dot(rows[ids[i * near + j]], mine[i], preferred_element_type=F32)
+        store[size * j : size * (j + 1), :] = matern_of_square(square)
+
+    def phase(current, previous, store, ready):
+        total = jnp.zeros((cols.shape[1], size), F32)
+        for j in range(near):
+            values(current, j, store)
+            total = total + jnp.dot(
+                cols[ids[previous * near + j]],
+                ready[size * j : size * (j + 1), :],
+                preferred_element_type=F32,
+            )
+        out[previous] = total
+
+    for j in range(near):
+        values(0, j, even)
+
+    def step(k, carry):
+        phase(2 * k + 1, 2 * k, odd, even)
+        phase(jnp.minimum(2 * k + 2, half - 1), 2 * k + 1, even, odd)
+        return carry
+
+    lax.fori_loop(0, half // 2, step, 0)
+
+
+def near_field(ids, pts, cols, half, near):
+    leaves, _, size = pts.shape
+    vmem = pl.BlockSpec(memory_space=pltpu.VMEM)
+    return pl.pallas_call(
+        functools.partial(near_kernel, near, leaves),
+        out_shape=jax.ShapeDtypeStruct((half, cols.shape[1], size), F32),
+        in_specs=[pl.BlockSpec(memory_space=pltpu.SMEM), vmem, vmem],
+        out_specs=vmem,
+        scratch_shapes=[
+            pltpu.VMEM((leaves, size, 2 * DIM), BF16),
+            pltpu.VMEM((half, 2 * DIM, size), BF16),
+            pltpu.VMEM((near * size, size), BF16),
+            pltpu.VMEM((near * size, size), BF16),
+        ],
+        compiler_params=pltpu.CompilerParams(vmem_limit_bytes=40 * 2**20),
+        cost_estimate=pl.CostEstimate(
+            flops=half * near * size * size * 64, bytes_accessed=4 * 2**20, transcendentals=0
+        ),
+        name="near",
+    )(ids, pts, cols)
 
 
 def with_halo(cells, sides, width):
@@ -93,22 +194,21 @@
     extended = with_halo(bundle, (("leaf", 0),), HALO)
     first_leaf = lax.axis_index("leaf") * leaf_dev - HALO
     near_count = near_list.shape[1]
-    group_size = math.gcd(leaf_dev, 8)
-    turns = leaf_dev // group_size
-    local_ids = (near_list - first_leaf).reshape(turns, group_size, near_count)
-
-    def near_block(pieces):
-        target_points, chosen = pieces
-        source_rows = extended[chosen]
-        kernel = matern(
-            target_points.astype(jnp.float32)[:, None], source_rows[:, :, :DIM].astype(jnp.float32)
-        ).astype(jnp.bfloat16)
-        return jnp.einsum(
-            "gjcs,gjts->gct", source_rows[:, :, DIM:], kernel, preferred_element_type=jnp.float32
-        )
-
-    near_part = lax.map(near_block, (points.reshape(turns, group_size, DIM, leaf_size), local_ids))
-    near_part = near_part.reshape(leaf_dev, columns, leaf_size)
+    half = leaf_dev // 2
+    core = lax.axis_index("rhs")
+    swap = [(0, 1), (1, 0)]
+    own = extended[:, DIM:]
+    cols = jnp.concatenate([own, lax.ppermute(own, "rhs", swap)], axis=1)
+    chosen = lax.dynamic_slice_in_dim(near_list - first_leaf, core * half, half, axis=0)
+    ids = jnp.concatenate([chosen.reshape(-1), (core * half + HALO)[None]]).astype(jnp.int32)
+    near_half = near_field(ids, extended[:, :DIM], cols, half, near_count)
+    near_mine = near_half[:, :columns]
+    near_theirs = lax.ppermute(near_half[:, columns:], "rhs", swap)
+    near_part = jnp.where(
+        core == 0,
+        jnp.concatenate([near_mine, near_theirs], axis=0),
+        jnp.concatenate([near_theirs, near_mine], axis=0),
+    )
     leaf_rows = leaf_coef.reshape(leaf_dev, columns * rank)
     leaf_skel_rows = leaf_skeleton.reshape(leaf_dev, DIM * rank)
     capacity = max(2, 2 * leaf_dev * far_count // owners)

time: 658 us -> 394 us (0.60)
  matrix products: 361 us -> 86.4 us
  Pallas kernels: 0 us -> 59.7 us
  local copies, waits for them, and re-layouts: 184 us -> 151 us
  other arithmetic: 38.5 us -> 24.3 us
    dot_general x16 -> x0, matrix products: 279 us -> none  [near_block(): jnp.einsum('gjcs,gjts->gct', source_rows[:, :, DIM:], kernel, preferred_e...]
    pallas_call x0 -> x1, Pallas kernels: none -> 59.7 us  [near_field(): pl.pallas_call(functools.partial(near_kernel, near, leaves), out_shape=ja...]
    gather x16 -> x0, local copies, waits for them, and re-layouts: 29.3 us -> none  [near_block(): source_rows = extended[chosen]]
    select_n x16 -> x0, other arithmetic: 12 us -> none  [near_block(): source_rows = extended[chosen]]
    sub x89 -> x9, local copies, waits for them, and re-layouts: 12.4 us -> 5.76 us  [matern(): offset = targets[..., coord, :, None] - sources[..., coord, None, :]]
    slice x19 -> x3, local copies, waits for them, and re-layouts: 32.7 us -> 28.4 us  [matern(): offset = targets[..., coord, :, None] - sources[..., coord, None, :]]
  transfers between devices with their start and end apart: 8 -> 10, of which waited for: 1 -> 1; matrix products, arithmetic and copies ran while one was open for 76% -> 58% of each run, Pallas kernels for 0% -> 15%
where the time goes in v1:
time: 394 us; the launch traced here: 393 us
  local copies, waits for them, and re-layouts  151 us (38%)
  matrix products  86.4 us (22%)
  starting transfers between devices  67.7 us (17%)
  Pallas kernels  59.7 us (15%)
  other arithmetic  24.3 us (6%)
    dot_general x2, matrix products, far_sum(): jnp.einsum('nfcb,nfab->nca', source_coef, kernel, preferred_element_type=...  75.5 us
    pallas_call x1, Pallas kernels, near_field(): pl.pallas_call(functools.partial(near_kernel, near, leaves), out_shape=ja...  59.7 us
    slice x3, local copies, waits for them, and re-layouts, matern(): offset = targets[..., coord, :, None] - sources[..., coord, None, :]  28.4 us
    scatter x1, local copies, waits for them, and re-layouts, slot_table(): jnp.zeros((owners, capacity), jnp.int32).at[flat_owner, slot_index]  25.2 us
    another operation x5, other arithmetic  19.4 us
    gather x1, local copies, waits for them, and re-layouts, body(): picked_coef = got_coef[flat_owner, slot_index]  13.5 us
    all_to_all x1, starting transfers between devices, body(): lax.all_to_all(upper_wanted, 'leaf', split_axis=0, concat_axis=0, tiled=T...  12 us
    all_to_all x1, starting transfers between devices, body(): lax.all_to_all(upper_rows[asked], 'leaf', split_axis=0, concat_axis=0, ti...  11 us
  transfers between devices with their start and end apart: 10, of which 1 were waited for; matrix products, arithmetic and copies ran while one was open for 58% of the time, Pallas kernels for 15%

profile of v1, /device:TPU:1, one launch (start us, length us, event | category | flops | bytes accessed | tf_op | source)
XLA Modules:
  0.0 393.2 jit_solution(14402475901482964071)
XLA Ops:
  0.0 0.8 copy.94
  1.1 1.2 reduce-window.16
  2.6 0.8 copy.98
  3.6 25.2 %scatter_fusion = s32[64,16]{0,1:T(8,128)S(1)} fusion(s32[64,16]{0,1:T(8,128)S(1)} %broadcast.161, s32[512]{0:T(512)S(1)} %bitcast.137, s32[512]{0:T(512)S(1)} %reshape.337), kind=kCustom, calls=%fused_computation.8 | custom fusion | bytes 10240 | tf_op jit(solution)/shard_map/scatter | solution.py:158
  29.5 12.0 %all-to-all-start.3 = ((s32[64,1,16]{2,1,0:T(1,128)}), s32[64,1,16]{2,1,0:T(1,128)S(1)}, u32[]{:S(2)}, u32[]{:S(2)}) async-start(s32[64,1,16]{2,1,0:T(1,128)} %copy.99), calls=%async_computation.3 | async-start | bytes 65536 | tf_op jit(solution)/shard_map/all_to_all | solution.py:234
  41.9 18.0 %reduce-window.14 = s32[64,8,128]{2,1,0:T(8,128)S(1)} reduce-window(s32[64,8,128]{2,1,0:T(8,128)S(1)} %fusion.13, s32[]{:T(128)} %constant.14.clone.1), window={size=1x1x128 pad=0_0x0_0x127_0}, to_apply=%region_0.1 | reduce-window | flops 8323072 | bytes 524292 | tf_op jit(solution)/shard_map/reduce-window
  61.2 4.3 %scatter_custom_fusion.1 = s32[2048]{0:T(1024)S(1)} fusion(s32[1024]{0:T(1024)S(1)} %broadcast_select_fusion.1, s32[1024]{0:T(1024)S(1)} %reshape.343, s32[]{:T(128)} %constant.14.clone.1), kind=kCustom, calls=%fused_computation.71 | custom fusion | bytes 8196
  66.3 9.8 %all-to-all-start = ((s32[64,1,32]{2,1,0:T(1,128)}), s32[64,1,32]{2,1,0:T(1,128)S(1)}, u32[]{:S(2)}, u32[]{:S(2)}) async-start(s32[64,1,32]{2,1,0:T(1,128)} %copy.82), calls=%async_computation | async-start | bytes 65536 | tf_op jit(solution)/shard_map/all_to_all | solution.py:216
  76.2 5.0 %gather_fusion.6 = bf16[1024,512]{1,0:T(8,128)(2,1)} fusion(bf16[64,512]{1,0:T(8,128)(2,1)S(1)} %reshape.268, s32[1024]{0:T(1024)S(1)} %broadcast_clamp_fusion.1), kind=kCustom, calls=%fused_computation.6 | custom fusion | bytes 2101248 | tf_op jit(solution)/shard_map/gather | solution.py:237
  81.2 3.1 all-to-all-done
  84.4 6.6 %all-to-all-start.5 = ((bf16[64,16,512]{2,1,0:T(8,128)(2,1)}), bf16[64,16,512]{2,1,0:T(8,128)(2,1)S(1)}, u32[]{:S(2)}, u32[]{:S(2)}) async-start(bf16[64,16,512]{2,1,0:T(8,128)(2,1)} %bitcast.44), calls=%async_computation.5 | async-start | bytes 2097152 | tf_op jit(solution)/shard_map/all_to_all | solution.py:236
  92.0 2.9 collective-permute-start
  94.9 1.3 collective-permute-start.1
  96.2 3.9 %copy.93 = bf16[128,64,64]{2,1,0:T(8,128)(2,1)S(1)} copy(bf16[128,64,64]{0,2,1:T(8,128)(2,1)} %param.16) | data formatting | bytes 2097152 | tf_op args[4]
  100.2 4.3 %convolution_convert_fusion = bf16[128,8,64]{2,1,0:T(8,128)(2,1)S(1)} fusion(bf16[128,8,256]{2,1,0:T(8,128)(2,1)} %copy-done.5, bf16[128,64,256]{2,1,0:T(8,128)(2,1)} %param.15), kind=kOutput, calls=%fused_computation.17 | convolution fusion | flops 33619968 | bytes 4849664 | tf_op jit(solution)/shard_map/lcp,lkp->lck/dot_general | solution.py:185
  104.4 1.4 fusion.6
  105.8 1.1 reshape.263
  106.9 5.1 %gather_fusion.4 = bf16[1024,512]{1,0:T(8,128)(2,1)} fusion(bf16[64,512]{1,0:T(8,128)(2,1)S(1)} %reshape.263, s32[1024]{0:T(1024)S(1)} %broadcast_clamp_fusion.1), kind=kCustom, calls=%fused_computation.4 | custom fusion | bytes 2101248 | tf_op jit(solution)/shard_map/gather | solution.py:235
  112.0 11.0 %all-to-all-start.4 = ((bf16[64,16,512]{2,1,0:T(8,128)(2,1)}), bf16[64,16,512]{2,1,0:T(8,128)(2,1)S(1)}, u32[]{:S(2)}, u32[]{:S(2)}) async-start(bf16[64,16,512]{2,1,0:T(8,128)(2,1)} %bitcast.141), calls=%async_computation.4 | async-start | bytes 2097152 | tf_op jit(solution)/shard_map/all_to_all | solution.py:235
  123.0 0.9 bitcast_convert_fusion.1
  124.2 1.0 copy.85
  125.3 0.7 copy.84
  127.5 0.7 copy.88
  128.2 0.7 copy.89
  131.5 9.2 %gather_fusion.2 = bf16[2048,512]{1,0:T(8,128)(2,1)} fusion(bf16[128,512]{1,0:T(8,128)(2,1)S(1)} %copy.85, s32[2048]{0:T(1024)S(1)} %broadcast_clamp_fusion), kind=kCustom, calls=%fused_computation.2 | custom fusion | bytes 4202496 | tf_op jit(solution)/shard_map/gather | solution.py:219
  140.7 9.7 %all-to-all-start.2 = ((bf16[64,32,512]{2,1,0:T(8,128)(2,1)}), bf16[64,32,512]{2,1,0:T(8,128)(2,1)S(1)}, u32[]{:S(2)}, u32[]{:S(2)}) async-start(bf16[64,32,512]{2,1,0:T(8,128)(2,1)} %bitcast.139), calls=%async_computation.2 | async-start | bytes 4194304 | tf_op jit(solution)/shard_map/all_to_all | solution.py:218
  150.5 1.3 pad_maximum_fusion
  151.8 0.9 fusion.28
  152.6 3.8 collective-permute-start.2
  156.4 0.8 fusion.30
  157.2 9.2 %gather_fusion = bf16[2048,512]{1,0:T(8,128)(2,1)} fusion(bf16[128,512]{1,0:T(8,128)(2,1)S(1)} %copy.83, s32[2048]{0:T(1024)S(1)} %broadcast_clamp_fusion), kind=kCustom, calls=%fused_computation | custom fusion | bytes 4202496 | tf_op jit(solution)/shard_map/gather | solution.py:217
  166.4 1.3 pad_maximum_fusion.1.cols
  167.7 59.7 %near.1 = f32[64,16,256]{2,1,0:T(8,128)S(1)} custom-call(s32[385]{0:T(512)S(1)} %pad_add_fusion.1.ids, bf16[136,8,256]{2,1,0:T(8,128)(2,1)S(1)} %get-tuple-element.24.pts, bf16[136,16,256]{2,1,0:T(8,128)(2,1)S(1)} %pad_maximum_fusion.1.cols), custom_call_target="tpu_custom_call" | custom-call | flops 1610612736 | bytes 4194304 | tf_op jit(solution)/shard_map/near/pallas_call | solution.py:98
  227.4 1.0 fusion.29
  228.5 9.5 %gather_fusion.7 = bf16[512,512]{1,0:T(8,128)(2,1)} fusion(bf16[64,16,512]{2,1,0:T(8,128)(2,1)} %copy-done, s32[512]{0:T(512)S(1)} %bitcast.135), kind=kCustom, calls=%fused_computation.7 | custom fusion | bytes 1052672 | tf_op jit(solution)/shard_map/gather | solution.py:240
  238.0 2.6 reshape.278
  240.6 6.4 %gather_fusion.5 = bf16[512,512]{1,0:T(8,128)(2,1)} fusion(bf16[64,16,512]{2,1,0:T(8,128)(2,1)S(1)} %copy-done.2, s32[512]{0:T(512)S(1)} %bitcast.136), kind=kCustom, calls=%fused_computation.5 | custom fusion | bytes 1052672 | tf_op jit(solution)/shard_map/gather | solution.py:239
  247.0 1.6 reshape.267
  248.7 10.0 %fusion.27 = (f32[64,8,1,64]{3,2,1,0:T(1,128)S(1)}, f32[64,8,1,64]{3,2,1,0:T(1,128)}, f32[64,8,1,64]{3,2,1,0:T(1,128)}, f32[64,8,1,64]{3,2,1,0:T(1,128)}, f32[64...) fusion(f32[64,8,8,64]{3,2,1,0:T(8,128)} %reshape.278), kind=kLoop, calls=%fused_computation.86 | loop fusion | bytes 2097152 | tf_op jit(solution)/shard_map/slice | solution.py:137
  258.7 10.5 %all-to-all-start.1 = ((bf16[64,32,512]{2,1,0:T(8,128)(2,1)}), bf16[64,32,512]{2,1,0:T(8,128)(2,1)}, u32[]{:S(2)}, u32[]{:S(2)}) async-start(bf16[64,32,512]{2,1,0:T(8,128)(2,1)} %bitcast.140), calls=%async_computation.1 | async-start | bytes 4194304 | tf_op jit(solution)/shard_map/all_to_all | solution.py:217
  269.3 25.9 %fusion.7 = bf16[64,8,64]{2,1,0:T(8,128)(2,1)} fusion(bf16[64,8,8,64]{3,2,1,0:T(8,128)(2,1)S(1)} %reshape.267, f32[64,8,64]{2,1,0:T(8,128)} %bitcast.156, f32[64,64]{1,0:T(8,128)S(1)} %bitcast.167, f32[64,8,64]{2,1,0:T(8,128)} %bitcast.157, f32[64,64]{1,0:T(8,128)S(1)} %bitcast.168, f32[64,8,64]{2,1,0:T(8,128)} %bitcast.158, f32[64,64]{1,0:T(8,128)S(1)} %bitcast.169, ...), kind=kOutput, calls=%fused_computation.22 | convolution fusion | flops 92307456 | bytes 1769472 | tf_op jit(solution)/shard_map/nfcb,nfab->nca/dot_general | solution.py:147
  295.2 7.3 %gather_fusion.3 = bf16[1024,512]{1,0:T(8,128)(2,1)S(1)} fusion(bf16[64,32,512]{2,1,0:T(8,128)(2,1)S(1)} %all-to-all-done.2, s32[1024]{0:T(1024)S(1)} %bitcast.133), kind=kCustom, calls=%fused_computation.3 | custom fusion | bytes 2105344 | tf_op jit(solution)/shard_map/gather | solution.py:222
  302.5 2.4 reshape.276
  304.9 17.6 %fusion.26 = (f32[128,8,1,64]{3,2,1,0:T(1,128)}, f32[128,8,1,64]{3,2,1,0:T(1,128)}, f32[128,8,1,64]{3,2,1,0:T(1,128)}, f32[128,8,1,64]{3,2,1,0:T(1,128)}, f32[12...) fusion(f32[128,8,8,64]{3,2,1,0:T(8,128)} %reshape.276), kind=kLoop, calls=%fused_computation.85 | loop fusion | bytes 4194304 | tf_op jit(solution)/shard_map/slice | solution.py:137
  322.5 13.5 %gather_fusion.1 = bf16[1024,512]{1,0:T(8,128)(2,1)S(1)} fusion(bf16[64,32,512]{2,1,0:T(8,128)(2,1)} %all-to-all-done.1, s32[1024]{0:T(1024)S(1)} %bitcast.134), kind=kCustom, calls=%fused_computation.1 | custom fusion | bytes 2105344 | tf_op jit(solution)/shard_map/gather | solution.py:221
  336.0 2.1 reshape.259
  338.2 49.6 %fusion.2 = f32[128,8,64]{2,1,0:T(8,128)S(1)} fusion(bf16[128,8,8,64]{3,2,1,0:T(8,128)(2,1)} %reshape.259, f32[128,8,64]{2,1,0:T(8,128)} %bitcast.146, f32[128,64]{1,0:T(8,128)} %copy.92, f32[128,8,64]{2,1,0:T(8,128)} %bitcast.147, f32[128,64]{1,0:T(8,128)} %copy.91, f32[128,8,64]{2,1,0:T(8,128)} %bitcast.148, f32[128,64]{1,0:T(8,128)} %copy.90, ...), kind=kOutput, calls=%fused_computation.15 | convolution fusion | flops 184549376 | bytes 3670016 | tf_op jit(solution)/shard_map/nfcb,nfab->nca/dot_general | solution.py:147
  387.9 5.2 %fusion.9 = f32[128,8,256]{2,1,0:T(8,128)} fusion(f32[64,8,256]{2,1,0:T(8,128)} %collective-permute-done.3, f32[64,8,256]{2,1,0:T(8,128)S(1)} %copy-done.7, pred[]{:T(512)S(6)} %eq.69, pred[128,256]{1,0:T(8,128)(4,1)S(1)} %copy-done.12, bf16[128,64,256]{2,1,0:T(8,128)(2,1)} %param.15, f32[128,8,64]{2,1,0:T(8,128)S(1)} %fusion.2, ...), kind=kOutput, calls=%fused_computation.27 | convolution fusion | flops 43384832 | bytes 7766017 | tf_op jit(solution)/shard_map/lck,lkp->lcp/dot_general | solution.py:250
  (117 shorter events, 9.3 us)
Async XLA Ops:
  0.0 60.6 %copy-start.24 = (s32[2]{0:T(128)S(1)}, s32[2]{0:T(128)}, u32[]{:S(2)}) copy-start(s32[2]{0:T(128)} %constant.11) | copy-start | bytes 28
  0.0 60.7 %copy-start.23 = (s32[2]{0:T(128)S(1)}, s32[2]{0:T(128)}, u32[]{:S(2)}) copy-start(s32[2]{0:T(128)} %constant.51) | copy-start | bytes 28
  0.0 41.5 %copy-start.19 = (s32[128,8]{0,1:T(8,128)S(1)}, s32[128,8]{0,1:T(8,128)}, u32[]{:S(2)}) copy-start(s32[128,8]{0,1:T(8,128)} %param.20) | copy-start | bytes 12292
  0.0 60.8 %copy-start.8 = (bf16[64,8,64]{2,1,0:T(8,128)(2,1)S(1)}, bf16[64,8,64]{2,1,0:T(8,128)(2,1)}, u32[]{:S(2)}) copy-start(bf16[64,8,64]{2,1,0:T(8,128)(2,1)} %param.18) | copy-start | bytes 196612
  1.0 59.9 %copy-start.20 = (s32[128,8]{0,1:T(8,128)S(1)}, s32[128,8]{0,1:T(8,128)}, u32[]{:S(2)}) copy-start(s32[128,8]{0,1:T(8,128)} %param.21) | copy-start | bytes 12292
  29.5 36.7 %all-to-all-start.3 = ((s32[64,1,16]{2,1,0:T(1,128)}), s32[64,1,16]{2,1,0:T(1,128)S(1)}, u32[]{:S(2)}, u32[]{:S(2)}) async-start(s32[64,1,16]{2,1,0:T(1,128)} %copy.99), calls=%async_computation.3 | async-start | bytes 65536 | tf_op jit(solution)/shard_map/all_to_all | solution.py:234
  66.3 18.1 %all-to-all-start = ((s32[64,1,32]{2,1,0:T(1,128)}), s32[64,1,32]{2,1,0:T(1,128)S(1)}, u32[]{:S(2)}, u32[]{:S(2)}) async-start(s32[64,1,32]{2,1,0:T(1,128)} %copy.82), calls=%async_computation | async-start | bytes 65536 | tf_op jit(solution)/shard_map/all_to_all | solution.py:216
  76.1 14.9 %copy-start.22 = (s32[128]{0:T(128)S(1)}, s32[128]{0:T(128)}, u32[]{:S(2)}) copy-start(s32[128]{0:T(128)} %param.14) | copy-start | bytes 1540
  76.1 15.0 %copy-start.10 = (bf16[128,8,256]{2,1,0:T(8,128)(2,1)S(1)}, bf16[128,8,256]{2,1,0:T(8,128)(2,1)}, u32[]{:S(2)}) copy-start(bf16[128,8,256]{2,1,0:T(8,128)(2,1)} %param.13) | copy-start | bytes 1572868
  76.2 15.1 %copy-start.6 = (bf16[128,8,256]{2,1,0:T(8,128)(2,1)S(1)}, bf16[128,8,256]{2,1,0:T(8,128)(2,1)}, u32[]{:S(2)}) copy-start(bf16[128,8,256]{2,1,0:T(8,128)(2,1)} %param.12) | copy-start | bytes 1572868
  84.4 27.6 %all-to-all-start.5 = ((bf16[64,16,512]{2,1,0:T(8,128)(2,1)}), bf16[64,16,512]{2,1,0:T(8,128)(2,1)S(1)}, u32[]{:S(2)}, u32[]{:S(2)}) async-start(bf16[64,16,512]{2,1,0:T(8,128)(2,1)} %bitcast.44), calls=%async_computation.5 | async-start | bytes 2097152 | tf_op jit(solution)/shard_map/all_to_all | solution.py:236
  91.1 3.8 copy-start.11
  91.3 3.6 copy-start.5
  92.0 58.5 %collective-permute-start = (bf16[4,16,256]{2,1,0:T(8,128)(2,1)}, bf16[4,16,256]{2,1,0:T(8,128)(2,1)S(1)}, u32[]{:S(2)}, u32[]{:S(2)}) collective-permute-start(bf16[4,16,256]{2,1,0:T(8,128)(2,1)} %get-tuple-element.27), channel_id=1, source_target_pairs={{0,2},{2,4},{4,6},{6,8},{8,10},{10,12},{12,14},{14,16},{16,18},{18... | collective-permute-start | bytes 98312 | tf_op jit(solution)/shard_map/ppermute | solution.py:125
  94.9 55.5 %collective-permute-start.1 = (bf16[4,16,256]{2,1,0:T(8,128)(2,1)}, bf16[4,16,256]{2,1,0:T(8,128)(2,1)}, u32[]{:S(2)}, u32[]{:S(2)}) collective-permute-start(bf16[4,16,256]{2,1,0:T(8,128)(2,1)} %get-tuple-element.28), channel_id=1, source_target_pairs={{2,0},{4,2},{6,4},{8,6},{10,8},{12,10},{14,12},{16,14},{18,16},{20... | collective-permute-start | bytes 98312 | tf_op jit(solution)/shard_map/ppermute | solution.py:127
  100.1 11.8 %copy-start.3 = (bf16[128,64,64]{2,1,0:T(8,128)(2,1)}, bf16[128,64,64]{2,1,0:T(8,128)(2,1)S(1)}, u32[]{:S(2)}) copy-start(bf16[128,64,64]{2,1,0:T(8,128)(2,1)S(1)} %copy.93) | copy-start | bytes 3145732
  112.0 19.1 %copy-start.21 = (s32[128,6]{0,1:T(8,128)S(1)}, s32[128,6]{0,1:T(8,128)}, u32[]{:S(2)}) copy-start(s32[128,6]{0,1:T(8,128)} %param.19) | copy-start | bytes 9220
  112.0 12.2 %copy-start = (bf16[64,16,512]{2,1,0:T(8,128)(2,1)}, bf16[64,16,512]{2,1,0:T(8,128)(2,1)S(1)}, u32[]{:S(2)}) copy-start(bf16[64,16,512]{2,1,0:T(8,128)(2,1)S(1)} %all-to-all-done.5) | copy-start | bytes 3145732
  112.0 28.7 %all-to-all-start.4 = ((bf16[64,16,512]{2,1,0:T(8,128)(2,1)}), bf16[64,16,512]{2,1,0:T(8,128)(2,1)S(1)}, u32[]{:S(2)}, u32[]{:S(2)}) async-start(bf16[64,16,512]{2,1,0:T(8,128)(2,1)} %bitcast.141), calls=%async_computation.4 | async-start | bytes 2097152 | tf_op jit(solution)/shard_map/all_to_all | solution.py:235
  140.7 9.8 %copy-start.1 = (bf16[64,16,512]{2,1,0:T(8,128)(2,1)}, bf16[64,16,512]{2,1,0:T(8,128)(2,1)S(1)}, u32[]{:S(2)}) copy-start(bf16[64,16,512]{2,1,0:T(8,128)(2,1)S(1)} %all-to-all-done.4) | copy-start | bytes 3145732
  140.7 15.7 %copy-start.9 = (bf16[64,8,64]{2,1,0:T(8,128)(2,1)S(1)}, bf16[64,8,64]{2,1,0:T(8,128)(2,1)}, u32[]{:S(2)}) copy-start(bf16[64,8,64]{2,1,0:T(8,128)(2,1)} %param.18) | copy-start | bytes 196612
  140.7 118.1 %all-to-all-start.2 = ((bf16[64,32,512]{2,1,0:T(8,128)(2,1)}), bf16[64,32,512]{2,1,0:T(8,128)(2,1)S(1)}, u32[]{:S(2)}, u32[]{:S(2)}) async-start(bf16[64,32,512]{2,1,0:T(8,128)(2,1)} %bitcast.139), calls=%async_computation.2 | async-start | bytes 4194304 | tf_op jit(solution)/shard_map/all_to_all | solution.py:218
  152.6 13.8 %collective-permute-start.2 = (bf16[136,8,256]{2,1,0:T(8,128)(2,1)}, bf16[136,8,256]{2,1,0:T(8,128)(2,1)}, u32[]{:S(2)}, u32[]{:S(2)}) collective-permute-start(bf16[136,8,256]{2,1,0:T(8,128)(2,1)} %get-tuple-element.23), channel_id=1, source_target_pairs={{0,1},{1,0},{2,3},{3,2},{4,5},{5,4},{6,7},{7,6},{8,9},{9,8},{10,11... | collective-permute-start | bytes 1671176 | tf_op jit(solution)/shard_map/ppermute | solution.py:201
  228.5 12.1 %copy-start.2 = (bf16[64,16,512]{2,1,0:T(8,128)(2,1)S(1)}, bf16[64,16,512]{2,1,0:T(8,128)(2,1)}, u32[]{:S(2)}) copy-start(bf16[64,16,512]{2,1,0:T(8,128)(2,1)} %copy-done.1) | copy-start | bytes 3145732
  228.5 159.3 %collective-permute-start.3 = (f32[64,8,256]{2,1,0:T(8,128)}, f32[64,8,256]{2,1,0:T(8,128)}, u32[]{:S(2)}, u32[]{:S(2)}) collective-permute-start(f32[64,8,256]{2,1,0:T(8,128)} %get-tuple-element.26), channel_id=1, source_target_pairs={{0,1},{1,0},{2,3},{3,2},{4,5},{5,4},{6,7},{7,6},{8,9},{9,8},{10,11... | collective-permute-start | bytes 1572872 | tf_op jit(solution)/shard_map/ppermute | solution.py:206
  258.7 63.8 %all-to-all-start.1 = ((bf16[64,32,512]{2,1,0:T(8,128)(2,1)}), bf16[64,32,512]{2,1,0:T(8,128)(2,1)}, u32[]{:S(2)}, u32[]{:S(2)}) async-start(bf16[64,32,512]{2,1,0:T(8,128)(2,1)} %bitcast.140), calls=%async_computation.1 | async-start | bytes 4194304 | tf_op jit(solution)/shard_map/all_to_all | solution.py:217
  322.4 15.7 %copy-start.14 = (f32[128,64]{1,0:T(8,128)S(1)}, f32[128,64]{1,0:T(8,128)}, u32[]{:S(2)}) copy-start(f32[128,64]{1,0:T(8,128)} %copy.84) | copy-start | bytes 98308
  322.4 15.7 %copy-start.15 = (f32[128,64]{1,0:T(8,128)S(1)}, f32[128,64]{1,0:T(8,128)}, u32[]{:S(2)}) copy-start(f32[128,64]{1,0:T(8,128)} %copy.86) | copy-start | bytes 98308
  322.4 15.7 %copy-start.16 = (f32[128,64]{1,0:T(8,128)S(1)}, f32[128,64]{1,0:T(8,128)}, u32[]{:S(2)}) copy-start(f32[128,64]{1,0:T(8,128)} %copy.87) | copy-start | bytes 98308
  322.5 15.7 %copy-start.17 = (f32[128,64]{1,0:T(8,128)S(1)}, f32[128,64]{1,0:T(8,128)}, u32[]{:S(2)}) copy-start(f32[128,64]{1,0:T(8,128)} %copy.88) | copy-start | bytes 98308
  322.5 15.7 %copy-start.18 = (f32[128,64]{1,0:T(8,128)S(1)}, f32[128,64]{1,0:T(8,128)}, u32[]{:S(2)}) copy-start(f32[128,64]{1,0:T(8,128)} %copy.89) | copy-start | bytes 98308
  338.2 49.7 %copy-start.13 = (bf16[64,8,64]{2,1,0:T(8,128)(2,1)S(1)}, bf16[64,8,64]{2,1,0:T(8,128)(2,1)}, u32[]{:S(2)}) copy-start(bf16[64,8,64]{2,1,0:T(8,128)(2,1)} %fusion.7) | copy-start | bytes 196612
  338.2 49.7 %copy-start.4 = (bf16[128,64,64]{2,1,0:T(8,128)(2,1)S(1)}, bf16[128,64,64]{2,1,0:T(8,128)(2,1)}, u32[]{:S(2)}) copy-start(bf16[128,64,64]{2,1,0:T(8,128)(2,1)} %copy-done.3) | copy-start | bytes 3145732
  338.2 49.7 %copy-start.7 = (f32[64,8,256]{2,1,0:T(8,128)S(1)}, f32[64,8,256]{2,1,0:T(8,128)}, u32[]{:S(2)}) copy-start(f32[64,8,256]{2,1,0:T(8,128)} %get-tuple-element.25) | copy-start | bytes 1572868
  338.2 49.7 %copy-start.12 = (pred[128,256]{1,0:T(8,128)(4,1)S(1)}, pred[128,256]{1,0:T(8,128)(4,1)}, u32[]{:S(2)}) copy-start(pred[128,256]{1,0:T(8,128)(4,1)} %copy-done.11) | copy-start | bytes 98308

commit v2 on v1

--- a/solution.py
+++ b/solution.py
@@ -131,32 +131,233 @@
     return cells
 
 
-def matern(targets, sources):
-    square = 0.0
-    for coord in range(targets.shape[-2]):
-        offset = targets[..., coord, :, None] - sources[..., coord, None, :]
-        square = square + offset * offset
-    scaled = SQRT_THREE / LENGTH_SCALE * jnp.sqrt(square)
-    return (1.0 + scaled) * jnp.exp(-scaled)
-
-
-def far_sum(target_skel, source_skel, source_coef):
-    kernel = matern(
-        target_skel.astype(jnp.float32)[:, None], source_skel.astype(jnp.float32)
-    ).astype(jnp.bfloat16)
-    return jnp.einsum("nfcb,nfab->nca", source_coef, kernel, preferred_element_type=jnp.float32)
-
-
-def slot_table(owner, local, owners, capacity):
-    flat_owner = owner.reshape(-1)
-    flat_local = local.reshape(-1)
-    owner_hits = (flat_owner[:, None] == jnp.arange(owners, dtype=jnp.int32)[None, :]).astype(
-        jnp.int32
+SIDE = 4
+
+
+def coef_kernel(values, basis, transfer, leaf_skel, upper_skel, table):
+    pairs = leaf_skel.shape[0] // 2
+    step_pairs = 4
+
+    def step(i, carry):
+        upper = []
+        for n in range(step_pairs):
+            p = i * step_pairs + n
+            halves = [
+                lax.dot_general(
+                    values[2 * p + k],
+                    basis[2 * p + k],
+                    (((1,), (1,)), ((), ())),
+                    preferred_element_type=F32,
+                )
+                for k in range(2)
+            ]
+            coef = jnp.concatenate(halves, axis=1)
+            skel = [leaf_skel[2 * p + k].astype(F32) for k in range(2)]
+            table[p] = jnp.concatenate([jnp.concatenate(skel, axis=1), coef], axis=0).astype(BF16)
+            stacked = jnp.concatenate([transfer[2 * p], transfer[2 * p + 1]], axis=0)
+            upper.append(jnp.dot(coef.astype(BF16), stacked, preferred_element_type=F32))
+        for n in range(step_pairs // 2):
+            p = i * (step_pairs // 2) + n
+            skel = [upper_skel[2 * p + k].astype(F32) for k in range(2)]
+            coef = jnp.concatenate(upper[2 * n : 2 * n + 2], axis=1)
+            table[pairs + p] = jnp.concatenate(
+                [jnp.concatenate(skel, axis=1), coef], axis=0
+            ).astype(BF16)
+        return carry
+
+    lax.fori_loop(0, pairs // step_pairs, step, 0)
+
+
+def far_kernel(units, rows_each, *refs):
+    pieces, refs = refs[:10], refs[10:]
+    skels, lists, outs = refs[:4], refs[4:8], refs[8:12]
+    table, sums, sems = refs[12:]
+    block = SIDE * rows_each
+    copies = []
+    for n, piece in enumerate(pieces):
+        order, part = divmod(n, 5)
+        start = order * SIDE * block + min(part, 3) * block
+        if part == 3:
+            where, size = table.at[pl.ds(start, block // 2)], block // 2
+        elif part == 4:
+            where, size = table.at[pl.ds(start + block // 2, block // 2)], block // 2
+        else:
+            where, size = table.at[pl.ds(start, block)], block
+        copy = pltpu.make_async_copy(piece, where, sems.at[n])
+        copy.start()
+        copies.append(copy)
+    targets = 2 * skels[0].shape[0]
+    rank = skels[0].shape[2] // 2
+    lane = lax.broadcasted_iota(jnp.int32, (DIM, 2 * rank), 1)
+    low = lane < rank
+
+    def clear(i, carry):
+        sums[i] = jnp.zeros(sums.shape[1:], F32)
+        return carry
+
+    lax.fori_loop(0, sums.shape[0], clear, 0)
+    for copy in copies:
+        copy.wait()
+
+    def turned(array):
+        return jnp.concatenate([array[:, rank:], array[:, :rank]], axis=1)
+
+    for r in range(4):
+        skel, listed, first = skels[r], lists[r], r * (targets + 1)
+
+        def step(i, carry):
+            for quad in range(units // 4):
+                where, left, right, coefs = [], [], [], []
+                for n in range(4):
+                    entry = listed[i * units + quad * 4 + n]
+                    target = entry >> 12
+                    row = (entry >> 1) & 2047
+                    source = table[row].astype(F32)
+                    swap = (entry & 1) != (n % 2)
+                    source = jnp.where(swap, turned(source), source)
+                    keep = low if n % 2 == 0 else jnp.logical_not(low)
+                    form = jnp.where(
+                        jnp.concatenate([keep, keep], axis=0), source_form(source[:DIM]), 0.0
+                    )
+                    coef = jnp.where(keep, source[DIM:], 0.0)
+                    blank = jnp.zeros_like(form)
+                    empty = jnp.zeros_like(coef)
+                    wide = [form, blank] if n < 2 else [blank, form]
+                    right.append(jnp.concatenate(wide, axis=1))
+                    wide = [coef, empty] if n < 2 else [empty, coef]
+                    coefs.append(jnp.concatenate(wide, axis=1))
+                    pair = skel[jnp.minimum(target, targets - 1) >> 1].astype(F32)
+                    pair = jnp.where((target & 1) == 1, turned(pair), pair)
+                    left.append(target_form(pair))
+                    where.append(first + target)
+                left = jnp.concatenate(left, axis=0)[:, :rank].astype(BF16)
+                right = jnp.concatenate(right, axis=0).astype(BF16)
+                square = lax.dot_general(
+                    left, right, (((0,), (0,)), ((), ())), preferred_element_type=F32
+                )
+                fields = lax.dot_general(
+                    jnp.concatenate(coefs, axis=0).astype(BF16),
+                    matern_of_square(square),
+                    (((1,), (1,)), ((), ())),
+                    preferred_element_type=F32,
+                )
+                for n in range(4):
+                    sums[where[n]] += fields[DIM * n : DIM * (n + 1)]
+            return carry
+
+        count = listed[listed.shape[0] - 128]
+        lax.fori_loop(0, (count + units - 1) // units, step, 0)
+
+        def pack(p, carry):
+            outs[r][p] = jnp.concatenate([sums[first + 2 * p], sums[first + 2 * p + 1]], axis=1)
+            return carry
+
+        lax.fori_loop(0, targets // 2, pack, 0)
+
+
+def final_kernel(counts, transfer, basis, near_mine, near_theirs, *refs):
+    parts, out = refs[:4], refs[4]
+    leaves = out.shape[0]
+    half = leaves // 2
+    rank = transfer.shape[1]
+    core = counts[leaves]
+    lane = lax.broadcasted_iota(jnp.int32, out.shape[1:], 1)
+
+    def total(p):
+        return (parts[0][p] + parts[1][p]) + (parts[2][p] + parts[3][p])
+
+    def step(i, carry):
+        for n in range(2):
+            upper = total(half + 2 * i + n).astype(BF16)
+            for m in range(2):
+                pair = 4 * i + 2 * n + m
+                field = total(pair)
+                for k in range(2):
+                    leaf = 2 * pair + k
+                    down = lax.dot_general(
+                        upper[:, m * rank : (m + 1) * rank],
+                        transfer[leaf],
+                        (((1,), (1,)), ((), ())),
+                        preferred_element_type=F32,
+                    )
+                    here = (field[:, k * rank : (k + 1) * rank] + down).astype(BF16)
+                    result = jnp.dot(here, basis[leaf], preferred_element_type=F32)
+                    owner = leaf // half
+                    inner = leaf - owner * half
+                    near = jnp.where(
+                        owner == core, near_mine[inner][: out.shape[1]], near_theirs[inner]
+                    )
+                    out[leaf] = jnp.where(lane < counts[leaf], result + near, 0.0)
+        return carry
+
+    lax.fori_loop(0, leaves // 8, step, 0)
+
+
+def z_shift(r):
+    return [
+        (SIDE * k + z, SIDE * k + (z - r) % SIDE) for k in range(SIDE * SIDE) for z in range(SIDE)
+    ]
+
+
+def line_gather(block, axis):
+    stride = SIDE * SIDE if axis == 0 else SIDE
+
+    def moved(array, by):
+        pairs = []
+        for i in range(SIDE**3):
+            at = i // stride % SIDE
+            pairs.append((i, i + ((at + by) % SIDE - at) * stride))
+        return lax.ppermute(array, "leaf", pairs)
+
+    cut = block.shape[0] // 2
+    ahead, behind = moved(block, -1), moved(block, 1)
+    return [block, ahead, behind, moved(behind[:cut], 1), moved(ahead[cut:], -1)]
+
+
+def plane_gather(block, axes):
+    first = line_gather(block, axes[0])
+    return line_gather(jnp.concatenate(first, axis=0), axes[1])
+
+
+def unit_lists(leaf_owner, leaf_local, upper_owner, upper_local, rows_each, capacity):
+    me = lax.axis_index("leaf")
+    leaves, far = leaf_owner.shape
+    parents = upper_owner.shape[0]
+    owner = jnp.concatenate([leaf_owner.reshape(-1), upper_owner.reshape(-1)])
+    local = jnp.concatenate([leaf_local.reshape(-1), leaves + upper_local.reshape(-1)])
+    target = jnp.arange((leaves + parents) * far, dtype=jnp.int32) // far
+
+    def slot(offset):
+        return jnp.where(offset == 2, 3, jnp.where(offset == 3, 2, offset))
+
+    x = slot((owner // (SIDE * SIDE) - me // (SIDE * SIDE)) % SIDE)
+    y = slot((owner // SIDE - me // SIDE) % SIDE)
+    pair = local // 2
+    in_first = pair < rows_each
+    row = jnp.where(
+        in_first,
+        (x * SIDE + y) * rows_each + pair,
+        SIDE * SIDE * rows_each + (y * SIDE + x) * rows_each + pair - rows_each,
     )
-    before = jnp.cumsum(owner_hits, axis=0) - owner_hits
-    slot_index = jnp.sum(before * owner_hits, axis=1)
-    wanted = jnp.zeros((owners, capacity), jnp.int32).at[flat_owner, slot_index].set(flat_local)
-    return (wanted, flat_owner, slot_index)
+    code = (target << 12) | (row << 1) | (local & 1)
+    hits = (owner[:, None] % SIDE == jnp.arange(SIDE, dtype=jnp.int32)[None, :]).astype(BF16)
+    number = owner.shape[0]
+    order = jnp.arange(number, dtype=jnp.int32)
+    before = (order[None, :] < order[:, None]).astype(BF16)
+    rank = jnp.sum(jnp.dot(before, hits, preferred_element_type=F32) * hits.astype(F32), axis=1)
+    spot = (rank.astype(jnp.int32)[:, None] == jnp.arange(capacity, dtype=jnp.int32)[None, :]).astype(
+        BF16
+    )
+    digits = jnp.stack(
+        [(code & 127), ((code >> 7) & 127), (code >> 14), jnp.ones_like(code)], axis=0
+    ).astype(BF16)
+    weights = (hits.T[:, None, :] * digits[None]).reshape(SIDE * 4, number)
+    found = jnp.dot(weights, spot, preferred_element_type=F32).astype(jnp.int32)
+    found = found.reshape(SIDE, 4, capacity)
+    codes = found[:, 0] + (found[:, 1] << 7) + (found[:, 2] << 14)
+    codes = codes + jnp.where(found[:, 3] == 0, (leaves + parents) << 12, 0)
+    counts = jnp.sum(found[:, 3], axis=1)
+    return jnp.concatenate([codes, jnp.broadcast_to(counts[:, None], (SIDE, 128))], axis=1)
 
 
 def body(
@@ -177,80 +378,79 @@
     leaf_size = points.shape[2]
     columns = values.shape[1]
     rank = leaf_basis.shape[1]
-    far_count = far_owner.shape[1]
-    par_dev = leaf_dev // 2
-    owners = lax.axis_size("leaf")
+    near_count = near_list.shape[1]
+    half = leaf_dev // 2
+    pairs = leaf_dev // 2 + leaf_dev // 4
+    rows_each = pairs // 2
+    capacity = leaf_dev * far_owner.shape[1] * 3 // 4
+    me = lax.axis_index("leaf")
+    core = lax.axis_index("rhs")
+    swap = [(0, 1), (1, 0)]
+    vmem = pl.BlockSpec(memory_space=pltpu.VMEM)
+    smem = pl.BlockSpec(memory_space=pltpu.SMEM)
+    anywhere = pl.BlockSpec(memory_space=pl.ANY)
+    params = pltpu.CompilerParams(vmem_limit_bytes=40 * 2**20)
+
     point_live = lax.broadcasted_iota(jnp.int32, (leaf_dev, leaf_size), 1) < counts[:, None]
     masked = jnp.where(point_live[:, None, :], values, jnp.zeros_like(values))
-    leaf_coef = jnp.einsum(
-        "lcp,lkp->lck", masked, leaf_basis, preferred_element_type=jnp.float32
-    ).astype(jnp.bfloat16)
-    child_coef = leaf_coef.reshape(par_dev, 2, columns, rank)
-    child_transfer = transfer.reshape(par_dev, 2, rank, rank)
-    upper_coef = jnp.einsum(
-        "pjck,pjkm->pcm", child_coef, child_transfer, preferred_element_type=jnp.float32
-    ).astype(jnp.bfloat16)
+    table = pl.pallas_call(
+        coef_kernel,
+        out_shape=jax.ShapeDtypeStruct((pairs, 2 * DIM, 2 * rank), BF16),
+        in_specs=[vmem] * 5,
+        out_specs=vmem,
+        compiler_params=params,
+        cost_estimate=pl.CostEstimate(flops=10**8, bytes_accessed=6 * 2**20, transcendentals=0),
+        name="coef",
+    )(masked, leaf_basis, transfer, leaf_skeleton, upper_skeleton)
+    pieces = plane_gather(table[:rows_each], (1, 0)) + plane_gather(table[rows_each:], (0, 1))
+
+    lists = unit_lists(far_owner, far_local, upper_owner, upper_local, rows_each, capacity)
+    skel = table[:, :DIM]
+    all_lists, all_skels = [lists[me % SIDE]], [skel]
+    for r in range(1, SIDE):
+        all_lists.append(lax.ppermute(lists[(me - r) % SIDE], "leaf", z_shift(r)))
+        all_skels.append(lax.ppermute(skel, "leaf", z_shift(r)))
+
     bundle = jnp.concatenate([points, masked], axis=1)
     extended = with_halo(bundle, (("leaf", 0),), HALO)
-    first_leaf = lax.axis_index("leaf") * leaf_dev - HALO
-    near_count = near_list.shape[1]
-    half = leaf_dev // 2
-    core = lax.axis_index("rhs")
-    swap = [(0, 1), (1, 0)]
     own = extended[:, DIM:]
     cols = jnp.concatenate([own, lax.ppermute(own, "rhs", swap)], axis=1)
+    first_leaf = me * leaf_dev - HALO
     chosen = lax.dynamic_slice_in_dim(near_list - first_leaf, core * half, half, axis=0)
     ids = jnp.concatenate([chosen.reshape(-1), (core * half + HALO)[None]]).astype(jnp.int32)
     near_half = near_field(ids, extended[:, :DIM], cols, half, near_count)
-    near_mine = near_half[:, :columns]
     near_theirs = lax.ppermute(near_half[:, columns:], "rhs", swap)
-    near_part = jnp.where(
-        core == 0,
-        jnp.concatenate([near_mine, near_theirs], axis=0),
-        jnp.concatenate([near_theirs, near_mine], axis=0),
-    )
-    leaf_rows = leaf_coef.reshape(leaf_dev, columns * rank)
-    leaf_skel_rows = leaf_skeleton.reshape(leaf_dev, DIM * rank)
-    capacity = max(2, 2 * leaf_dev * far_count // owners)
-    wanted, flat_owner, slot_index = slot_table(far_owner, far_local, owners, capacity)
-    asked = lax.all_to_all(wanted, "leaf", split_axis=0, concat_axis=0, tiled=True)
-    got_coef = lax.all_to_all(leaf_rows[asked], "leaf", split_axis=0, concat_axis=0, tiled=True)
-    got_skel = lax.all_to_all(
-        leaf_skel_rows[asked], "leaf", split_axis=0, concat_axis=0, tiled=True
-    )
-    picked_coef = got_coef[flat_owner, slot_index]
-    picked_skel = got_skel[flat_owner, slot_index]
-    leaf_far = far_sum(
-        leaf_skeleton,
-        picked_skel.reshape(leaf_dev, far_count, DIM, rank),
-        picked_coef.reshape(leaf_dev, far_count, columns, rank),
-    )
-    upper_rows = upper_coef.reshape(par_dev, columns * rank)
-    upper_skel_rows = upper_skeleton.reshape(par_dev, DIM * rank)
-    upper_capacity = max(2, 2 * par_dev * far_count // owners)
-    upper_wanted, upper_flat, upper_slot = slot_table(
-        upper_owner, upper_local, owners, upper_capacity
-    )
-    asked = lax.all_to_all(upper_wanted, "leaf", split_axis=0, concat_axis=0, tiled=True)
-    got_upper = lax.all_to_all(upper_rows[asked], "leaf", split_axis=0, concat_axis=0, tiled=True)
-    got_upper_skel = lax.all_to_all(
-        upper_skel_rows[asked], "leaf", split_axis=0, concat_axis=0, tiled=True
-    )
-    chosen_coef = got_upper[upper_flat, upper_slot]
-    chosen_skel = got_upper_skel[upper_flat, upper_slot]
-    upper_field = far_sum(
-        upper_skeleton,
-        chosen_skel.reshape(par_dev, far_count, DIM, rank),
-        chosen_coef.reshape(par_dev, far_count, columns, rank),
-    ).astype(jnp.bfloat16)
-    spread = jnp.repeat(upper_field, 2, axis=0)
-    leaf_field = (
-        leaf_far + jnp.einsum("lcm,lkm->lck", spread, transfer, preferred_element_type=jnp.float32)
-    ).astype(jnp.bfloat16)
-    far_part = jnp.einsum(
-        "lck,lkp->lcp", leaf_field, leaf_basis, preferred_element_type=jnp.float32
-    )
-    return jnp.where(point_live[:, None, :], far_part + near_part, 0.0)
+
+    part = jax.ShapeDtypeStruct((pairs, columns, 2 * rank), F32)
+    parts = pl.pallas_call(
+        functools.partial(far_kernel, 16, rows_each),
+        out_shape=[part] * 4,
+        in_specs=[anywhere] * 10 + [vmem] * 4 + [smem] * 4,
+        out_specs=[vmem] * 4,
+        scratch_shapes=[
+            pltpu.VMEM((2 * SIDE * SIDE * rows_each, 2 * DIM, 2 * rank), BF16),
+            pltpu.VMEM((4 * (2 * pairs + 1), columns, rank), F32),
+            pltpu.SemaphoreType.DMA((10,)),
+        ],
+        compiler_params=params,
+        cost_estimate=pl.CostEstimate(
+            flops=3 * 10**10, bytes_accessed=10 * 2**20, transcendentals=0
+        ),
+        name="far",
+    )(*pieces, *all_skels, *all_lists)
+    mine = [parts[0]]
+    for r in range(1, SIDE):
+        mine.append(lax.ppermute(parts[r], "leaf", z_shift(-r)))
+
+    limits = jnp.concatenate([counts, core[None]]).astype(jnp.int32)
+    return pl.pallas_call(
+        final_kernel,
+        out_shape=jax.ShapeDtypeStruct((leaf_dev, columns, leaf_size), F32),
+        in_specs=[smem] + [vmem] * 8,
+        out_specs=vmem,
+        compiler_params=params,
+        name="final",
+    )(limits, transfer, leaf_basis, near_half, near_theirs, *mine)
 
 
 def solution(mesh):

time: 394 us -> 303 us (0.77)
  Pallas kernels: 59.7 us -> 182 us
  local copies, waits for them, and re-layouts: 151 us -> 29.6 us
  matrix products: 86.4 us -> 3.32 us
  other arithmetic: 24.3 us -> 6.46 us
  waiting for transfers between devices: 3.17 us -> 20.1 us
  starting transfers between devices: 67.7 us -> 58.1 us
    pallas_call x0 -> x3, Pallas kernels: none -> 123 us  [the longest x1 78.7 us: body(): pl.pallas_call(functools.partial(far_kernel, 16, rows_each), out_shape=[p...]
    dot_general x5 -> x2, matrix products: 86.4 us -> 3.32 us  [the longest x1 2.44 us: unit_lists(): found = jnp.dot(weights, spot, preferred_element_type=F32).astype(jnp.int32)]
    gather x8 -> x0, local copies, waits for them, and re-layouts: 65.2 us -> none  [the longest x1 13.5 us: body(): picked_coef = got_coef[flat_owner, slot_index]]
    all_to_all x6 -> x0, starting transfers between devices: 59.7 us -> none  [the longest x1 12 us: body(): lax.all_to_all(upper_wanted, 'leaf', split_axis=0, concat_axis=0, tiled=T...]
    ppermute x0 -> x25, starting transfers between devices: none -> 41.2 us  [the longest x16 26.6 us: moved(): return lax.ppermute(array, 'leaf', pairs)]
    scatter x1 -> x0, local copies, waits for them, and re-layouts: 25.2 us -> none  [slot_table(): jnp.zeros((owners, capacity), jnp.int32).at[flat_owner, slot_index]]
    slice x6 -> x11, local copies, waits for them, and re-layouts: 29.7 us -> 8.85 us  [the longest x4 3.9 us: line_gather(): ahead[cut:]]
    ppermute x0 -> x25, waiting for transfers between devices: none -> 20.1 us  [the longest x3 15.5 us: body(): mine.append(lax.ppermute(parts[r], 'leaf', z_shift(-r)))]
  transfers between devices with their start and end apart: 10 -> 29, of which waited for: 1 -> 6; matrix products, arithmetic and copies ran while one was open for 58% -> 10% of each run, Pallas kernels for 15% -> 46%
where the time goes in v2:
time: 303 us; the launch traced here: 300 us
  Pallas kernels  182 us (60%)
  starting transfers between devices  58.1 us (19%)
  local copies, waits for them, and re-layouts  29.6 us (10%)
  waiting for transfers between devices  20.1 us (7%)
  other arithmetic  6.46 us (2%)
  matrix products  3.32 us (1%)
    pallas_call x1, Pallas kernels, body(): pl.pallas_call(functools.partial(far_kernel, 16, rows_each), out_shape=[p...  78.7 us
    pallas_call x1, Pallas kernels, near_field(): pl.pallas_call(functools.partial(near_kernel, near, leaves), out_shape=ja...  59.1 us
    pallas_call x1, Pallas kernels, body(): pl.pallas_call(final_kernel, out_shape=jax.ShapeDtypeStruct((leaf_dev, co...  28.9 us
    ppermute x16, starting transfers between devices, moved(): return lax.ppermute(array, 'leaf', pairs)  26.6 us
    pallas_call x1, Pallas kernels, body(): pl.pallas_call(coef_kernel, out_shape=jax.ShapeDtypeStruct((pairs, 2 * DI...  15.5 us
    ppermute x3, waiting for transfers between devices, body(): mine.append(lax.ppermute(parts[r], 'leaf', z_shift(-r)))  15.5 us
    unnamed x49, local copies, waits for them, and re-layouts  15.2 us
    ppermute x3, starting transfers between devices, body(): mine.append(lax.ppermute(parts[r], 'leaf', z_shift(-r)))  11 us
  transfers between devices with their start and end apart: 29, of which 6 were waited for; matrix products, arithmetic and copies ran while one was open for 10% of the time, Pallas kernels for 46%

profile of v2, /device:TPU:1, one launch (start us, length us, event | category | flops | bytes accessed | tf_op | source)
XLA Modules:
  0.0 300.3 jit_solution(17625758948950696781)
XLA Ops:
  0.8 4.0 %copy.35.transfer = bf16[128,64,64]{2,1,0:T(8,128)(2,1)S(1)} copy(bf16[128,64,64]{0,2,1:T(8,128)(2,1)} %param.16) | data formatting | bytes 2097152 | tf_op args[4]
  5.0 1.2 broadcast_select_fusion.values
  6.2 2.2 copy-done
  8.4 15.5 %coef.1 = bf16[96,16,128]{2,1,0:T(8,128)(2,1)S(1)} custom-call(bf16[128,8,256]{2,1,0:T(8,128)(2,1)S(1)} %broadcast_select_fusion.values, bf16[128,64,256]{2,1,0:T(8,128)(2,1)S(1)} %copy-done, bf16[128,64,64]{2,1,0:T(8,128)(2,1)S(1)} %copy.35.transfer, bf16[128,8,64]{2,1,0:T(8,128)(2,1)S(1)} %copy.28.leaf_skel, bf16[64,8,64]{2,1,0:T(8,128)(2,1)S(1)} %copy-done.3), custom_call_target="tpu_custom_call" | custom-call | flops 100000000 | bytes 6291456 | tf_op jit(solution)/shard_map/coef/pallas_call | solution.py:396
  23.9 1.0 fusion.29
  25.0 3.3 %collective-permute-start.12 = (bf16[48,16,128]{2,1,0:T(8,128)(2,1)}, bf16[48,16,128]{2,1,0:T(8,128)(2,1)}, u32[]{:S(2)}, u32[]{:S(2)}) collective-permute-start(bf16[48,16,128]{2,1,0:T(8,128)(2,1)} %get-tuple-element.23), channel_id=1, source_target_pairs={{0,96},{2,98},{4,100},{6,102},{8,104},{10,106},{12,108},{14,110},{... | collective-permute-start | bytes 589832 | tf_op jit(solution)/shard_map/ppermute | solution.py:310
  28.3 2.7 collective-permute-start.4
  31.7 4.3 %collective-permute-start = (bf16[4,16,256]{2,1,0:T(8,128)(2,1)}, bf16[4,16,256]{2,1,0:T(8,128)(2,1)}, u32[]{:S(2)}, u32[]{:S(2)}) collective-permute-start(bf16[4,16,256]{2,1,0:T(8,128)(2,1)} %get-tuple-element.21), channel_id=1, source_target_pairs={{0,2},{2,4},{4,6},{6,8},{8,10},{10,12},{12,14},{14,16},{16,18},{18... | collective-permute-start | bytes 98312 | tf_op jit(solution)/shard_map/ppermute | solution.py:125
  36.6 0.9 fusion.5
  39.0 2.4 fusion.4
  41.4 1.4 reshape.1090
  42.8 1.4 collective-permute-start.1
  44.3 0.9 slice.90
  45.2 5.8 %collective-permute-start.14 = (bf16[24,16,128]{2,1,0:T(8,128)(2,1)S(1)}, bf16[24,16,128]{2,1,0:T(8,128)(2,1)S(1)}, u32[]{:S(2)}, u32[]{:S(2)}) collective-permute-start(bf16[24,16,128]{2,1,0:T(8,128)(2,1)S(1)} %slice.90), channel_id=1, source_target_pairs={{0,32},{2,34},{4,36},{6,38},{8,40},{10,42},{12,44},{14,46},{16,48}... | collective-permute-start | bytes 294920 | tf_op jit(solution)/shard_map/ppermute | solution.py:310
  51.0 0.9 slice.91
  51.9 1.1 collective-permute-start.15
  53.0 0.9 slice.85
  53.9 1.6 constant_dynamic-update-slice_fusion.8
  55.5 1.6 constant_dynamic-update-slice_fusion.7
  57.1 0.9 slice.86
  58.0 1.6 constant_dynamic-update-slice_fusion.3
  59.6 1.6 constant_dynamic-update-slice_fusion.2
  61.2 2.7 collective-permute-start.7
  65.2 2.7 collective-permute-start.16
  69.6 2.2 collective-permute-start.8
  74.2 0.9 pad_maximum_fusion
  75.0 1.1 fusion.28
  76.9 4.8 %collective-permute-start.2 = (bf16[136,8,256]{2,1,0:T(8,128)(2,1)}, bf16[136,8,256]{2,1,0:T(8,128)(2,1)}, u32[]{:S(2)}, u32[]{:S(2)}) collective-permute-start(bf16[136,8,256]{2,1,0:T(8,128)(2,1)} %get-tuple-element.19), channel_id=1, source_target_pairs={{0,1},{1,0},{2,3},{3,2},{4,5},{5,4},{6,7},{7,6},{8,9},{9,8},{10,11... | collective-permute-start | bytes 1671176 | tf_op jit(solution)/shard_map/ppermute | solution.py:417
  81.7 1.2 collective-permute-done.17.refs_7_
  83.6 2.6 collective-permute-done.9.refs_2_
  86.3 1.1 collective-permute-start.25
  87.7 1.0 slice.92
  88.7 1.1 slice.93
  89.8 1.0 slice.87
  90.8 1.0 slice.88
  92.1 2.7 collective-permute-start.19
  95.2 2.2 collective-permute-start.11
  97.5 1.6 collective-permute-start.22
  99.1 1.3 pad_maximum_fusion.1.cols
  100.4 59.1 %near.1.near_mine = f32[64,16,256]{2,1,0:T(8,128)S(1)} custom-call(s32[385]{0:T(512)S(1)} %pad_add_fusion.ids, bf16[136,8,256]{2,1,0:T(8,128)(2,1)S(1)} %copy-done.2, bf16[136,16,256]{2,1,0:T(8,128)(2,1)S(1)} %pad_maximum_fusion.1.cols), custom_call_target="tpu_custom_call" | custom-call | flops 1610612736 | bytes 4194304 | tf_op jit(solution)/shard_map/near/pallas_call | solution.py:98
  159.6 6.4 %collective-permute-start.3 = (f32[64,8,256]{2,1,0:T(8,128)S(1)}, f32[64,8,256]{2,1,0:T(8,128)S(1)}, u32[]{:S(2)}, u32[]{:S(2)}) collective-permute-start(f32[64,8,256]{2,1,0:T(8,128)S(1)} %slice.83), channel_id=1, source_target_pairs={{0,1},{1,0},{2,3},{3,2},{4,5},{5,4},{6,7},{7,6},{8,9},{9,8},{10,11... | collective-permute-start | bytes 1572872 | tf_op jit(solution)/shard_map/ppermute | solution.py:422
  166.1 78.7 %far.1 = (f32[96,8,128]{2,1,0:T(8,128)S(1)}, f32[96,8,128]{2,1,0:T(8,128)S(1)}, f32[96,8,128]{2,1,0:T(8,128)S(1)}, f32[96,8,128]{2,1,0:T(8,128)S(1)}) custom-call(bf16[192,16,128]{2,1,0:T(8,128)(2,1)S(1)} %copy-done.4, bf16[192,16,128]{2,1,0:T(8,128)(2,1)} %collective-permute-done.8.refs_1_, bf16[192,16,128]{2,1,0:T(8,128)(2,1)} %collective-permute-done.9.refs_2_, ...), custom_call_target="tpu_custom_call" | custom-call | flops 30000001024 | bytes 10485760 | tf_op jit(solution)/shard_map/far/pallas_call | solution.py:425
  244.9 8.5 %collective-permute-start.26 = (f32[96,8,128]{2,1,0:T(8,128)S(1)}, f32[96,8,128]{2,1,0:T(8,128)S(1)}, u32[]{:S(2)}, u32[]{:S(2)}) collective-permute-start(f32[96,8,128]{2,1,0:T(8,128)S(1)} %get-tuple-element.10), channel_id=1, source_target_pairs={{0,2},{2,4},{4,6},{6,0},{8,10},{10,12},{12,14},{14,8},{16,18},{18,... | collective-permute-start | bytes 1179656 | tf_op jit(solution)/shard_map/ppermute | solution.py:443
  253.4 2.5 collective-permute-start.28
  255.9 6.0 %collective-permute-done.26.refs_1_ = f32[96,8,128]{2,1,0:T(8,128)S(1)} collective-permute-done((f32[96,8,128]{2,1,0:T(8,128)S(1)}, f32[96,8,128]{2,1,0:T(8,128)S(1)}, u32[]{:S(2)}, u32[]{:S(2)}) %collective-permute-start.26) | collective-permute-done | bytes 393248 | tf_op jit(solution)/shard_map/ppermute | solution.py:443
  261.9 8.4 %collective-permute-done.27.refs_2_ = f32[96,8,128]{2,1,0:T(8,128)S(1)} collective-permute-done((f32[96,8,128]{2,1,0:T(8,128)S(1)}, f32[96,8,128]{2,1,0:T(8,128)S(1)}, u32[]{:S(2)}, u32[]{:S(2)}) %collective-permute-start.27) | collective-permute-done | bytes 393248 | tf_op jit(solution)/shard_map/ppermute | solution.py:443
  270.3 1.1 collective-permute-done.28.refs_3_
  271.4 28.9 %final.1 = f32[128,8,256]{2,1,0:T(8,128)} custom-call(s32[129]{0:T(256)S(1)} %pad_add_fusion.1.counts, bf16[128,64,64]{2,1,0:T(8,128)(2,1)S(1)} %copy.35.transfer, bf16[128,64,256]{2,1,0:T(8,128)(2,1)S(1)} %copy-done.1, f32[64,16,256]{2,1,0:T(8,128)S(1)} %near.1.near_mine, f32[64,8,256]{2,1,0:T(8,128)S(1)} %collective-permute-done.3.near_theirs, ...), custom_call_target="tpu_custom_call" | custom-call | tf_op jit(solution)/shard_map/final/pallas_call | solution.py:446
  (113 shorter events, 11.7 us)
Async XLA Ops:
  0.0 4.8 %copy-start.9 = (bf16[128,8,64]{0,2,1:T(8,128)(2,1)S(1)}, bf16[128,8,64]{0,2,1:T(8,128)(2,1)}, u32[]{:S(2)}) copy-start(bf16[128,8,64]{0,2,1:T(8,128)(2,1)} %param.17) | copy-start | bytes 393220
  0.8 5.4 %copy-start.3 = (bf16[64,8,64]{2,1,0:T(8,128)(2,1)S(1)}, bf16[64,8,64]{2,1,0:T(8,128)(2,1)}, u32[]{:S(2)}) copy-start(bf16[64,8,64]{2,1,0:T(8,128)(2,1)} %upper_skel.1) | copy-start | bytes 196612
  6.2 2.2 copy-start
  8.4 22.6 %copy-start.6 = (bf16[128,8,256]{2,1,0:T(8,128)(2,1)S(1)}, bf16[128,8,256]{2,1,0:T(8,128)(2,1)}, u32[]{:S(2)}) copy-start(bf16[128,8,256]{2,1,0:T(8,128)(2,1)} %param.12) | copy-start | bytes 1572868
  23.9 12.0 %copy-start.10 = (s32[128,8]{0,1:T(8,128)S(1)}, s32[128,8]{0,1:T(8,128)}, u32[]{:S(2)}) copy-start(s32[128,8]{0,1:T(8,128)} %param.20) | copy-start | bytes 12292
  23.9 12.3 %copy-start.11 = (s32[64,8]{0,1:T(8,128)S(1)}, s32[64,8]{0,1:T(8,128)}, u32[]{:S(2)}) copy-start(s32[64,8]{0,1:T(8,128)} %param.22) | copy-start | bytes 6148
  25.0 20.2 %collective-permute-start.12 = (bf16[48,16,128]{2,1,0:T(8,128)(2,1)}, bf16[48,16,128]{2,1,0:T(8,128)(2,1)}, u32[]{:S(2)}, u32[]{:S(2)}) collective-permute-start(bf16[48,16,128]{2,1,0:T(8,128)(2,1)} %get-tuple-element.23), channel_id=1, source_target_pairs={{0,96},{2,98},{4,100},{6,102},{8,104},{10,106},{12,108},{14,110},{... | collective-permute-start | bytes 589832 | tf_op jit(solution)/shard_map/ppermute | solution.py:310
  28.3 14.6 %collective-permute-start.13 = (bf16[48,16,128]{2,1,0:T(8,128)(2,1)}, bf16[48,16,128]{2,1,0:T(8,128)(2,1)}, u32[]{:S(2)}, u32[]{:S(2)}) collective-permute-start(bf16[48,16,128]{2,1,0:T(8,128)(2,1)} %get-tuple-element.23), channel_id=1, source_target_pairs={{0,32},{2,34},{4,36},{6,38},{8,40},{10,42},{12,44},{14,46},{16,48}... | collective-permute-start | bytes 589832 | tf_op jit(solution)/shard_map/ppermute | solution.py:310
  28.3 28.8 %collective-permute-start.4 = (bf16[48,16,128]{2,1,0:T(8,128)(2,1)}, bf16[48,16,128]{2,1,0:T(8,128)(2,1)}, u32[]{:S(2)}, u32[]{:S(2)}) collective-permute-start(bf16[48,16,128]{2,1,0:T(8,128)(2,1)} %get-tuple-element.26), channel_id=1, source_target_pairs={{0,24},{2,26},{4,28},{6,30},{8,0},{10,2},{12,4},{14,6},{16,8},{18,... | collective-permute-start | bytes 589832 | tf_op jit(solution)/shard_map/ppermute | solution.py:310
  31.0 20.9 %collective-permute-start.5 = (bf16[48,16,128]{2,1,0:T(8,128)(2,1)}, bf16[48,16,128]{2,1,0:T(8,128)(2,1)}, u32[]{:S(2)}, u32[]{:S(2)}) collective-permute-start(bf16[48,16,128]{2,1,0:T(8,128)(2,1)} %get-tuple-element.26), channel_id=1, source_target_pairs={{0,8},{2,10},{4,12},{6,14},{8,16},{10,18},{12,20},{14,22},{16,24},... | collective-permute-start | bytes 589832 | tf_op jit(solution)/shard_map/ppermute | solution.py:310
  31.6 5.8 %copy-start.12 = (s32[128,8]{0,1:T(8,128)S(1)}, s32[128,8]{0,1:T(8,128)}, u32[]{:S(2)}) copy-start(s32[128,8]{0,1:T(8,128)} %param.21) | copy-start | bytes 12292
  31.7 38.0 %collective-permute-start = (bf16[4,16,256]{2,1,0:T(8,128)(2,1)}, bf16[4,16,256]{2,1,0:T(8,128)(2,1)}, u32[]{:S(2)}, u32[]{:S(2)}) collective-permute-start(bf16[4,16,256]{2,1,0:T(8,128)(2,1)} %get-tuple-element.21), channel_id=1, source_target_pairs={{0,2},{2,4},{4,6},{6,8},{8,10},{10,12},{12,14},{14,16},{16,18},{18... | collective-permute-start | bytes 98312 | tf_op jit(solution)/shard_map/ppermute | solution.py:125
  36.1 1.6 copy-start.13
  39.0 35.2 %copy-start.7 = (bf16[128,8,256]{2,1,0:T(8,128)(2,1)S(1)}, bf16[128,8,256]{2,1,0:T(8,128)(2,1)}, u32[]{:S(2)}) copy-start(bf16[128,8,256]{2,1,0:T(8,128)(2,1)} %param.12) | copy-start | bytes 1572868
  42.8 29.0 %copy-start.8 = (s32[4,4,768]{2,1,0:T(4,128)S(1)}, s32[4,4,768]{2,1,0:T(4,128)}, u32[]{:S(2)}) copy-start(s32[4,4,768]{2,1,0:T(4,128)} %reshape.1090) | copy-start | bytes 147460
  42.8 31.2 %collective-permute-start.1 = (bf16[4,16,256]{2,1,0:T(8,128)(2,1)}, bf16[4,16,256]{2,1,0:T(8,128)(2,1)}, u32[]{:S(2)}, u32[]{:S(2)}) collective-permute-start(bf16[4,16,256]{2,1,0:T(8,128)(2,1)} %get-tuple-element.22), channel_id=1, source_target_pairs={{2,0},{4,2},{6,4},{8,6},{10,8},{12,10},{14,12},{16,14},{18,16},{20... | collective-permute-start | bytes 98312 | tf_op jit(solution)/shard_map/ppermute | solution.py:127
  45.2 16.1 %collective-permute-start.14 = (bf16[24,16,128]{2,1,0:T(8,128)(2,1)S(1)}, bf16[24,16,128]{2,1,0:T(8,128)(2,1)S(1)}, u32[]{:S(2)}, u32[]{:S(2)}) collective-permute-start(bf16[24,16,128]{2,1,0:T(8,128)(2,1)S(1)} %slice.90), channel_id=1, source_target_pairs={{0,32},{2,34},{4,36},{6,38},{8,40},{10,42},{12,44},{14,46},{16,48}... | collective-permute-start | bytes 294920 | tf_op jit(solution)/shard_map/ppermute | solution.py:310
  51.9 12.7 %collective-permute-start.15 = (bf16[24,16,128]{2,1,0:T(8,128)(2,1)S(1)}, bf16[24,16,128]{2,1,0:T(8,128)(2,1)S(1)}, u32[]{:S(2)}, u32[]{:S(2)}) collective-permute-start(bf16[24,16,128]{2,1,0:T(8,128)(2,1)S(1)} %slice.91), channel_id=1, source_target_pairs={{0,96},{2,98},{4,100},{6,102},{8,104},{10,106},{12,108},{14,110},{... | collective-permute-start | bytes 294920 | tf_op jit(solution)/shard_map/ppermute | solution.py:310
  57.1 8.1 %collective-permute-start.6 = (bf16[24,16,128]{2,1,0:T(8,128)(2,1)S(1)}, bf16[24,16,128]{2,1,0:T(8,128)(2,1)S(1)}, u32[]{:S(2)}, u32[]{:S(2)}) collective-permute-start(bf16[24,16,128]{2,1,0:T(8,128)(2,1)S(1)} %slice.85), channel_id=1, source_target_pairs={{0,8},{2,10},{4,12},{6,14},{8,16},{10,18},{12,20},{14,22},{16,24},... | collective-permute-start | bytes 294920 | tf_op jit(solution)/shard_map/ppermute | solution.py:310
  61.2 7.3 %collective-permute-start.7 = (bf16[24,16,128]{2,1,0:T(8,128)(2,1)S(1)}, bf16[24,16,128]{2,1,0:T(8,128)(2,1)S(1)}, u32[]{:S(2)}, u32[]{:S(2)}) collective-permute-start(bf16[24,16,128]{2,1,0:T(8,128)(2,1)S(1)} %slice.86), channel_id=1, source_target_pairs={{0,24},{2,26},{4,28},{6,30},{8,0},{10,2},{12,4},{14,6},{16,8},{18,... | collective-permute-start | bytes 294920 | tf_op jit(solution)/shard_map/ppermute | solution.py:310
  65.2 17.6 %collective-permute-start.17 = (bf16[192,16,128]{2,1,0:T(8,128)(2,1)}, bf16[192,16,128]{2,1,0:T(8,128)(2,1)}, u32[]{:S(2)}, u32[]{:S(2)}) collective-permute-start(bf16[192,16,128]{2,1,0:T(8,128)(2,1)} %constant_dynamic-update-slice_fusion.5.refs_5_), channel_id=1, source_target_pairs={{0,8},{2,10},{4,12},{6,14},{8,16},{10,18},{12,20},{14,22},{16,24},... | collective-permute-start | bytes 2359304 | tf_op jit(solution)/shard_map/ppermute | solution.py:310
  65.2 17.9 %collective-permute-start.16 = (bf16[192,16,128]{2,1,0:T(8,128)(2,1)}, bf16[192,16,128]{2,1,0:T(8,128)(2,1)}, u32[]{:S(2)}, u32[]{:S(2)}) collective-permute-start(bf16[192,16,128]{2,1,0:T(8,128)(2,1)} %constant_dynamic-update-slice_fusion.5.refs_5_), channel_id=1, source_target_pairs={{0,24},{2,26},{4,28},{6,30},{8,0},{10,2},{12,4},{14,6},{16,8},{18,... | collective-permute-start | bytes 2359304 | tf_op jit(solution)/shard_map/ppermute | solution.py:310
  69.2 17.1 %collective-permute-start.9 = (bf16[192,16,128]{2,1,0:T(8,128)(2,1)}, bf16[192,16,128]{2,1,0:T(8,128)(2,1)}, u32[]{:S(2)}, u32[]{:S(2)}) collective-permute-start(bf16[192,16,128]{2,1,0:T(8,128)(2,1)} %constant_dynamic-update-slice_fusion.refs_0_), channel_id=1, source_target_pairs={{0,32},{2,34},{4,36},{6,38},{8,40},{10,42},{12,44},{14,46},{16,48}... | collective-permute-start | bytes 2359304 | tf_op jit(solution)/shard_map/ppermute | solution.py:310
  69.6 16.7 %collective-permute-start.8 = (bf16[192,16,128]{2,1,0:T(8,128)(2,1)}, bf16[192,16,128]{2,1,0:T(8,128)(2,1)}, u32[]{:S(2)}, u32[]{:S(2)}) collective-permute-start(bf16[192,16,128]{2,1,0:T(8,128)(2,1)} %constant_dynamic-update-slice_fusion.refs_0_), channel_id=1, source_target_pairs={{0,96},{2,98},{4,100},{6,102},{8,104},{10,106},{12,108},{14,110},{... | collective-permute-start | bytes 2359304 | tf_op jit(solution)/shard_map/ppermute | solution.py:310
  74.0 9.6 %copy-start.14 = (s32[128,6]{0,1:T(8,128)S(1)}, s32[128,6]{0,1:T(8,128)}, u32[]{:S(2)}) copy-start(s32[128,6]{0,1:T(8,128)} %param.19) | copy-start | bytes 9220
  74.0 12.3 %copy-start.15 = (s32[896]{0:T(1024)S(1)}, s32[896]{0:T(1024)}, u32[]{:S(2)}) copy-start(s32[896]{0:T(1024)} %get-tuple-element.13) | copy-start | bytes 10756
  74.0 2.9 collective-permute-start.23
  76.9 20.6 %collective-permute-start.2 = (bf16[136,8,256]{2,1,0:T(8,128)(2,1)}, bf16[136,8,256]{2,1,0:T(8,128)(2,1)}, u32[]{:S(2)}, u32[]{:S(2)}) collective-permute-start(bf16[136,8,256]{2,1,0:T(8,128)(2,1)} %get-tuple-element.19), channel_id=1, source_target_pairs={{0,1},{1,0},{2,3},{3,2},{4,5},{5,4},{6,7},{7,6},{8,9},{9,8},{10,11... | collective-permute-start | bytes 1671176 | tf_op jit(solution)/shard_map/ppermute | solution.py:417
  82.8 12.0 %collective-permute-start.20 = (bf16[96,8,128]{2,1,0:T(8,128)(2,1)S(1)}, bf16[96,8,128]{2,1,0:T(8,128)(2,1)S(1)}, u32[]{:S(2)}, u32[]{:S(2)}) collective-permute-start(bf16[96,8,128]{2,1,0:T(8,128)(2,1)S(1)} %slice.94.refs_10_), channel_id=1, source_target_pairs={{0,6},{2,0},{4,2},{6,4},{8,14},{10,8},{12,10},{14,12},{16,22},{18,... | collective-permute-start | bytes 589832 | tf_op jit(solution)/shard_map/ppermute | solution.py:412
  83.1 12.1 %collective-permute-start.21 = (bf16[96,8,128]{2,1,0:T(8,128)(2,1)S(1)}, bf16[96,8,128]{2,1,0:T(8,128)(2,1)S(1)}, u32[]{:S(2)}, u32[]{:S(2)}) collective-permute-start(bf16[96,8,128]{2,1,0:T(8,128)(2,1)S(1)} %slice.94.refs_10_), channel_id=1, source_target_pairs={{0,4},{2,6},{4,0},{6,2},{8,12},{10,14},{12,8},{14,10},{16,20},{18,... | collective-permute-start | bytes 589832 | tf_op jit(solution)/shard_map/ppermute | solution.py:412
  86.3 5.6 %collective-permute-start.24 = (s32[896]{0:T(1024)}, s32[896]{0:T(1024)S(1)}, u32[]{:S(2)}, u32[]{:S(2)}) collective-permute-start(s32[896]{0:T(1024)} %get-tuple-element.16), channel_id=1, source_target_pairs={{0,4},{2,6},{4,0},{6,2},{8,12},{10,14},{12,8},{14,10},{16,20},{18,... | collective-permute-start | bytes 10760 | tf_op jit(solution)/shard_map/ppermute | solution.py:411
  86.3 5.9 %collective-permute-start.25 = (s32[896]{0:T(1024)S(1)}, s32[896]{0:T(1024)S(1)}, u32[]{:S(2)}, u32[]{:S(2)}) collective-permute-start(s32[896]{0:T(1024)S(1)} %copy-done.15), channel_id=1, source_target_pairs={{0,2},{2,4},{4,6},{6,0},{8,10},{10,12},{12,14},{14,8},{16,18},{18,... | collective-permute-start | bytes 10760 | tf_op jit(solution)/shard_map/ppermute | solution.py:411
  88.7 11.7 %copy-start.2 = (bf16[136,8,256]{2,1,0:T(8,128)(2,1)S(1)}, bf16[136,8,256]{2,1,0:T(8,128)(2,1)}, u32[]{:S(2)}) copy-start(bf16[136,8,256]{2,1,0:T(8,128)(2,1)} %get-tuple-element.20.pts) | copy-start | bytes 1671172
  91.9 74.2 %collective-permute-start.18 = (bf16[96,16,128]{2,1,0:T(8,128)(2,1)S(1)}, bf16[96,16,128]{2,1,0:T(8,128)(2,1)S(1)}, u32[]{:S(2)}, u32[]{:S(2)}) collective-permute-start(bf16[96,16,128]{2,1,0:T(8,128)(2,1)S(1)} %slice.92), channel_id=1, source_target_pairs={{0,8},{2,10},{4,12},{6,14},{8,16},{10,18},{12,20},{14,22},{16,24},... | collective-permute-start | bytes 1179656 | tf_op jit(solution)/shard_map/ppermute | solution.py:310
  92.1 73.9 %collective-permute-start.19 = (bf16[96,16,128]{2,1,0:T(8,128)(2,1)S(1)}, bf16[96,16,128]{2,1,0:T(8,128)(2,1)S(1)}, u32[]{:S(2)}, u32[]{:S(2)}) collective-permute-start(bf16[96,16,128]{2,1,0:T(8,128)(2,1)S(1)} %slice.93), channel_id=1, source_target_pairs={{0,24},{2,26},{4,28},{6,30},{8,0},{10,2},{12,4},{14,6},{16,8},{18,... | collective-permute-start | bytes 1179656 | tf_op jit(solution)/shard_map/ppermute | solution.py:310
  94.8 71.3 %collective-permute-start.10 = (bf16[96,16,128]{2,1,0:T(8,128)(2,1)S(1)}, bf16[96,16,128]{2,1,0:T(8,128)(2,1)S(1)}, u32[]{:S(2)}, u32[]{:S(2)}) collective-permute-start(bf16[96,16,128]{2,1,0:T(8,128)(2,1)S(1)} %slice.87), channel_id=1, source_target_pairs={{0,32},{2,34},{4,36},{6,38},{8,40},{10,42},{12,44},{14,46},{16,48}... | collective-permute-start | bytes 1179656 | tf_op jit(solution)/shard_map/ppermute | solution.py:310
  95.2 70.8 %collective-permute-start.11 = (bf16[96,16,128]{2,1,0:T(8,128)(2,1)S(1)}, bf16[96,16,128]{2,1,0:T(8,128)(2,1)S(1)}, u32[]{:S(2)}, u32[]{:S(2)}) collective-permute-start(bf16[96,16,128]{2,1,0:T(8,128)(2,1)S(1)} %slice.88), channel_id=1, source_target_pairs={{0,96},{2,98},{4,100},{6,102},{8,104},{10,106},{12,108},{14,110},{... | collective-permute-start | bytes 1179656 | tf_op jit(solution)/shard_map/ppermute | solution.py:310
  97.5 62.1 %collective-permute-start.22 = (bf16[96,8,128]{2,1,0:T(8,128)(2,1)S(1)}, bf16[96,8,128]{2,1,0:T(8,128)(2,1)S(1)}, u32[]{:S(2)}, u32[]{:S(2)}) collective-permute-start(bf16[96,8,128]{2,1,0:T(8,128)(2,1)S(1)} %slice.94.refs_10_), channel_id=1, source_target_pairs={{0,2},{2,4},{4,6},{6,0},{8,10},{10,12},{12,14},{14,8},{16,18},{18,... | collective-permute-start | bytes 589832 | tf_op jit(solution)/shard_map/ppermute | solution.py:412
  100.4 65.7 %copy-start.4 = (bf16[192,16,128]{2,1,0:T(8,128)(2,1)S(1)}, bf16[192,16,128]{2,1,0:T(8,128)(2,1)}, u32[]{:S(2)}) copy-start(bf16[192,16,128]{2,1,0:T(8,128)(2,1)} %constant_dynamic-update-slice_fusion.refs_0_) | copy-start | bytes 2359300
  100.4 65.7 %copy-start.5 = (bf16[192,16,128]{2,1,0:T(8,128)(2,1)S(1)}, bf16[192,16,128]{2,1,0:T(8,128)(2,1)}, u32[]{:S(2)}) copy-start(bf16[192,16,128]{2,1,0:T(8,128)(2,1)} %constant_dynamic-update-slice_fusion.5.refs_5_) | copy-start | bytes 2359300
  159.6 96.3 %collective-permute-start.3 = (f32[64,8,256]{2,1,0:T(8,128)S(1)}, f32[64,8,256]{2,1,0:T(8,128)S(1)}, u32[]{:S(2)}, u32[]{:S(2)}) collective-permute-start(f32[64,8,256]{2,1,0:T(8,128)S(1)} %slice.83), channel_id=1, source_target_pairs={{0,1},{1,0},{2,3},{3,2},{4,5},{5,4},{6,7},{7,6},{8,9},{9,8},{10,11... | collective-permute-start | bytes 1572872 | tf_op jit(solution)/shard_map/ppermute | solution.py:422
  166.1 89.8 %copy-start.16 = (s32[128]{0:T(128)S(1)}, s32[128]{0:T(128)}, u32[]{:S(2)}) copy-start(s32[128]{0:T(128)} %param.14) | copy-start | bytes 1540
  166.1 105.3 %copy-start.1 = (bf16[128,64,256]{2,1,0:T(8,128)(2,1)S(1)}, bf16[128,64,256]{2,1,0:T(8,128)(2,1)}, u32[]{:S(2)}) copy-start(bf16[128,64,256]{2,1,0:T(8,128)(2,1)} %basis.3) | copy-start | bytes 12582916
  244.9 17.0 %collective-permute-start.26 = (f32[96,8,128]{2,1,0:T(8,128)S(1)}, f32[96,8,128]{2,1,0:T(8,128)S(1)}, u32[]{:S(2)}, u32[]{:S(2)}) collective-permute-start(f32[96,8,128]{2,1,0:T(8,128)S(1)} %get-tuple-element.10), channel_id=1, source_target_pairs={{0,2},{2,4},{4,6},{6,0},{8,10},{10,12},{12,14},{14,8},{16,18},{18,... | collective-permute-start | bytes 1179656 | tf_op jit(solution)/shard_map/ppermute | solution.py:443
  253.4 16.9 %collective-permute-start.27 = (f32[96,8,128]{2,1,0:T(8,128)S(1)}, f32[96,8,128]{2,1,0:T(8,128)S(1)}, u32[]{:S(2)}, u32[]{:S(2)}) collective-permute-start(f32[96,8,128]{2,1,0:T(8,128)S(1)} %get-tuple-element.11), channel_id=1, source_target_pairs={{0,4},{2,6},{4,0},{6,2},{8,12},{10,14},{12,8},{14,10},{16,20},{18,... | collective-permute-start | bytes 1179656 | tf_op jit(solution)/shard_map/ppermute | solution.py:443
  253.4 18.0 %collective-permute-start.28 = (f32[96,8,128]{2,1,0:T(8,128)S(1)}, f32[96,8,128]{2,1,0:T(8,128)S(1)}, u32[]{:S(2)}, u32[]{:S(2)}) collective-permute-start(f32[96,8,128]{2,1,0:T(8,128)S(1)} %get-tuple-element.12), channel_id=1, source_target_pairs={{0,6},{2,0},{4,2},{6,4},{8,14},{10,8},{12,10},{14,12},{16,22},{18,... | collective-permute-start | bytes 1179656 | tf_op jit(solution)/shard_map/ppermute | solution.py:443

commit v3 on v2

--- a/solution.py
+++ b/solution.py
@@ -136,26 +136,31 @@
 
 def coef_kernel(values, basis, transfer, leaf_skel, upper_skel, table):
     pairs = leaf_skel.shape[0] // 2
-    step_pairs = 4
+    step_pairs = 8
 
     def step(i, carry):
+        first = i * step_pairs
+        coefs = [
+            lax.dot_general(
+                values[2 * first + n],
+                basis[2 * first + n],
+                (((1,), (1,)), ((), ())),
+                preferred_element_type=F32,
+            )
+            for n in range(2 * step_pairs)
+        ]
+        coefs = [jnp.concatenate(coefs[2 * n : 2 * n + 2], axis=1) for n in range(step_pairs)]
         upper = []
         for n in range(step_pairs):
-            p = i * step_pairs + n
-            halves = [
-                lax.dot_general(
-                    values[2 * p + k],
-                    basis[2 * p + k],
-                    (((1,), (1,)), ((), ())),
-                    preferred_element_type=F32,
-                )
-                for k in range(2)
-            ]
-            coef = jnp.concatenate(halves, axis=1)
+            p = first + n
+            stacked = jnp.concatenate([transfer[2 * p], transfer[2 * p + 1]], axis=0)
+            upper.append(jnp.dot(coefs[n].astype(BF16), stacked, preferred_element_type=F32))
+        for n in range(step_pairs):
+            p = first + n
             skel = [leaf_skel[2 * p + k].astype(F32) for k in range(2)]
-            table[p] = jnp.concatenate([jnp.concatenate(skel, axis=1), coef], axis=0).astype(BF16)
-            stacked = jnp.concatenate([transfer[2 * p], transfer[2 * p + 1]], axis=0)
-            upper.append(jnp.dot(coef.astype(BF16), stacked, preferred_element_type=F32))
+            table[p] = jnp.concatenate(
+                [jnp.concatenate(skel, axis=1), coefs[n]], axis=0
+            ).astype(BF16)
         for n in range(step_pairs // 2):
             p = i * (step_pairs // 2) + n
             skel = [upper_skel[2 * p + k].astype(F32) for k in range(2)]
@@ -168,26 +173,16 @@
     lax.fori_loop(0, pairs // step_pairs, step, 0)
 
 
-def far_kernel(units, rows_each, *refs):
-    pieces, refs = refs[:10], refs[10:]
-    skels, lists, outs = refs[:4], refs[4:8], refs[8:12]
-    table, sums, sems = refs[12:]
-    block = SIDE * rows_each
-    copies = []
-    for n, piece in enumerate(pieces):
-        order, part = divmod(n, 5)
-        start = order * SIDE * block + min(part, 3) * block
-        if part == 3:
-            where, size = table.at[pl.ds(start, block // 2)], block // 2
-        elif part == 4:
-            where, size = table.at[pl.ds(start + block // 2, block // 2)], block // 2
-        else:
-            where, size = table.at[pl.ds(start, block)], block
-        copy = pltpu.make_async_copy(piece, where, sems.at[n])
+def far_kernel(units, listed, first_half, second_half, skels, outs, table, sums, sems):
+    block = first_half.shape[0]
+    copies = [
+        pltpu.make_async_copy(first_half, table.at[pl.ds(0, block)], sems.at[0]),
+        pltpu.make_async_copy(second_half, table.at[pl.ds(block, block)], sems.at[1]),
+    ]
+    for copy in copies:
         copy.start()
-        copies.append(copy)
-    targets = 2 * skels[0].shape[0]
-    rank = skels[0].shape[2] // 2
+    targets = 2 * skels.shape[1]
+    rank = skels.shape[3] // 2
     lane = lax.broadcasted_iota(jnp.int32, (DIM, 2 * rank), 1)
     low = lane < rank
 
@@ -202,14 +197,15 @@
     def turned(array):
         return jnp.concatenate([array[:, rank:], array[:, :rank]], axis=1)
 
-    for r in range(4):
-        skel, listed, first = skels[r], lists[r], r * (targets + 1)
+    for r in range(SIDE):
+        first = r * (targets + 1)
 
         def step(i, carry):
+            where, squares, weights = [], [], []
             for quad in range(units // 4):
-                where, left, right, coefs = [], [], [], []
+                left, right, coefs = [], [], []
                 for n in range(4):
-                    entry = listed[i * units + quad * 4 + n]
+                    entry = listed[r, i * units + quad * 4 + n]
                     target = entry >> 12
                     row = (entry >> 1) & 2047
                     source = table[row].astype(F32)
@@ -226,112 +222,99 @@
                     right.append(jnp.concatenate(wide, axis=1))
                     wide = [coef, empty] if n < 2 else [empty, coef]
                     coefs.append(jnp.concatenate(wide, axis=1))
-                    pair = skel[jnp.minimum(target, targets - 1) >> 1].astype(F32)
+                    pair = skels[r, jnp.minimum(target, targets - 1) >> 1].astype(F32)
                     pair = jnp.where((target & 1) == 1, turned(pair), pair)
                     left.append(target_form(pair))
                     where.append(first + target)
                 left = jnp.concatenate(left, axis=0)[:, :rank].astype(BF16)
                 right = jnp.concatenate(right, axis=0).astype(BF16)
-                square = lax.dot_general(
-                    left, right, (((0,), (0,)), ((), ())), preferred_element_type=F32
+                weights.append(jnp.concatenate(coefs, axis=0).astype(BF16))
+                squares.append(
+                    lax.dot_general(
+                        left, right, (((0,), (0,)), ((), ())), preferred_element_type=F32
+                    )
                 )
-                fields = lax.dot_general(
-                    jnp.concatenate(coefs, axis=0).astype(BF16),
-                    matern_of_square(square),
-                    (((1,), (1,)), ((), ())),
-                    preferred_element_type=F32,
+            kernels = [matern_of_square(square) for square in squares]
+            fields = [
+                lax.dot_general(
+                    weight, kernel, (((1,), (1,)), ((), ())), preferred_element_type=F32
                 )
-                for n in range(4):
-                    sums[where[n]] += fields[DIM * n : DIM * (n + 1)]
+                for weight, kernel in zip(weights, kernels)
+            ]
+            for n in range(units):
+                at = DIM * (n % 4)
+                sums[where[n]] += fields[n // 4][at : at + DIM]
             return carry
 
-        count = listed[listed.shape[0] - 128]
+        count = listed[r, listed.shape[1] - 128]
         lax.fori_loop(0, (count + units - 1) // units, step, 0)
 
         def pack(p, carry):
-            outs[r][p] = jnp.concatenate([sums[first + 2 * p], sums[first + 2 * p + 1]], axis=1)
+            outs[r, p] = jnp.concatenate([sums[first + 2 * p], sums[first + 2 * p + 1]], axis=1)
             return carry
 
         lax.fori_loop(0, targets // 2, pack, 0)
 
 
-def final_kernel(counts, transfer, basis, near_mine, near_theirs, *refs):
-    parts, out = refs[:4], refs[4]
+def final_kernel(counts, transfer, basis, near_mine, near_theirs, total, out):
     leaves = out.shape[0]
     half = leaves // 2
     rank = transfer.shape[1]
     core = counts[leaves]
     lane = lax.broadcasted_iota(jnp.int32, out.shape[1:], 1)
-
-    def total(p):
-        return (parts[0][p] + parts[1][p]) + (parts[2][p] + parts[3][p])
+    group = 16
 
     def step(i, carry):
-        for n in range(2):
-            upper = total(half + 2 * i + n).astype(BF16)
-            for m in range(2):
-                pair = 4 * i + 2 * n + m
-                field = total(pair)
-                for k in range(2):
-                    leaf = 2 * pair + k
-                    down = lax.dot_general(
-                        upper[:, m * rank : (m + 1) * rank],
-                        transfer[leaf],
-                        (((1,), (1,)), ((), ())),
-                        preferred_element_type=F32,
-                    )
-                    here = (field[:, k * rank : (k + 1) * rank] + down).astype(BF16)
-                    result = jnp.dot(here, basis[leaf], preferred_element_type=F32)
-                    owner = leaf // half
-                    inner = leaf - owner * half
-                    near = jnp.where(
-                        owner == core, near_mine[inner][: out.shape[1]], near_theirs[inner]
-                    )
-                    out[leaf] = jnp.where(lane < counts[leaf], result + near, 0.0)
-        return carry
-
-    lax.fori_loop(0, leaves // 8, step, 0)
-
-
-def z_shift(r):
-    return [
-        (SIDE * k + z, SIDE * k + (z - r) % SIDE) for k in range(SIDE * SIDE) for z in range(SIDE)
-    ]
+        first = i * group
+        upper = [total[half + first // 4 + n].astype(BF16) for n in range(group // 4)]
+        down = [
+            lax.dot_general(
+                upper[n // 4][:, (n // 2 % 2) * rank : (n // 2 % 2 + 1) * rank],
+                transfer[first + n],
+                (((1,), (1,)), ((), ())),
+                preferred_element_type=F32,
+            )
+            for n in range(group)
+        ]
+        pairs = [total[first // 2 + n] for n in range(group // 2)]
+        field = [
+            (pairs[n // 2][:, (n % 2) * rank : (n % 2 + 1) * rank] + down[n]).astype(BF16)
+            for n in range(group)
+        ]
+        result = [
+            jnp.dot(field[n], basis[first + n], preferred_element_type=F32) for n in range(group)
+        ]
+        owner = first // half
+        inner = first - owner * half
+        for n in range(group):
+            near = jnp.where(
+                owner == core, near_mine[inner + n][: out.shape[1]], near_theirs[inner + n]
+            )
+            out[first + n] = jnp.where(lane < counts[first + n], result[n] + near, 0.0)
+        return carry
+
+    lax.fori_loop(0, leaves // group, step, 0)
+
+
+def lines(axis):
+    stride = (SIDE * SIDE, SIDE, 1)[axis]
+    starts = [i for i in range(SIDE**3) if i // stride % SIDE == 0]
+    return [[start + stride * k for k in range(SIDE)] for start in starts]
 
 
 def line_gather(block, axis):
-    stride = SIDE * SIDE if axis == 0 else SIDE
-
-    def moved(array, by):
-        pairs = []
-        for i in range(SIDE**3):
-            at = i // stride % SIDE
-            pairs.append((i, i + ((at + by) % SIDE - at) * stride))
-        return lax.ppermute(array, "leaf", pairs)
-
-    cut = block.shape[0] // 2
-    ahead, behind = moved(block, -1), moved(block, 1)
-    return [block, ahead, behind, moved(behind[:cut], 1), moved(ahead[cut:], -1)]
-
-
-def plane_gather(block, axes):
-    first = line_gather(block, axes[0])
-    return line_gather(jnp.concatenate(first, axis=0), axes[1])
+    return lax.all_gather(block, "leaf", axis_index_groups=lines(axis), tiled=True)
 
 
 def unit_lists(leaf_owner, leaf_local, upper_owner, upper_local, rows_each, capacity):
-    me = lax.axis_index("leaf")
     leaves, far = leaf_owner.shape
     parents = upper_owner.shape[0]
     owner = jnp.concatenate([leaf_owner.reshape(-1), upper_owner.reshape(-1)])
     local = jnp.concatenate([leaf_local.reshape(-1), leaves + upper_local.reshape(-1)])
     target = jnp.arange((leaves + parents) * far, dtype=jnp.int32) // far
 
-    def slot(offset):
-        return jnp.where(offset == 2, 3, jnp.where(offset == 3, 2, offset))
-
-    x = slot((owner // (SIDE * SIDE) - me // (SIDE * SIDE)) % SIDE)
-    y = slot((owner // SIDE - me // SIDE) % SIDE)
+    x = owner // (SIDE * SIDE)
+    y = owner // SIDE % SIDE
     pair = local // 2
     in_first = pair < rows_each
     row = jnp.where(
@@ -402,14 +385,12 @@
         cost_estimate=pl.CostEstimate(flops=10**8, bytes_accessed=6 * 2**20, transcendentals=0),
         name="coef",
     )(masked, leaf_basis, transfer, leaf_skeleton, upper_skeleton)
-    pieces = plane_gather(table[:rows_each], (1, 0)) + plane_gather(table[rows_each:], (0, 1))
-
+    first_half = line_gather(line_gather(table[:rows_each], 1), 0)
+    second_half = line_gather(line_gather(table[rows_each:], 0), 1)
     lists = unit_lists(far_owner, far_local, upper_owner, upper_local, rows_each, capacity)
-    skel = table[:, :DIM]
-    all_lists, all_skels = [lists[me % SIDE]], [skel]
-    for r in range(1, SIDE):
-        all_lists.append(lax.ppermute(lists[(me - r) % SIDE], "leaf", z_shift(r)))
-        all_skels.append(lax.ppermute(skel, "leaf", z_shift(r)))
+    lists = line_gather(lists, 2).reshape(SIDE, SIDE, -1)
+    lists = lax.dynamic_index_in_dim(lists, me % SIDE, axis=1, keepdims=False)
+    skels = line_gather(table[:, :DIM], 2).reshape(SIDE, pairs, DIM, 2 * rank)
 
     bundle = jnp.concatenate([points, masked], axis=1)
     extended = with_halo(bundle, (("leaf", 0),), HALO)
@@ -417,40 +398,53 @@
     cols = jnp.concatenate([own, lax.ppermute(own, "rhs", swap)], axis=1)
     first_leaf = me * leaf_dev - HALO
     chosen = lax.dynamic_slice_in_dim(near_list - first_leaf, core * half, half, axis=0)
-    ids = jnp.concatenate([chosen.reshape(-1), (core * half + HALO)[None]]).astype(jnp.int32)
-    near_half = near_field(ids, extended[:, :DIM], cols, half, near_count)
-    near_theirs = lax.ppermute(near_half[:, columns:], "rhs", swap)
-
-    part = jax.ShapeDtypeStruct((pairs, columns, 2 * rank), F32)
+    start = core * half + HALO
+    early = half * 3 // 4
+
+    def near_ids(rows, offset):
+        return jnp.concatenate([rows.reshape(-1), (start + offset)[None]]).astype(jnp.int32)
+
+    near_first = near_field(
+        near_ids(chosen[:early], 0), extended[:, :DIM], cols, early, near_count
+    )
+    theirs_first = lax.ppermute(near_first[:, columns:], "rhs", swap)
+    first_half, second_half, _ = lax.optimization_barrier((first_half, second_half, near_first))
+
     parts = pl.pallas_call(
-        functools.partial(far_kernel, 16, rows_each),
-        out_shape=[part] * 4,
-        in_specs=[anywhere] * 10 + [vmem] * 4 + [smem] * 4,
-        out_specs=[vmem] * 4,
+        functools.partial(far_kernel, 32),
+        out_shape=jax.ShapeDtypeStruct((SIDE, pairs, columns, 2 * rank), F32),
+        in_specs=[smem] + [anywhere] * 2 + [vmem],
+        out_specs=vmem,
         scratch_shapes=[
             pltpu.VMEM((2 * SIDE * SIDE * rows_each, 2 * DIM, 2 * rank), BF16),
-            pltpu.VMEM((4 * (2 * pairs + 1), columns, rank), F32),
-            pltpu.SemaphoreType.DMA((10,)),
+            pltpu.VMEM((SIDE * (2 * pairs + 1), columns, rank), F32),
+            pltpu.SemaphoreType.DMA((2,)),
         ],
         compiler_params=params,
         cost_estimate=pl.CostEstimate(
             flops=3 * 10**10, bytes_accessed=10 * 2**20, transcendentals=0
         ),
         name="far",
-    )(*pieces, *all_skels, *all_lists)
-    mine = [parts[0]]
-    for r in range(1, SIDE):
-        mine.append(lax.ppermute(parts[r], "leaf", z_shift(-r)))
+    )(lists, first_half, second_half, skels)
+    total = lax.psum_scatter(
+        parts, "leaf", scatter_dimension=0, axis_index_groups=lines(2), tiled=True
+    )[0]
+
+    late_ids, _ = lax.optimization_barrier((near_ids(chosen[early:], early), parts))
+    near_last = near_field(late_ids, extended[:, :DIM], cols, half - early, near_count)
+    theirs_last = lax.ppermute(near_last[:, columns:], "rhs", swap)
+    near_half = jnp.concatenate([near_first, near_last], axis=0)
+    near_theirs = jnp.concatenate([theirs_first, theirs_last], axis=0)
 
     limits = jnp.concatenate([counts, core[None]]).astype(jnp.int32)
     return pl.pallas_call(
         final_kernel,
         out_shape=jax.ShapeDtypeStruct((leaf_dev, columns, leaf_size), F32),
-        in_specs=[smem] + [vmem] * 8,
+        in_specs=[smem] + [vmem] * 5,
         out_specs=vmem,
         compiler_params=params,
         name="final",
-    )(limits, transfer, leaf_basis, near_half, near_theirs, *mine)
+    )(limits, transfer, leaf_basis, near_half, near_theirs, total)
 
 
 def solution(mesh):

time: 303 us -> 295 us (0.974)
  the two profiles are of different devices: /device:TPU:1 before, /device:TPU:91 now
where the time goes in v3:
time: 295 us; the launch traced here: 289 us
  Pallas kernels  154 us (52%)
  blocking collectives  52.3 us (18%)
  local copies, waits for them, and re-layouts  38.4 us (13%)
  starting transfers between devices  17.4 us (6%)
  between operations  13.4 us (5%)
  other arithmetic  9.05 us (3%)
    pallas_call x2, Pallas kernels, near_field(): pl.pallas_call(functools.partial(near_kernel, near, leaves), out_shape=ja...  76.5 us
    pallas_call x1, Pallas kernels, body(): pl.pallas_call(functools.partial(far_kernel, 32), out_shape=jax.ShapeDtyp...  68.1 us
    all_gather x4, blocking collectives, line_gather(): lax.all_gather(block, 'leaf', axis_index_groups=lines(axis), tiled=True)  52.3 us
    unnamed x55, local copies, waits for them, and re-layouts  21.5 us
    ppermute x1, starting transfers between devices, body(): cols = jnp.concatenate([own, lax.ppermute(own, 'rhs', swap)], axis=1)  10.3 us
  transfers between devices with their start and end apart: 8, of which 1 were waited for; matrix products, arithmetic and copies ran while one was open for 10% of the time, Pallas kernels for 26%

profile of v3, /device:TPU:91, one launch (start us, length us, event | category | flops | bytes accessed | tf_op | source)
XLA Modules:
  0.0 288.8 jit_solution(16221672033086650784)
XLA Ops:
  6.5 4.0 %copy.50.transfer = bf16[128,64,64]{2,1,0:T(8,128)(2,1)S(1)} copy(bf16[128,64,64]{0,2,1:T(8,128)(2,1)} %param.16) | data formatting | bytes 2097152 | tf_op args[4]
  10.8 1.2 broadcast_select_fusion.values
  12.0 2.2 copy-done
  14.2 4.0 %coef.1 = bf16[96,16,128]{2,1,0:T(8,128)(2,1)S(1)} custom-call(bf16[128,8,256]{2,1,0:T(8,128)(2,1)S(1)} %broadcast_select_fusion.values, bf16[128,64,256]{2,1,0:T(8,128)(2,1)S(1)} %copy-done, bf16[128,64,64]{2,1,0:T(8,128)(2,1)S(1)} %copy.50.transfer, bf16[128,8,64]{2,1,0:T(8,128)(2,1)S(1)} %copy.49.leaf_skel, bf16[64,8,64]{2,1,0:T(8,128)(2,1)S(1)} %copy-done.10), custom_call_target="tpu_custom_call" | custom-call | flops 100000000 | bytes 6291456 | tf_op jit(solution)/shard_map/coef/pallas_call | solution.py:379
  18.2 0.7 fusion.21
  19.0 11.3 %all_gather.19 = bf16[192,16,128]{2,1,0:T(8,128)(2,1)} all-gather(bf16[48,16,128]{2,1,0:T(8,128)(2,1)S(1)} %get-tuple-element.18), channel_id=1, replica_groups={{0,8,16,24},{2,10,18,26},{4,12,20,28},{6,14,22,30},{32,40,48,56},{34,42..., dimensions={0}, use_global_device_ids=true | all-gather | bytes 983040 | tf_op jit(solution)/shard_map/all_gather | solution.py:306
  31.0 1.9 collective-permute-start.1
  32.9 3.4 %collective-permute-start = (bf16[4,16,256]{2,1,0:T(8,128)(2,1)}, bf16[4,16,256]{2,1,0:T(8,128)(2,1)}, u32[]{:S(2)}, u32[]{:S(2)}) collective-permute-start(bf16[4,16,256]{2,1,0:T(8,128)(2,1)} %get-tuple-element.15), channel_id=1, source_target_pairs={{0,2},{2,4},{4,6},{6,8},{8,10},{10,12},{12,14},{14,16},{16,18},{18... | collective-permute-start | bytes 98312 | tf_op jit(solution)/shard_map/ppermute | solution.py:125
  36.3 15.0 %all_gather.21 = bf16[192,16,128]{2,1,0:T(8,128)(2,1)} all-gather(bf16[48,16,128]{2,1,0:T(8,128)(2,1)} %get-tuple-element.17), channel_id=1, replica_groups={{0,32,64,96},{2,34,66,98},{4,36,68,100},{6,38,70,102},{8,40,72,104},{10..., dimensions={0}, use_global_device_ids=true | all-gather | bytes 983040 | tf_op jit(solution)/shard_map/all_gather | solution.py:306
  51.4 0.7 copy.38
  52.1 0.9 concatenate.242
  53.0 0.9 concatenate.236
  54.0 0.7 copy.39
  54.7 1.4 concatenate.243
  56.1 1.4 concatenate.237
  57.6 0.7 copy.40
  58.3 1.5 concatenate.239
  60.5 1.3 broadcast_add_fusion
  61.8 1.4 copy.41
  63.1 1.4 concatenate.240
  66.9 1.4 mul.132
  68.4 0.9 fusion.5
  69.3 1.6 fusion.4
  70.9 1.4 reshape.1037
  72.9 1.1 fusion.22
  74.1 12.3 %all-gather = s32[4,4,896]{2,1,0:T(4,128)S(1)} all-gather(s32[1,4,896]{2,1,0:T(4,128)S(1)} %add_bitcast_fusion), channel_id=1, replica_groups={{0,2,4,6},{8,10,12,14},{16,18,20,22},{24,26,28,30},{32,34,36,38},{40,42..., dimensions={0}, use_global_device_ids=true | all-gather | bytes 71680 | tf_op jit(solution)/shard_map/all_gather | solution.py:306
  86.5 0.9 pad_maximum_fusion
  87.4 1.1 fusion.20
  88.4 10.3 %collective-permute-start.2 = (bf16[136,8,256]{2,1,0:T(8,128)(2,1)}, bf16[136,8,256]{2,1,0:T(8,128)(2,1)}, u32[]{:S(2)}, u32[]{:S(2)}) collective-permute-start(bf16[136,8,256]{2,1,0:T(8,128)(2,1)} %get-tuple-element.13), channel_id=1, source_target_pairs={{0,1},{1,0},{2,3},{3,2},{4,5},{5,4},{6,7},{7,6},{8,9},{9,8},{10,11... | collective-permute-start | bytes 1671176 | tf_op jit(solution)/shard_map/ppermute | solution.py:398
  99.2 13.7 %all_gather.23 = bf16[384,8,128]{2,1,0:T(8,128)(2,1)} all-gather(bf16[96,8,128]{2,1,0:T(8,128)(2,1)S(1)} %slice.70), channel_id=1, replica_groups={{0,2,4,6},{8,10,12,14},{16,18,20,22},{24,26,28,30},{32,34,36,38},{40,42..., dimensions={0}, use_global_device_ids=true | all-gather | bytes 983040 | tf_op jit(solution)/shard_map/all_gather | solution.py:306
  112.9 1.3 pad_maximum_fusion.1.cols
  114.2 48.7 %near.2 = f32[48,16,256]{2,1,0:T(8,128)S(1)} custom-call(s32[289]{0:T(512)S(1)} %pad_add_fusion.ids, bf16[136,8,256]{2,1,0:T(8,128)(2,1)S(1)} %copy-done.2, bf16[136,16,256]{2,1,0:T(8,128)(2,1)S(1)} %pad_maximum_fusion.1.cols), custom_call_target="tpu_custom_call" | custom-call | flops 1207959552 | bytes 4194304 | tf_op jit(solution)/shard_map/near/pallas_call | solution.py:98
  162.9 0.9 copy-done.5
  163.8 1.1 copy-done.8
  164.9 1.9 copy-done.11
  166.8 1.9 copy-done.12
  168.7 68.1 %far.1 = f32[4,96,8,128]{3,2,1,0:T(8,128)S(1)} custom-call(s32[4,896]{1,0:T(4,128)S(1)} %bitcast.17, bf16[768,16,128]{2,1,0:T(8,128)(2,1)S(1)} %copy-done.11, bf16[768,16,128]{2,1,0:T(8,128)(2,1)S(1)} %copy-done.12, bf16[4,96,8,128]{3,2,1,0:T(8,128)(2,1)S(1)} %bitcast.15), custom_call_target="tpu_custom_call" | custom-call | flops 30000001024 | bytes 10485760 | tf_op jit(solution)/shard_map/far/pallas_call | solution.py:413
  236.8 1.2 copy-done.7
  238.2 1.1 slice.71
  239.3 1.6 collective-permute-start.3
  241.1 1.0 copy-done.3
  242.1 27.8 %near.3 = f32[16,16,256]{2,1,0:T(8,128)S(1)} custom-call(s32[97]{0:T(128)S(1)} %pad_add_fusion.2.ids, bf16[136,8,256]{2,1,0:T(8,128)(2,1)S(1)} %copy-done.3, bf16[136,16,256]{2,1,0:T(8,128)(2,1)S(1)} %pad_maximum_fusion.1.cols), custom_call_target="tpu_custom_call" | custom-call | flops 402653184 | bytes 4194304 | tf_op jit(solution)/shard_map/near/pallas_call | solution.py:98
  270.1 1.2 collective-permute-done.4
  271.4 0.8 pad_maximum_fusion.3.near_theirs
  272.2 2.2 copy-done.1
  274.4 1.0 copy-done.4
  275.4 1.0 copy-done.9
  276.4 5.9 %final.1 = f32[128,8,256]{2,1,0:T(8,128)} custom-call(s32[129]{0:T(256)S(1)} %pad_add_fusion.1.counts, bf16[128,64,64]{2,1,0:T(8,128)(2,1)S(1)} %copy.50.transfer, bf16[128,64,256]{2,1,0:T(8,128)(2,1)S(1)} %copy-done.1, f32[64,16,256]{2,1,0:T(8,128)S(1)} %pad_maximum_fusion.2.near_mine, f32[64,8,256]{2,1,0:T(8,128)S(1)} %copy-done.4, f32[96,8,128]{2,1,0:T(8,128)S(1)} %bitcast.16), custom_call_target="tpu_custom_call" | custom-call | tf_op jit(solution)/shard_map/final/pallas_call | solution.py:440
  (84 shorter events, 5.8 us)
Async XLA Ops:
  6.5 4.0 %copy-start.21 = (s32[128]{0:T(128)S(1)}, s32[128]{0:T(128)}, u32[]{:S(2)}) copy-start(s32[128]{0:T(128)} %param.14) | copy-start | bytes 1540
  6.5 4.1 %copy-start.14 = (bf16[128,8,64]{0,2,1:T(8,128)(2,1)S(1)}, bf16[128,8,64]{0,2,1:T(8,128)(2,1)}, u32[]{:S(2)}) copy-start(bf16[128,8,64]{0,2,1:T(8,128)(2,1)} %param.17) | copy-start | bytes 393220
  6.5 5.5 %copy-start.10 = (bf16[64,8,64]{2,1,0:T(8,128)(2,1)S(1)}, bf16[64,8,64]{2,1,0:T(8,128)(2,1)}, u32[]{:S(2)}) copy-start(bf16[64,8,64]{2,1,0:T(8,128)(2,1)} %upper_skel.1) | copy-start | bytes 196612
  6.5 157.2 %all-gather.4.cloned.1.call-start = ((), (), s32[]{:S(2)}) async-start(), calls=%async_computation.1 | async-start | bytes 3932160 | tf_op jit(solution)/shard_map/all_gather | solution.py:306
  12.0 2.2 copy-start
  18.2 12.1 %copy-start.13 = (bf16[128,8,256]{2,1,0:T(8,128)(2,1)S(1)}, bf16[128,8,256]{2,1,0:T(8,128)(2,1)}, u32[]{:S(2)}) copy-start(bf16[128,8,256]{2,1,0:T(8,128)(2,1)} %param.12) | copy-start | bytes 1572868
  19.0 32.4 %copy-start.17 = (s32[128,8]{0,1:T(8,128)S(1)}, s32[128,8]{0,1:T(8,128)}, u32[]{:S(2)}) copy-start(s32[128,8]{0,1:T(8,128)} %param.20) | copy-start | bytes 12292
  19.0 35.0 %copy-start.18 = (s32[64,8]{0,1:T(8,128)S(1)}, s32[64,8]{0,1:T(8,128)}, u32[]{:S(2)}) copy-start(s32[64,8]{0,1:T(8,128)} %param.22) | copy-start | bytes 6148
  30.3 27.3 %copy-start.19 = (s32[128,8]{0,1:T(8,128)S(1)}, s32[128,8]{0,1:T(8,128)}, u32[]{:S(2)}) copy-start(s32[128,8]{0,1:T(8,128)} %param.21) | copy-start | bytes 12292
  30.3 133.5 %all-gather.6.cloned.1.call-start = ((), (), s32[]{:S(2)}) async-start(), calls=%async_computation.2 | async-start | bytes 3932160 | tf_op jit(solution)/shard_map/all_gather | solution.py:306
  31.0 55.5 %collective-permute-start.1 = (bf16[4,16,256]{2,1,0:T(8,128)(2,1)}, bf16[4,16,256]{2,1,0:T(8,128)(2,1)}, u32[]{:S(2)}, u32[]{:S(2)}) collective-permute-start(bf16[4,16,256]{2,1,0:T(8,128)(2,1)} %get-tuple-element.16), channel_id=1, source_target_pairs={{2,0},{4,2},{6,4},{8,6},{10,8},{12,10},{14,12},{16,14},{18,16},{20... | collective-permute-start | bytes 98312 | tf_op jit(solution)/shard_map/ppermute | solution.py:127
  32.9 53.6 %collective-permute-start = (bf16[4,16,256]{2,1,0:T(8,128)(2,1)}, bf16[4,16,256]{2,1,0:T(8,128)(2,1)}, u32[]{:S(2)}, u32[]{:S(2)}) collective-permute-start(bf16[4,16,256]{2,1,0:T(8,128)(2,1)} %get-tuple-element.15), channel_id=1, source_target_pairs={{0,2},{2,4},{4,6},{6,8},{8,10},{10,12},{12,14},{14,16},{16,18},{18... | collective-permute-start | bytes 98312 | tf_op jit(solution)/shard_map/ppermute | solution.py:125
  51.3 220.9 %reduce-scatter.2.cloned.1.call-start = ((), (), s32[]{:S(2)}) async-start(), calls=%async_computation.3 | async-start | bytes 1966080 | tf_op jit(solution)/shard_map/reduce_scatter | solution.py:429
  68.4 0.9 copy-start.15
  68.4 3.9 %copy-start.20 = (s32[128,6]{0,1:T(8,128)S(1)}, s32[128,6]{0,1:T(8,128)}, u32[]{:S(2)}) copy-start(s32[128,6]{0,1:T(8,128)} %param.19) | copy-start | bytes 9220
  86.5 12.3 %copy-start.16 = (s32[128,6]{0,1:T(8,128)S(1)}, s32[128,6]{0,1:T(8,128)}, u32[]{:S(2)}) copy-start(s32[128,6]{0,1:T(8,128)} %broadcast_subtract_fusion) | copy-start | bytes 9220
  88.4 24.4 %collective-permute-start.2 = (bf16[136,8,256]{2,1,0:T(8,128)(2,1)}, bf16[136,8,256]{2,1,0:T(8,128)(2,1)}, u32[]{:S(2)}, u32[]{:S(2)}) collective-permute-start(bf16[136,8,256]{2,1,0:T(8,128)(2,1)} %get-tuple-element.13), channel_id=1, source_target_pairs={{0,1},{1,0},{2,3},{3,2},{4,5},{5,4},{6,7},{7,6},{8,9},{9,8},{10,11... | collective-permute-start | bytes 1671176 | tf_op jit(solution)/shard_map/ppermute | solution.py:398
  99.1 15.1 %copy-start.2 = (bf16[136,8,256]{2,1,0:T(8,128)(2,1)S(1)}, bf16[136,8,256]{2,1,0:T(8,128)(2,1)}, u32[]{:S(2)}) copy-start(bf16[136,8,256]{2,1,0:T(8,128)(2,1)} %get-tuple-element.14.pts) | copy-start | bytes 1671172
  162.9 0.9 copy-start.5
  163.8 1.1 copy-start.8
  164.9 1.9 copy-start.11
  166.8 1.9 copy-start.12
  236.8 1.2 copy-start.7
  237.9 3.1 %copy-start.22 = (s32[128]{0:T(128)S(1)}, s32[128]{0:T(128)}, u32[]{:S(2)}) copy-start(s32[128]{0:T(128)} %param.14) | copy-start | bytes 1540
  238.2 31.8 %copy-start.6 = (f32[48,16,256]{2,1,0:T(8,128)S(1)}, f32[48,16,256]{2,1,0:T(8,128)}, u32[]{:S(2)}) copy-start(f32[48,16,256]{2,1,0:T(8,128)} %copy-done.5) | copy-start | bytes 2359300
  239.3 30.8 %collective-permute-start.3 = (f32[48,8,256]{2,1,0:T(8,128)S(1)}, f32[48,8,256]{2,1,0:T(8,128)S(1)}, u32[]{:S(2)}, u32[]{:S(2)}) collective-permute-start(f32[48,8,256]{2,1,0:T(8,128)S(1)} %slice.71), channel_id=1, source_target_pairs={{0,1},{1,0},{2,3},{3,2},{4,5},{5,4},{6,7},{7,6},{8,9},{9,8},{10,11... | collective-permute-start | bytes 1179656 | tf_op jit(solution)/shard_map/ppermute | solution.py:410
  241.1 1.1 copy-start.3
  269.9 1.4 collective-permute-start.4
  272.2 2.2 copy-start.1
  274.4 1.0 copy-start.4
  275.4 1.0 copy-start.9
Sparse Core Ops, SparseCore 0:
  30.4 46.3 all-gather.3
  78.5 40.6 all-gather.5
  238.1 28.8 reduce-scatter.1

commit v4 on v3

--- a/solution.py
+++ b/solution.py
@@ -54,17 +54,24 @@
     size = pts.shape[2]
     base = ids[half * near]
 
-    def stage(q, carry):
-        rows[q] = source_form(pts[q].astype(F32)).T.astype(BF16)
+    group = 8
+
+    def stage(k, carry):
+        forms = [source_form(pts[k * group + n].astype(F32)) for n in range(group)]
+        turned = [form.T.astype(BF16) for form in forms]
+        for n in range(group):
+            rows[k * group + n] = turned[n]
         return carry
 
-    lax.fori_loop(0, leaves, stage, 0)
-
-    def stage_target(i, carry):
-        mine[i] = target_form(pts[base + i].astype(F32)).astype(BF16)
+    lax.fori_loop(0, leaves // group, stage, 0)
+
+    def stage_target(k, carry):
+        forms = [target_form(pts[base + k * group + n].astype(F32)) for n in range(group)]
+        for n in range(group):
+            mine[k * group + n] = forms[n].astype(BF16)
         return carry
 
-    lax.fori_loop(0, half, stage_target, 0)
+    lax.fori_loop(0, half // group, stage_target, 0)
 
     def values(i, j, store):
         square = jnp.dot(rows[ids[i * near + j]], mine[i], preferred_element_type=F32)
@@ -173,24 +180,30 @@
     lax.fori_loop(0, pairs // step_pairs, step, 0)
 
 
-def far_kernel(units, listed, first_half, second_half, skels, outs, table, sums, sems):
+def far_kernel(units, *refs):
+    lists, (first_half, *rest), skels = refs[:4], refs[4:9], refs[9:13]
+    outs, table, sums, sems = refs[13:]
     block = first_half.shape[0]
     copies = [
         pltpu.make_async_copy(first_half, table.at[pl.ds(0, block)], sems.at[0]),
-        pltpu.make_async_copy(second_half, table.at[pl.ds(block, block)], sems.at[1]),
     ]
+    for n, piece in enumerate(rest):
+        size = piece.shape[0]
+        place = table.at[pl.ds(block + n * size, size)]
+        copies.append(pltpu.make_async_copy(piece, place, sems.at[n + 1]))
     for copy in copies:
         copy.start()
-    targets = 2 * skels.shape[1]
-    rank = skels.shape[3] // 2
+    targets = 2 * skels[0].shape[0]
+    rank = skels[0].shape[2] // 2
     lane = lax.broadcasted_iota(jnp.int32, (DIM, 2 * rank), 1)
     low = lane < rank
 
     def clear(i, carry):
-        sums[i] = jnp.zeros(sums.shape[1:], F32)
+        for n in range(4):
+            sums[i * 4 + n] = jnp.zeros(sums.shape[1:], F32)
         return carry
 
-    lax.fori_loop(0, sums.shape[0], clear, 0)
+    lax.fori_loop(0, sums.shape[0] // 4, clear, 0)
     for copy in copies:
         copy.wait()
 
@@ -198,14 +211,14 @@
         return jnp.concatenate([array[:, rank:], array[:, :rank]], axis=1)
 
     for r in range(SIDE):
-        first = r * (targets + 1)
+        listed, skel, first = lists[r], skels[r], r * (targets + 1)
 
         def step(i, carry):
             where, squares, weights = [], [], []
             for quad in range(units // 4):
                 left, right, coefs = [], [], []
                 for n in range(4):
-                    entry = listed[r, i * units + quad * 4 + n]
+                    entry = listed[i * units + quad * 4 + n]
                     target = entry >> 12
                     row = (entry >> 1) & 2047
                     source = table[row].astype(F32)
@@ -222,7 +235,7 @@
                     right.append(jnp.concatenate(wide, axis=1))
                     wide = [coef, empty] if n < 2 else [empty, coef]
                     coefs.append(jnp.concatenate(wide, axis=1))
-                    pair = skels[r, jnp.minimum(target, targets - 1) >> 1].astype(F32)
+                    pair = skel[jnp.minimum(target, targets - 1) >> 1].astype(F32)
                     pair = jnp.where((target & 1) == 1, turned(pair), pair)
                     left.append(target_form(pair))
                     where.append(first + target)
@@ -246,14 +259,18 @@
                 sums[where[n]] += fields[n // 4][at : at + DIM]
             return carry
 
-        count = listed[r, listed.shape[1] - 128]
+        count = listed[listed.shape[0] - 128]
+        origin = listed[listed.shape[0] - 127]
         lax.fori_loop(0, (count + units - 1) // units, step, 0)
 
-        def pack(p, carry):
-            outs[r, p] = jnp.concatenate([sums[first + 2 * p], sums[first + 2 * p + 1]], axis=1)
+        def pack(k, carry):
+            for n in range(8):
+                p = k * 8 + n
+                both = [sums[first + 2 * p], sums[first + 2 * p + 1]]
+                outs[origin, p] = jnp.concatenate(both, axis=1)
             return carry
 
-        lax.fori_loop(0, targets // 2, pack, 0)
+        lax.fori_loop(0, targets // 16, pack, 0)
 
 
 def final_kernel(counts, transfer, basis, near_mine, near_theirs, total, out):
@@ -306,25 +323,45 @@
     return lax.all_gather(block, "leaf", axis_index_groups=lines(axis), tiled=True)
 
 
+def line_shift(block, axis, by):
+    pairs = [
+        (line[(k + by) % SIDE], line[k]) for line in lines(axis) for k in range(SIDE)
+    ]
+    return lax.ppermute(block, "leaf", pairs)
+
+
+def line_shifts(block, axis):
+    return [block] + [line_shift(block, axis, by) for by in range(1, SIDE)]
+
+
 def unit_lists(leaf_owner, leaf_local, upper_owner, upper_local, rows_each, capacity):
-    leaves, far = leaf_owner.shape
+    me = lax.axis_index("leaf")
+    leaves = leaf_owner.shape[0]
     parents = upper_owner.shape[0]
-    owner = jnp.concatenate([leaf_owner.reshape(-1), upper_owner.reshape(-1)])
-    local = jnp.concatenate([leaf_local.reshape(-1), leaves + upper_local.reshape(-1)])
-    target = jnp.arange((leaves + parents) * far, dtype=jnp.int32) // far
-
-    x = owner // (SIDE * SIDE)
-    y = owner // SIDE % SIDE
-    pair = local // 2
-    in_first = pair < rows_each
-    row = jnp.where(
-        in_first,
-        (x * SIDE + y) * rows_each + pair,
-        SIDE * SIDE * rows_each + (y * SIDE + x) * rows_each + pair - rows_each,
-    )
-    code = (target << 12) | (row << 1) | (local & 1)
-    hits = (owner[:, None] % SIDE == jnp.arange(SIDE, dtype=jnp.int32)[None, :]).astype(BF16)
-    number = owner.shape[0]
+
+    def coded(owner, local, first_pair, first_target):
+        x = owner // (SIDE * SIDE)
+        x_ahead = (x - me // (SIDE * SIDE)) % SIDE
+        y_ahead = (owner // SIDE - me // SIDE) % SIDE
+        pair = first_pair + local // 2
+        row = jnp.where(
+            pair < rows_each,
+            (x * SIDE + y_ahead) * rows_each + pair,
+            (SIDE * SIDE + y_ahead * SIDE + x_ahead - 1) * rows_each + pair,
+        )
+        target = first_target + lax.broadcasted_iota(jnp.int32, owner.shape, 0)
+        return (owner % SIDE << 20) | (target << 12) | (row << 1) | (local & 1)
+
+    code = jnp.concatenate(
+        [
+            coded(leaf_owner, leaf_local, 0, 0),
+            coded(upper_owner, upper_local, leaves // 2, leaves),
+        ],
+        axis=0,
+    ).reshape(-1)
+    hits = (code[:, None] >> 20 == jnp.arange(SIDE, dtype=jnp.int32)[None, :]).astype(BF16)
+    code = code & (2**20 - 1)
+    number = code.shape[0]
     order = jnp.arange(number, dtype=jnp.int32)
     before = (order[None, :] < order[:, None]).astype(BF16)
     rank = jnp.sum(jnp.dot(before, hits, preferred_element_type=F32) * hits.astype(F32), axis=1)
@@ -340,7 +377,8 @@
     codes = found[:, 0] + (found[:, 1] << 7) + (found[:, 2] << 14)
     codes = codes + jnp.where(found[:, 3] == 0, (leaves + parents) << 12, 0)
     counts = jnp.sum(found[:, 3], axis=1)
-    return jnp.concatenate([codes, jnp.broadcast_to(counts[:, None], (SIDE, 128))], axis=1)
+    tail = jnp.where(jnp.arange(128)[None, :] == 0, counts[:, None], me % SIDE)
+    return jnp.concatenate([codes, tail], axis=1)
 
 
 def body(
@@ -385,12 +423,13 @@
         cost_estimate=pl.CostEstimate(flops=10**8, bytes_accessed=6 * 2**20, transcendentals=0),
         name="coef",
     )(masked, leaf_basis, transfer, leaf_skeleton, upper_skeleton)
-    first_half = line_gather(line_gather(table[:rows_each], 1), 0)
-    second_half = line_gather(line_gather(table[rows_each:], 0), 1)
+    first_half = line_gather(jnp.concatenate(line_shifts(table[:rows_each], 1), axis=0), 0)
+    second_half = line_shifts(jnp.concatenate(line_shifts(table[rows_each:], 0), axis=0), 1)
+    skels = line_shifts(table[:, :DIM], 2)
     lists = unit_lists(far_owner, far_local, upper_owner, upper_local, rows_each, capacity)
-    lists = line_gather(lists, 2).reshape(SIDE, SIDE, -1)
-    lists = lax.dynamic_index_in_dim(lists, me % SIDE, axis=1, keepdims=False)
-    skels = line_gather(table[:, :DIM], 2).reshape(SIDE, pairs, DIM, 2 * rank)
+    all_lists = [lists[me % SIDE]]
+    for r in range(1, SIDE):
+        all_lists.append(line_shift(lists[(me - r) % SIDE], 2, r))
 
     bundle = jnp.concatenate([points, masked], axis=1)
     extended = with_halo(bundle, (("leaf", 0),), HALO)
@@ -399,7 +438,7 @@
     first_leaf = me * leaf_dev - HALO
     chosen = lax.dynamic_slice_in_dim(near_list - first_leaf, core * half, half, axis=0)
     start = core * half + HALO
-    early = half * 3 // 4
+    early = half * 5 // 8
 
     def near_ids(rows, offset):
         return jnp.concatenate([rows.reshape(-1), (start + offset)[None]]).astype(jnp.int32)
@@ -408,24 +447,24 @@
         near_ids(chosen[:early], 0), extended[:, :DIM], cols, early, near_count
     )
     theirs_first = lax.ppermute(near_first[:, columns:], "rhs", swap)
-    first_half, second_half, _ = lax.optimization_barrier((first_half, second_half, near_first))
+    first_half, _ = lax.optimization_barrier((first_half, near_first))
 
     parts = pl.pallas_call(
         functools.partial(far_kernel, 32),
         out_shape=jax.ShapeDtypeStruct((SIDE, pairs, columns, 2 * rank), F32),
-        in_specs=[smem] + [anywhere] * 2 + [vmem],
+        in_specs=[smem] * 4 + [anywhere] * 5 + [vmem] * 4,
         out_specs=vmem,
         scratch_shapes=[
             pltpu.VMEM((2 * SIDE * SIDE * rows_each, 2 * DIM, 2 * rank), BF16),
             pltpu.VMEM((SIDE * (2 * pairs + 1), columns, rank), F32),
-            pltpu.SemaphoreType.DMA((2,)),
+            pltpu.SemaphoreType.DMA((5,)),
         ],
         compiler_params=params,
         cost_estimate=pl.CostEstimate(
             flops=3 * 10**10, bytes_accessed=10 * 2**20, transcendentals=0
         ),
         name="far",
-    )(lists, first_half, second_half, skels)
+    )(*all_lists, first_half, *second_half, *skels)
     total = lax.psum_scatter(
         parts, "leaf", scatter_dimension=0, axis_index_groups=lines(2), tiled=True
     )[0]

time: 295 us -> 225 us (0.76)
  the two profiles are of different devices: /device:TPU:91 before, /device:TPU:1 now
where the time goes in v4:
time: 225 us; the launch traced here: 221 us
  Pallas kernels  97.9 us (44%)
  starting transfers between devices  41.2 us (18%)
  local copies, waits for them, and re-layouts  31.6 us (14%)
  waiting for transfers between devices  22.2 us (10%)
  between operations  13.8 us (6%)
  other arithmetic  12.1 us (5%)
  matrix products  2.46 us (1%)
    pallas_call x2, Pallas kernels, near_field(): pl.pallas_call(functools.partial(near_kernel, near, leaves), out_shape=ja...  50.9 us
    pallas_call x1, Pallas kernels, body(): pl.pallas_call(functools.partial(far_kernel, 32), out_shape=jax.ShapeDtyp...  37.2 us
    ppermute x15, starting transfers between devices, line_shift(): return lax.ppermute(block, 'leaf', pairs)  27.6 us
    ppermute x15, waiting for transfers between devices, line_shift(): return lax.ppermute(block, 'leaf', pairs)  17.6 us
    unnamed x53, local copies, waits for them, and re-layouts  17.2 us
    pallas_call x1, Pallas kernels, body(): pl.pallas_call(final_kernel, out_shape=jax.ShapeDtypeStruct((leaf_dev, co...  5.86 us
    ppermute x1, starting transfers between devices, with_halo(): lax.ppermute(tail, axis, [(i, (i + 1) % count) for i in range(ends)])  4.79 us
    ppermute x1, starting transfers between devices, body(): theirs_first = lax.ppermute(near_first[:, columns:], 'rhs', swap)  4.62 us
  transfers between devices with their start and end apart: 22, of which 8 were waited for; matrix products, arithmetic and copies ran while one was open for 12% of the time, Pallas kernels for 23%

profile of v4, /device:TPU:1, one launch (start us, length us, event | category | flops | bytes accessed | tf_op | source)
XLA Modules:
  0.0 221.3 jit_solution(5033083204962204988)
XLA Ops:
  6.5 4.0 %copy.33.transfer = bf16[128,64,64]{2,1,0:T(8,128)(2,1)S(1)} copy(bf16[128,64,64]{0,2,1:T(8,128)(2,1)} %param.16) | data formatting | bytes 2097152 | tf_op args[4]
  10.8 1.2 broadcast_select_fusion.values
  12.0 2.2 copy-done
  14.2 4.0 %coef.1 = bf16[96,16,128]{2,1,0:T(8,128)(2,1)S(1)} custom-call(bf16[128,8,256]{2,1,0:T(8,128)(2,1)S(1)} %broadcast_select_fusion.values, bf16[128,64,256]{2,1,0:T(8,128)(2,1)S(1)} %copy-done, bf16[128,64,64]{2,1,0:T(8,128)(2,1)S(1)} %copy.33.transfer, bf16[128,8,64]{2,1,0:T(8,128)(2,1)S(1)} %copy.32.leaf_skel, bf16[64,8,64]{2,1,0:T(8,128)(2,1)S(1)} %copy-done.11), custom_call_target="tpu_custom_call" | custom-call | flops 100000000 | bytes 6291456 | tf_op jit(solution)/shard_map/coef/pallas_call | solution.py:417
  19.0 2.1 collective-permute-start.8
  21.1 2.6 %collective-permute-start.7 = (bf16[48,16,128]{2,1,0:T(8,128)(2,1)S(1)}, bf16[48,16,128]{2,1,0:T(8,128)(2,1)S(1)}, u32[]{:S(2)}, u32[]{:S(2)}) collective-permute-start(bf16[48,16,128]{2,1,0:T(8,128)(2,1)S(1)} %get-tuple-element.18), channel_id=1, source_target_pairs={{16,0},{24,8},{0,16},{8,24},{18,2},{26,10},{2,18},{10,26},{20,4},{... | collective-permute-start | bytes 589832 | tf_op jit(solution)/shard_map/ppermute | solution.py:330
  23.7 1.1 collective-permute-start.6
  24.8 2.2 %collective-permute-done.8 = bf16[48,16,128]{2,1,0:T(8,128)(2,1)S(1)} collective-permute-done((bf16[48,16,128]{2,1,0:T(8,128)(2,1)S(1)}, bf16[48,16,128]{2,1,0:T(8,128)(2,1)S(1)}, u32[]{:S(2)}, u32[]{:S(2)}) %collective-permute-start.8) | collective-permute-done | bytes 196640 | tf_op jit(solution)/shard_map/ppermute | solution.py:330
  27.0 5.2 %collective-permute-done.7 = bf16[48,16,128]{2,1,0:T(8,128)(2,1)S(1)} collective-permute-done((bf16[48,16,128]{2,1,0:T(8,128)(2,1)S(1)}, bf16[48,16,128]{2,1,0:T(8,128)(2,1)S(1)}, u32[]{:S(2)}, u32[]{:S(2)}) %collective-permute-start.7) | collective-permute-done | bytes 196640 | tf_op jit(solution)/shard_map/ppermute | solution.py:330
  33.3 1.3 collective-permute-start.11
  34.6 2.5 %collective-permute-start.10 = (bf16[48,16,128]{2,1,0:T(8,128)(2,1)}, bf16[48,16,128]{2,1,0:T(8,128)(2,1)}, u32[]{:S(2)}, u32[]{:S(2)}) collective-permute-start(bf16[48,16,128]{2,1,0:T(8,128)(2,1)} %get-tuple-element.17), channel_id=1, source_target_pairs={{64,0},{96,32},{0,64},{32,96},{66,2},{98,34},{2,66},{34,98},{68,4}... | collective-permute-start | bytes 589832 | tf_op jit(solution)/shard_map/ppermute | solution.py:330
  37.0 1.2 collective-permute-start.9
  38.8 1.3 collective-permute-start.1
  40.1 4.8 %collective-permute-start = (bf16[4,16,256]{2,1,0:T(8,128)(2,1)}, bf16[4,16,256]{2,1,0:T(8,128)(2,1)}, u32[]{:S(2)}, u32[]{:S(2)}) collective-permute-start(bf16[4,16,256]{2,1,0:T(8,128)(2,1)} %get-tuple-element.15), channel_id=1, source_target_pairs={{0,2},{2,4},{4,6},{6,8},{8,10},{10,12},{12,14},{14,16},{16,18},{18... | collective-permute-start | bytes 98312 | tf_op jit(solution)/shard_map/ppermute | solution.py:132
  47.3 1.4 copy.29
  48.7 1.5 and.168
  50.2 1.4 copy.28
  51.6 1.5 and.166
  56.4 1.4 mul.64
  58.7 1.6 fusion.4
  60.3 1.4 reshape.149
  61.7 1.1 fusion.8
  65.3 2.8 %collective-permute-start.2 = (bf16[136,8,256]{2,1,0:T(8,128)(2,1)S(1)}, bf16[136,8,256]{2,1,0:T(8,128)(2,1)}, u32[]{:S(2)}, u32[]{:S(2)}) collective-permute-start(bf16[136,8,256]{2,1,0:T(8,128)(2,1)S(1)} %get-tuple-element.13), channel_id=1, source_target_pairs={{0,1},{1,0},{2,3},{3,2},{4,5},{5,4},{6,7},{7,6},{8,9},{9,8},{10,11... | collective-permute-start | bytes 1671176 | tf_op jit(solution)/shard_map/ppermute | solution.py:437
  68.1 2.2 pad_maximum_fusion.4.refs_5_
  70.2 3.8 %collective-permute-start.12 = (bf16[192,16,128]{2,1,0:T(8,128)(2,1)}, bf16[192,16,128]{2,1,0:T(8,128)(2,1)}, u32[]{:S(2)}, u32[]{:S(2)}) collective-permute-start(bf16[192,16,128]{2,1,0:T(8,128)(2,1)} %pad_maximum_fusion.4.refs_5_), channel_id=1, source_target_pairs={{8,0},{16,8},{24,16},{0,24},{10,2},{18,10},{26,18},{2,26},{12,4},{... | collective-permute-start | bytes 2359304 | tf_op jit(solution)/shard_map/ppermute | solution.py:330
  75.1 5.2 %collective-permute-start.3 = (s32[896]{0:T(1024)S(1)}, s32[896]{0:T(1024)S(1)}, u32[]{:S(2)}, u32[]{:S(2)}) collective-permute-start(s32[896]{0:T(1024)S(1)} %get-tuple-element.11), channel_id=1, source_target_pairs={{2,0},{4,2},{6,4},{0,6},{10,8},{12,10},{14,12},{8,14},{18,16},{20,... | collective-permute-start | bytes 10760 | tf_op jit(solution)/shard_map/ppermute | solution.py:330
  81.0 1.8 collective-permute-start.4
  82.8 2.5 %collective-permute-done.4.refs_2_ = s32[896]{0:T(1024)S(1)} collective-permute-done((s32[896]{0:T(1024)S(1)}, s32[896]{0:T(1024)S(1)}, u32[]{:S(2)}, u32[]{:S(2)}) %collective-permute-start.4) | collective-permute-done | bytes 3616 | tf_op jit(solution)/shard_map/ppermute | solution.py:330
  85.9 3.8 %collective-permute-done.5.refs_3_ = s32[896]{0:T(1024)S(1)} collective-permute-done((s32[896]{0:T(1024)S(1)}, s32[896]{0:T(1024)S(1)}, u32[]{:S(2)}, u32[]{:S(2)}) %collective-permute-start.5) | collective-permute-done | bytes 3616 | tf_op jit(solution)/shard_map/ppermute | solution.py:330
  89.6 1.5 collective-permute-start.15
  91.5 3.1 %collective-permute-done.15.refs_10_ = bf16[96,8,128]{2,1,0:T(8,128)(2,1)S(1)} collective-permute-done((bf16[96,8,128]{2,1,0:T(8,128)(2,1)S(1)}, bf16[96,8,128]{2,1,0:T(8,128)(2,1)S(1)}, u32[]{:S(2)}, u32[]{:S(2)}) %collective-permute-start.15) | collective-permute-done | bytes 196640 | tf_op jit(solution)/shard_map/ppermute | solution.py:330
  94.6 1.2 collective-permute-start.16
  95.7 2.1 collective-permute-start.17
  97.8 1.1 pad_maximum_fusion.1.cols
  99.0 30.6 %near.2 = f32[40,16,256]{2,1,0:T(8,128)S(1)} custom-call(s32[241]{0:T(256)S(1)} %pad_add_fusion.2.ids, bf16[136,8,256]{2,1,0:T(8,128)(2,1)S(1)} %copy-done.8, bf16[136,16,256]{2,1,0:T(8,128)(2,1)S(1)} %pad_maximum_fusion.1.cols), custom_call_target="tpu_custom_call" | custom-call | flops 1006632960 | bytes 4194304 | tf_op jit(solution)/shard_map/near/pallas_call | solution.py:105
  129.5 1.0 copy-done.6
  130.6 2.1 copy-done.12
  132.7 37.2 %far.1 = f32[4,96,8,128]{3,2,1,0:T(8,128)S(1)} custom-call(s32[896]{0:T(1024)S(1)} %get-tuple-element.10.refs_0_, s32[896]{0:T(1024)S(1)} %collective-permute-done.3.refs_1_, s32[896]{0:T(1024)S(1)} %collective-permute-done.4.refs_2_, s32[896]{0:T(1024)S(1)} %collective-permute-done.5.refs_3_, bf16[768,16,128]{2,1,0:T(8,128)(2,1)S(1)} %copy-done.12, ...), custom_call_target="tpu_custom_call" | custom-call | flops 30000001024 | bytes 10485760 | tf_op jit(solution)/shard_map/far/pallas_call | solution.py:452
  169.9 1.2 copy-done.3
  171.4 4.6 %collective-permute-start.18 = (f32[40,8,256]{2,1,0:T(8,128)S(1)}, f32[40,8,256]{2,1,0:T(8,128)S(1)}, u32[]{:S(2)}, u32[]{:S(2)}) collective-permute-start(f32[40,8,256]{2,1,0:T(8,128)S(1)} %slice.71), channel_id=1, source_target_pairs={{0,1},{1,0},{2,3},{3,2},{4,5},{5,4},{6,7},{7,6},{8,9},{9,8},{10,11... | collective-permute-start | bytes 983048 | tf_op jit(solution)/shard_map/ppermute | solution.py:449
  176.1 1.2 copy-done.7
  177.3 1.1 copy-done.9
  178.4 20.3 %near.3 = f32[24,16,256]{2,1,0:T(8,128)S(1)} custom-call(s32[145]{0:T(256)S(1)} %pad_add_fusion.3.ids, bf16[136,8,256]{2,1,0:T(8,128)(2,1)S(1)} %copy-done.9, bf16[136,16,256]{2,1,0:T(8,128)(2,1)S(1)} %copy-done.7), custom_call_target="tpu_custom_call" | custom-call | flops 603979776 | bytes 4194304 | tf_op jit(solution)/shard_map/near/pallas_call | solution.py:105
  199.0 1.3 collective-permute-done.19
  201.1 3.3 %reduce-scatter.2.cloned.1.call-done = f32[1,96,8,128]{3,2,1,0:T(8,128)} async-done(((f32[4,96,8,128]{3,2,1,0:T(8,128)}), f32[1,96,8,128]{3,2,1,0:T(8,128)}) %reduce-scatter.2.cloned.1.call-update) | async-done | bytes 393232 | tf_op jit(solution)/shard_map/reduce_scatter | solution.py:468
  204.4 2.2 copy-done.1
  206.6 1.0 copy-done.2
  208.6 5.9 %final.1 = f32[128,8,256]{2,1,0:T(8,128)} custom-call(s32[129]{0:T(256)S(1)} %pad_add_fusion.1.counts, bf16[128,64,64]{2,1,0:T(8,128)(2,1)S(1)} %copy.33.transfer, bf16[128,64,256]{2,1,0:T(8,128)(2,1)S(1)} %copy-done.1, f32[64,16,256]{2,1,0:T(8,128)S(1)} %pad_maximum_fusion.2.near_mine, f32[64,8,256]{2,1,0:T(8,128)S(1)} %copy-done.2, f32[96,8,128]{2,1,0:T(8,128)S(1)} %bitcast.10), custom_call_target="tpu_custom_call" | custom-call | tf_op jit(solution)/shard_map/final/pallas_call | solution.py:479
  (106 shorter events, 16.8 us)
Async XLA Ops:
  6.5 4.0 %copy-start.22 = (s32[128]{0:T(128)S(1)}, s32[128]{0:T(128)}, u32[]{:S(2)}) copy-start(s32[128]{0:T(128)} %param.14) | copy-start | bytes 1540
  6.5 4.1 %copy-start.15 = (bf16[128,8,64]{0,2,1:T(8,128)(2,1)S(1)}, bf16[128,8,64]{0,2,1:T(8,128)(2,1)}, u32[]{:S(2)}) copy-start(bf16[128,8,64]{0,2,1:T(8,128)(2,1)} %param.17) | copy-start | bytes 393220
  6.5 5.5 %copy-start.11 = (bf16[64,8,64]{2,1,0:T(8,128)(2,1)S(1)}, bf16[64,8,64]{2,1,0:T(8,128)(2,1)}, u32[]{:S(2)}) copy-start(bf16[64,8,64]{2,1,0:T(8,128)(2,1)} %upper_skel.1) | copy-start | bytes 196612
  6.5 124.0 %all-gather.2.cloned.1.call-start = ((), (), s32[]{:S(2)}) async-start(), calls=%async_computation.1 | async-start | bytes 3932160 | tf_op jit(solution)/shard_map/all_gather | solution.py:323
  12.0 2.2 copy-start
  18.2 20.0 %copy-start.13 = (bf16[128,8,256]{2,1,0:T(8,128)(2,1)S(1)}, bf16[128,8,256]{2,1,0:T(8,128)(2,1)}, u32[]{:S(2)}) copy-start(bf16[128,8,256]{2,1,0:T(8,128)(2,1)} %param.12) | copy-start | bytes 1572868
  18.2 26.7 %copy-start.17 = (s32[64,8]{0,1:T(8,128)S(1)}, s32[64,8]{0,1:T(8,128)}, u32[]{:S(2)}) copy-start(s32[64,8]{0,1:T(8,128)} %param.23) | copy-start | bytes 6148
  18.2 26.7 %copy-start.18 = (s32[64,8]{0,1:T(8,128)S(1)}, s32[64,8]{0,1:T(8,128)}, u32[]{:S(2)}) copy-start(s32[64,8]{0,1:T(8,128)} %param.22) | copy-start | bytes 6148
  18.2 26.7 %copy-start.19 = (s32[128,8]{0,1:T(8,128)S(1)}, s32[128,8]{0,1:T(8,128)}, u32[]{:S(2)}) copy-start(s32[128,8]{0,1:T(8,128)} %param.21) | copy-start | bytes 12292
  18.3 26.7 %copy-start.20 = (s32[128,8]{0,1:T(8,128)S(1)}, s32[128,8]{0,1:T(8,128)}, u32[]{:S(2)}) copy-start(s32[128,8]{0,1:T(8,128)} %param.20) | copy-start | bytes 12292
  19.0 8.0 %collective-permute-start.8 = (bf16[48,16,128]{2,1,0:T(8,128)(2,1)S(1)}, bf16[48,16,128]{2,1,0:T(8,128)(2,1)S(1)}, u32[]{:S(2)}, u32[]{:S(2)}) collective-permute-start(bf16[48,16,128]{2,1,0:T(8,128)(2,1)S(1)} %get-tuple-element.18), channel_id=1, source_target_pairs={{24,0},{0,8},{8,16},{16,24},{26,2},{2,10},{10,18},{18,26},{28,4},{... | collective-permute-start | bytes 589832 | tf_op jit(solution)/shard_map/ppermute | solution.py:330
  21.1 11.1 %collective-permute-start.7 = (bf16[48,16,128]{2,1,0:T(8,128)(2,1)S(1)}, bf16[48,16,128]{2,1,0:T(8,128)(2,1)S(1)}, u32[]{:S(2)}, u32[]{:S(2)}) collective-permute-start(bf16[48,16,128]{2,1,0:T(8,128)(2,1)S(1)} %get-tuple-element.18), channel_id=1, source_target_pairs={{16,0},{24,8},{0,16},{8,24},{18,2},{26,10},{2,18},{10,26},{20,4},{... | collective-permute-start | bytes 589832 | tf_op jit(solution)/shard_map/ppermute | solution.py:330
  23.7 8.5 %collective-permute-start.6 = (bf16[48,16,128]{2,1,0:T(8,128)(2,1)S(1)}, bf16[48,16,128]{2,1,0:T(8,128)(2,1)S(1)}, u32[]{:S(2)}, u32[]{:S(2)}) collective-permute-start(bf16[48,16,128]{2,1,0:T(8,128)(2,1)S(1)} %get-tuple-element.18), channel_id=1, source_target_pairs={{8,0},{16,8},{24,16},{0,24},{10,2},{18,10},{26,18},{2,26},{12,4},{... | collective-permute-start | bytes 589832 | tf_op jit(solution)/shard_map/ppermute | solution.py:330
  33.3 171.1 %reduce-scatter.2.cloned.1.call-start = ((), (), s32[]{:S(2)}) async-start(), calls=%async_computation.2 | async-start | bytes 1966080 | tf_op jit(solution)/shard_map/reduce_scatter | solution.py:468
  33.3 34.7 %collective-permute-start.11 = (bf16[48,16,128]{2,1,0:T(8,128)(2,1)}, bf16[48,16,128]{2,1,0:T(8,128)(2,1)}, u32[]{:S(2)}, u32[]{:S(2)}) collective-permute-start(bf16[48,16,128]{2,1,0:T(8,128)(2,1)} %get-tuple-element.17), channel_id=1, source_target_pairs={{96,0},{0,32},{32,64},{64,96},{98,2},{2,34},{34,66},{66,98},{100,4... | collective-permute-start | bytes 589832 | tf_op jit(solution)/shard_map/ppermute | solution.py:330
  34.6 33.5 %collective-permute-start.10 = (bf16[48,16,128]{2,1,0:T(8,128)(2,1)}, bf16[48,16,128]{2,1,0:T(8,128)(2,1)}, u32[]{:S(2)}, u32[]{:S(2)}) collective-permute-start(bf16[48,16,128]{2,1,0:T(8,128)(2,1)} %get-tuple-element.17), channel_id=1, source_target_pairs={{64,0},{96,32},{0,64},{32,96},{66,2},{98,34},{2,66},{34,98},{68,4}... | collective-permute-start | bytes 589832 | tf_op jit(solution)/shard_map/ppermute | solution.py:330
  37.0 31.0 %collective-permute-start.9 = (bf16[48,16,128]{2,1,0:T(8,128)(2,1)}, bf16[48,16,128]{2,1,0:T(8,128)(2,1)}, u32[]{:S(2)}, u32[]{:S(2)}) collective-permute-start(bf16[48,16,128]{2,1,0:T(8,128)(2,1)} %get-tuple-element.17), channel_id=1, source_target_pairs={{32,0},{64,32},{96,64},{0,96},{34,2},{66,34},{98,66},{2,98},{36,4}... | collective-permute-start | bytes 589832 | tf_op jit(solution)/shard_map/ppermute | solution.py:330
  38.8 24.6 %collective-permute-start.1 = (bf16[4,16,256]{2,1,0:T(8,128)(2,1)}, bf16[4,16,256]{2,1,0:T(8,128)(2,1)}, u32[]{:S(2)}, u32[]{:S(2)}) collective-permute-start(bf16[4,16,256]{2,1,0:T(8,128)(2,1)} %get-tuple-element.16), channel_id=1, source_target_pairs={{2,0},{4,2},{6,4},{8,6},{10,8},{12,10},{14,12},{16,14},{18,16},{20... | collective-permute-start | bytes 98312 | tf_op jit(solution)/shard_map/ppermute | solution.py:134
  40.1 23.3 %collective-permute-start = (bf16[4,16,256]{2,1,0:T(8,128)(2,1)}, bf16[4,16,256]{2,1,0:T(8,128)(2,1)}, u32[]{:S(2)}, u32[]{:S(2)}) collective-permute-start(bf16[4,16,256]{2,1,0:T(8,128)(2,1)} %get-tuple-element.15), channel_id=1, source_target_pairs={{0,2},{2,4},{4,6},{6,8},{8,10},{10,12},{12,14},{14,16},{16,18},{18... | collective-permute-start | bytes 98312 | tf_op jit(solution)/shard_map/ppermute | solution.py:132
  57.8 0.9 copy-start.16
  63.4 4.6 %copy-start.14 = (bf16[48,16,128]{2,1,0:T(8,128)(2,1)S(1)}, bf16[48,16,128]{2,1,0:T(8,128)(2,1)}, u32[]{:S(2)}) copy-start(bf16[48,16,128]{2,1,0:T(8,128)(2,1)} %get-tuple-element.17) | copy-start | bytes 589828
  64.3 10.6 %copy-start.24 = (pred[128]{0:T(512)(128)(4,1)S(1)}, pred[128]{0:T(512)(128)(4,1)}, u32[]{:S(2)}) copy-start(pred[128]{0:T(512)(128)(4,1)} %iota_compare_fusion.14) | copy-start | bytes 388
  64.4 21.5 %copy-start.21 = (s32[128,6]{0,1:T(8,128)S(1)}, s32[128,6]{0,1:T(8,128)}, u32[]{:S(2)}) copy-start(s32[128,6]{0,1:T(8,128)} %param.19) | copy-start | bytes 9220
  65.3 30.5 %collective-permute-start.2 = (bf16[136,8,256]{2,1,0:T(8,128)(2,1)S(1)}, bf16[136,8,256]{2,1,0:T(8,128)(2,1)}, u32[]{:S(2)}, u32[]{:S(2)}) collective-permute-start(bf16[136,8,256]{2,1,0:T(8,128)(2,1)S(1)} %get-tuple-element.13), channel_id=1, source_target_pairs={{0,1},{1,0},{2,3},{3,2},{4,5},{5,4},{6,7},{7,6},{8,9},{9,8},{10,11... | collective-permute-start | bytes 1671176 | tf_op jit(solution)/shard_map/ppermute | solution.py:437
  70.2 60.4 %collective-permute-start.12 = (bf16[192,16,128]{2,1,0:T(8,128)(2,1)}, bf16[192,16,128]{2,1,0:T(8,128)(2,1)}, u32[]{:S(2)}, u32[]{:S(2)}) collective-permute-start(bf16[192,16,128]{2,1,0:T(8,128)(2,1)} %pad_maximum_fusion.4.refs_5_), channel_id=1, source_target_pairs={{8,0},{16,8},{24,16},{0,24},{10,2},{18,10},{26,18},{2,26},{12,4},{... | collective-permute-start | bytes 2359304 | tf_op jit(solution)/shard_map/ppermute | solution.py:330
  74.0 56.6 %collective-permute-start.13 = (bf16[192,16,128]{2,1,0:T(8,128)(2,1)}, bf16[192,16,128]{2,1,0:T(8,128)(2,1)}, u32[]{:S(2)}, u32[]{:S(2)}) collective-permute-start(bf16[192,16,128]{2,1,0:T(8,128)(2,1)} %pad_maximum_fusion.4.refs_5_), channel_id=1, source_target_pairs={{16,0},{24,8},{0,16},{8,24},{18,2},{26,10},{2,18},{10,26},{20,4},{... | collective-permute-start | bytes 2359304 | tf_op jit(solution)/shard_map/ppermute | solution.py:330
  74.7 55.9 %collective-permute-start.14 = (bf16[192,16,128]{2,1,0:T(8,128)(2,1)}, bf16[192,16,128]{2,1,0:T(8,128)(2,1)}, u32[]{:S(2)}, u32[]{:S(2)}) collective-permute-start(bf16[192,16,128]{2,1,0:T(8,128)(2,1)} %pad_maximum_fusion.4.refs_5_), channel_id=1, source_target_pairs={{24,0},{0,8},{8,16},{16,24},{26,2},{2,10},{10,18},{18,26},{28,4},{... | collective-permute-start | bytes 2359304 | tf_op jit(solution)/shard_map/ppermute | solution.py:330
  75.1 5.9 %collective-permute-start.3 = (s32[896]{0:T(1024)S(1)}, s32[896]{0:T(1024)S(1)}, u32[]{:S(2)}, u32[]{:S(2)}) collective-permute-start(s32[896]{0:T(1024)S(1)} %get-tuple-element.11), channel_id=1, source_target_pairs={{2,0},{4,2},{6,4},{0,6},{10,8},{12,10},{14,12},{8,14},{18,16},{20,... | collective-permute-start | bytes 10760 | tf_op jit(solution)/shard_map/ppermute | solution.py:330
  81.0 4.4 %collective-permute-start.4 = (s32[896]{0:T(1024)S(1)}, s32[896]{0:T(1024)S(1)}, u32[]{:S(2)}, u32[]{:S(2)}) collective-permute-start(s32[896]{0:T(1024)S(1)} %get-tuple-element.12), channel_id=1, source_target_pairs={{4,0},{6,2},{0,4},{2,6},{12,8},{14,10},{8,12},{10,14},{20,16},{22,... | collective-permute-start | bytes 10760 | tf_op jit(solution)/shard_map/ppermute | solution.py:330
  85.3 4.3 %collective-permute-start.5 = (s32[896]{0:T(1024)S(1)}, s32[896]{0:T(1024)S(1)}, u32[]{:S(2)}, u32[]{:S(2)}) collective-permute-start(s32[896]{0:T(1024)S(1)} %get-tuple-element.9), channel_id=1, source_target_pairs={{6,0},{0,2},{2,4},{4,6},{14,8},{8,10},{10,12},{12,14},{22,16},{16,... | collective-permute-start | bytes 10760 | tf_op jit(solution)/shard_map/ppermute | solution.py:330
  89.6 4.9 %collective-permute-start.15 = (bf16[96,8,128]{2,1,0:T(8,128)(2,1)S(1)}, bf16[96,8,128]{2,1,0:T(8,128)(2,1)S(1)}, u32[]{:S(2)}, u32[]{:S(2)}) collective-permute-start(bf16[96,8,128]{2,1,0:T(8,128)(2,1)S(1)} %slice.70.refs_9_), channel_id=1, source_target_pairs={{2,0},{4,2},{6,4},{0,6},{10,8},{12,10},{14,12},{8,14},{18,16},{20,... | collective-permute-start | bytes 589832 | tf_op jit(solution)/shard_map/ppermute | solution.py:330
  91.4 7.6 %copy-start.8 = (bf16[136,8,256]{2,1,0:T(8,128)(2,1)S(1)}, bf16[136,8,256]{2,1,0:T(8,128)(2,1)}, u32[]{:S(2)}) copy-start(bf16[136,8,256]{2,1,0:T(8,128)(2,1)} %get-tuple-element.14.pts) | copy-start | bytes 1671172
  94.6 36.0 %collective-permute-start.16 = (bf16[96,8,128]{2,1,0:T(8,128)(2,1)S(1)}, bf16[96,8,128]{2,1,0:T(8,128)(2,1)S(1)}, u32[]{:S(2)}, u32[]{:S(2)}) collective-permute-start(bf16[96,8,128]{2,1,0:T(8,128)(2,1)S(1)} %slice.70.refs_9_), channel_id=1, source_target_pairs={{4,0},{6,2},{0,4},{2,6},{12,8},{14,10},{8,12},{10,14},{20,16},{22,... | collective-permute-start | bytes 589832 | tf_op jit(solution)/shard_map/ppermute | solution.py:330
  95.7 34.8 %collective-permute-start.17 = (bf16[96,8,128]{2,1,0:T(8,128)(2,1)S(1)}, bf16[96,8,128]{2,1,0:T(8,128)(2,1)}, u32[]{:S(2)}, u32[]{:S(2)}) collective-permute-start(bf16[96,8,128]{2,1,0:T(8,128)(2,1)S(1)} %slice.70.refs_9_), channel_id=1, source_target_pairs={{6,0},{0,2},{2,4},{4,6},{14,8},{8,10},{10,12},{12,14},{22,16},{16,... | collective-permute-start | bytes 589832 | tf_op jit(solution)/shard_map/ppermute | solution.py:330
  129.5 1.0 copy-start.6
  130.6 40.8 %copy-start.4 = (f32[40,16,256]{2,1,0:T(8,128)}, f32[40,16,256]{2,1,0:T(8,128)S(1)}, u32[]{:S(2)}) copy-start(f32[40,16,256]{2,1,0:T(8,128)S(1)} %near.2) | copy-start | bytes 1966084
  130.6 2.1 copy-start.12
  169.9 1.2 copy-start.3
  171.0 27.8 %copy-start.23 = (s32[128]{0:T(128)S(1)}, s32[128]{0:T(128)}, u32[]{:S(2)}) copy-start(s32[128]{0:T(128)} %param.14) | copy-start | bytes 1540
  171.4 27.5 %copy-start.5 = (f32[40,16,256]{2,1,0:T(8,128)S(1)}, f32[40,16,256]{2,1,0:T(8,128)}, u32[]{:S(2)}) copy-start(f32[40,16,256]{2,1,0:T(8,128)} %copy-done.4) | copy-start | bytes 1966084
  171.4 27.6 %collective-permute-start.18 = (f32[40,8,256]{2,1,0:T(8,128)S(1)}, f32[40,8,256]{2,1,0:T(8,128)S(1)}, u32[]{:S(2)}, u32[]{:S(2)}) collective-permute-start(f32[40,8,256]{2,1,0:T(8,128)S(1)} %slice.71), channel_id=1, source_target_pairs={{0,1},{1,0},{2,3},{3,2},{4,5},{5,4},{6,7},{7,6},{8,9},{9,8},{10,11... | collective-permute-start | bytes 983048 | tf_op jit(solution)/shard_map/ppermute | solution.py:449
  176.1 1.2 copy-start.7
  177.3 1.1 copy-start.9
  198.7 1.5 collective-permute-start.19
  204.4 2.2 copy-start.1
  206.6 1.0 copy-start.2
  207.6 1.0 copy-start.10
Sparse Core Ops, SparseCore 0:
  33.4 42.1 all-gather.1
  171.2 33.1 reduce-scatter.1

commit v5 on v4

--- a/solution.py
+++ b/solution.py
@@ -181,18 +181,10 @@
 
 
 def far_kernel(units, *refs):
-    lists, (first_half, *rest), skels = refs[:4], refs[4:9], refs[9:13]
-    outs, table, sums, sems = refs[13:]
-    block = first_half.shape[0]
-    copies = [
-        pltpu.make_async_copy(first_half, table.at[pl.ds(0, block)], sems.at[0]),
-    ]
-    for n, piece in enumerate(rest):
-        size = piece.shape[0]
-        place = table.at[pl.ds(block + n * size, size)]
-        copies.append(pltpu.make_async_copy(piece, place, sems.at[n + 1]))
-    for copy in copies:
-        copy.start()
+    lists, gathered, skels = refs[:4], refs[4], refs[5:9]
+    outs, table, sums, sem = refs[9:]
+    copy = pltpu.make_async_copy(gathered, table, sem)
+    copy.start()
     targets = 2 * skels[0].shape[0]
     rank = skels[0].shape[2] // 2
     lane = lax.broadcasted_iota(jnp.int32, (DIM, 2 * rank), 1)
@@ -204,8 +196,7 @@
         return carry
 
     lax.fori_loop(0, sums.shape[0] // 4, clear, 0)
-    for copy in copies:
-        copy.wait()
+    copy.wait()
 
     def turned(array):
         return jnp.concatenate([array[:, rank:], array[:, :rank]], axis=1)
@@ -319,8 +310,9 @@
     return [[start + stride * k for k in range(SIDE)] for start in starts]
 
 
-def line_gather(block, axis):
-    return lax.all_gather(block, "leaf", axis_index_groups=lines(axis), tiled=True)
+def plane_gather(block):
+    groups = [[SIDE * k + z for k in range(SIDE * SIDE)] for z in range(SIDE)]
+    return lax.all_gather(block, "leaf", axis_index_groups=groups, tiled=True)
 
 
 def line_shift(block, axis, by):
@@ -334,21 +326,50 @@
     return [block] + [line_shift(block, axis, by) for by in range(1, SIDE)]
 
 
-def unit_lists(leaf_owner, leaf_local, upper_owner, upper_local, rows_each, capacity):
+def list_kernel(codes, lists):
+    count = codes.shape[1]
+    capacity = lists.shape[1] - 128
+    code = codes[0:1, :]
+    row = lax.broadcasted_iota(jnp.int32, (8, count), 0)
+    hits = jnp.where(row == code >> 20, 1.0, 0.0)
+    code = jnp.broadcast_to(code & (2**20 - 1), (8, count))
+    digits = [code & 127, (code >> 7) & 127, code >> 14]
+    weights = [hits * digit.astype(F32) for digit in digits] + [hits]
+    weights = jnp.concatenate(weights, axis=0).astype(BF16)
+    chunk = 256
+    ranks = jnp.zeros((8, count), F32)
+    for n in range(count // chunk):
+        before = lax.broadcasted_iota(jnp.int32, (chunk, count), 0) + n * chunk
+        after = lax.broadcasted_iota(jnp.int32, (chunk, count), 1)
+        ranks = ranks + jnp.dot(
+            hits[:, n * chunk : (n + 1) * chunk].astype(BF16),
+            jnp.where(before < after, 1.0, 0.0).astype(BF16),
+            preferred_element_type=F32,
+        )
+    rank = jnp.sum(ranks * hits, axis=0, keepdims=True).astype(jnp.int32)
+    parts = capacity // chunk
+    for n in range(parts):
+        place = lax.broadcasted_iota(jnp.int32, (chunk, count), 0) + n * chunk
+        spot = jnp.where(place == rank, 1.0, 0.0).astype(BF16)
+        found = lax.dot_general(
+            weights, spot, (((1,), (1,)), ((), ())), preferred_element_type=F32
+        ).astype(jnp.int32)
+        joined = found[:8] + (found[8:16] << 7) + (found[16:24] << 14)
+        dummy = codes[1:2, 0:chunk]
+        lists[:, n * chunk : (n + 1) * chunk] = jnp.where(found[24:] == 0, dummy, joined)
+    total = jnp.sum(hits, axis=1, keepdims=True).astype(jnp.int32)
+    lane = lax.broadcasted_iota(jnp.int32, (8, 128), 1)
+    lists[:, capacity:] = jnp.where(lane == 0, total, codes[2:3, 0:128])
+
+
+def unit_lists(leaf_owner, leaf_local, upper_owner, upper_local, capacity):
     me = lax.axis_index("leaf")
     leaves = leaf_owner.shape[0]
     parents = upper_owner.shape[0]
+    pairs = (leaves + parents) // 2
 
     def coded(owner, local, first_pair, first_target):
-        x = owner // (SIDE * SIDE)
-        x_ahead = (x - me // (SIDE * SIDE)) % SIDE
-        y_ahead = (owner // SIDE - me // SIDE) % SIDE
-        pair = first_pair + local // 2
-        row = jnp.where(
-            pair < rows_each,
-            (x * SIDE + y_ahead) * rows_each + pair,
-            (SIDE * SIDE + y_ahead * SIDE + x_ahead - 1) * rows_each + pair,
-        )
+        row = owner // SIDE * pairs + first_pair + local // 2
         target = first_target + lax.broadcasted_iota(jnp.int32, owner.shape, 0)
         return (owner % SIDE << 20) | (target << 12) | (row << 1) | (local & 1)
 
@@ -358,27 +379,20 @@
             coded(upper_owner, upper_local, leaves // 2, leaves),
         ],
         axis=0,
-    ).reshape(-1)
-    hits = (code[:, None] >> 20 == jnp.arange(SIDE, dtype=jnp.int32)[None, :]).astype(BF16)
-    code = code & (2**20 - 1)
-    number = code.shape[0]
-    order = jnp.arange(number, dtype=jnp.int32)
-    before = (order[None, :] < order[:, None]).astype(BF16)
-    rank = jnp.sum(jnp.dot(before, hits, preferred_element_type=F32) * hits.astype(F32), axis=1)
-    spot = (rank.astype(jnp.int32)[:, None] == jnp.arange(capacity, dtype=jnp.int32)[None, :]).astype(
-        BF16
-    )
-    digits = jnp.stack(
-        [(code & 127), ((code >> 7) & 127), (code >> 14), jnp.ones_like(code)], axis=0
-    ).astype(BF16)
-    weights = (hits.T[:, None, :] * digits[None]).reshape(SIDE * 4, number)
-    found = jnp.dot(weights, spot, preferred_element_type=F32).astype(jnp.int32)
-    found = found.reshape(SIDE, 4, capacity)
-    codes = found[:, 0] + (found[:, 1] << 7) + (found[:, 2] << 14)
-    codes = codes + jnp.where(found[:, 3] == 0, (leaves + parents) << 12, 0)
-    counts = jnp.sum(found[:, 3], axis=1)
-    tail = jnp.where(jnp.arange(128)[None, :] == 0, counts[:, None], me % SIDE)
-    return jnp.concatenate([codes, tail], axis=1)
+    ).reshape(1, -1)
+    kind = lax.broadcasted_iota(jnp.int32, (8, code.shape[1]), 0)
+    dummy = (leaves + parents) << 12
+    codes = jnp.where(kind == 0, code, jnp.where(kind == 1, dummy, me % SIDE))
+    vmem = pl.BlockSpec(memory_space=pltpu.VMEM)
+    return pl.pallas_call(
+        list_kernel,
+        out_shape=jax.ShapeDtypeStruct((8, capacity + 128), jnp.int32),
+        in_specs=[vmem],
+        out_specs=vmem,
+        compiler_params=pltpu.CompilerParams(vmem_limit_bytes=40 * 2**20),
+        cost_estimate=pl.CostEstimate(flops=10**8, bytes_accessed=10**5, transcendentals=0),
+        name="lists",
+    )(codes)
 
 
 def body(
@@ -402,7 +416,6 @@
     near_count = near_list.shape[1]
     half = leaf_dev // 2
     pairs = leaf_dev // 2 + leaf_dev // 4
-    rows_each = pairs // 2
     capacity = leaf_dev * far_owner.shape[1] * 3 // 4
     me = lax.axis_index("leaf")
     core = lax.axis_index("rhs")
@@ -423,10 +436,9 @@
         cost_estimate=pl.CostEstimate(flops=10**8, bytes_accessed=6 * 2**20, transcendentals=0),
         name="coef",
     )(masked, leaf_basis, transfer, leaf_skeleton, upper_skeleton)
-    first_half = line_gather(jnp.concatenate(line_shifts(table[:rows_each], 1), axis=0), 0)
-    second_half = line_shifts(jnp.concatenate(line_shifts(table[rows_each:], 0), axis=0), 1)
+    gathered = plane_gather(table)
     skels = line_shifts(table[:, :DIM], 2)
-    lists = unit_lists(far_owner, far_local, upper_owner, upper_local, rows_each, capacity)
+    lists = unit_lists(far_owner, far_local, upper_owner, upper_local, capacity)
     all_lists = [lists[me % SIDE]]
     for r in range(1, SIDE):
         all_lists.append(line_shift(lists[(me - r) % SIDE], 2, r))
@@ -447,24 +459,24 @@
         near_ids(chosen[:early], 0), extended[:, :DIM], cols, early, near_count
     )
     theirs_first = lax.ppermute(near_first[:, columns:], "rhs", swap)
-    first_half, _ = lax.optimization_barrier((first_half, near_first))
+    gathered, _ = lax.optimization_barrier((gathered, near_first))
 
     parts = pl.pallas_call(
         functools.partial(far_kernel, 32),
         out_shape=jax.ShapeDtypeStruct((SIDE, pairs, columns, 2 * rank), F32),
-        in_specs=[smem] * 4 + [anywhere] * 5 + [vmem] * 4,
+        in_specs=[smem] * 4 + [anywhere] + [vmem] * 4,
         out_specs=vmem,
         scratch_shapes=[
-            pltpu.VMEM((2 * SIDE * SIDE * rows_each, 2 * DIM, 2 * rank), BF16),
+            pltpu.VMEM((SIDE * SIDE * pairs, 2 * DIM, 2 * rank), BF16),
             pltpu.VMEM((SIDE * (2 * pairs + 1), columns, rank), F32),
-            pltpu.SemaphoreType.DMA((5,)),
+            pltpu.SemaphoreType.DMA,
         ],
         compiler_params=params,
         cost_estimate=pl.CostEstimate(
             flops=3 * 10**10, bytes_accessed=10 * 2**20, transcendentals=0
         ),
         name="far",
-    )(*all_lists, first_half, *second_half, *skels)
+    )(*all_lists, gathered, *skels)
     total = lax.psum_scatter(
         parts, "leaf", scatter_dimension=0, axis_index_groups=lines(2), tiled=True
     )[0]

time: 225 us -> 173 us (0.77); the launches traced: 221 us -> 172 us
  starting transfers between devices: 41.2 us -> 19.4 us
  local copies, waits for them, and re-layouts: 31.6 us -> 18.7 us
  waiting for transfers between devices: 22.2 us -> 12.2 us
  other arithmetic: 12.1 us -> 6.37 us
  Pallas kernels: 97.9 us -> 102 us
  matrix products: 2.46 us -> 0 us
    ppermute x15 -> x6, waiting for transfers between devices: 17.6 us -> 0.02 us  [line_shift(): return lax.ppermute(block, 'leaf', pairs)]
    ppermute x15 -> x6, starting transfers between devices: 27.6 us -> 10.5 us  [line_shift(): return lax.ppermute(block, 'leaf', pairs)]
    all_gather x1, waiting for transfers between devices: 0.01 us -> 7.75 us  [plane_gather(): return lax.all_gather(block, 'leaf', axis_index_groups=groups, tiled=True)]
    ppermute x1, starting transfers between devices: 4.62 us -> 0.93 us  [body(): theirs_first = lax.ppermute(near_first[:, columns:], 'rhs', swap)]
    another operation x4 -> x0, local copies, waits for them, and re-layouts: 3.63 us -> none
    concatenate x2 -> x1, other arithmetic: 3.14 us -> 0.01 us  [unit_lists(): jnp.concatenate([coded(leaf_owner, leaf_local, 0, 0), coded(upper_owner,...]
    and x2 -> x0, local copies, waits for them, and re-layouts: 3.01 us -> none  [the longest x1 1.5 us: unit_lists(): code >> 7 & 127]
    shift_right_arithmetic x3 -> x0, local copies, waits for them, and re-layouts: 2.67 us -> none  [the longest x2 1.75 us: unit_lists(): code[:, None] >> 20 == jnp.arange(SIDE, dtype=jnp.int32)[None, :]]
  transfers between devices with their start and end apart: 22 -> 13, of which waited for: 8 -> 3; matrix products, arithmetic and copies ran while one was open for 12% -> 4% of each run, Pallas kernels for 23% -> 30%
where the time goes in v5:
time: 173 us; the launch traced here: 172 us
  Pallas kernels  102 us (59%)
  starting transfers between devices  19.4 us (11%)
  local copies, waits for them, and re-layouts  18.7 us (11%)
  between operations  13.8 us (8%)
  waiting for transfers between devices  12.2 us (7%)
  other arithmetic  6.37 us (4%)
    pallas_call x2, Pallas kernels, near_field(): pl.pallas_call(functools.partial(near_kernel, near, leaves), out_shape=ja...  50.9 us
    pallas_call x1, Pallas kernels, body(): pl.pallas_call(functools.partial(far_kernel, 32), out_shape=jax.ShapeDtyp...  38.8 us
    unnamed x46, local copies, waits for them, and re-layouts  16.8 us
    ppermute x6, starting transfers between devices, line_shift(): return lax.ppermute(block, 'leaf', pairs)  10.5 us
    all_gather x1, waiting for transfers between devices, plane_gather(): return lax.all_gather(block, 'leaf', axis_index_groups=groups, tiled=True)  7.75 us
    pallas_call x1, Pallas kernels, body(): pl.pallas_call(final_kernel, out_shape=jax.ShapeDtypeStruct((leaf_dev, co...  5.86 us
    pallas_call x1, Pallas kernels, body(): pl.pallas_call(coef_kernel, out_shape=jax.ShapeDtypeStruct((pairs, 2 * DI...  4.78 us
    ppermute x1, starting transfers between devices, with_halo(): lax.ppermute(tail, axis, [(i, (i + 1) % count) for i in range(ends)])  4.48 us
  transfers between devices with their start and end apart: 13, of which 3 were waited for; matrix products, arithmetic and copies ran while one was open for 4% of the time, Pallas kernels for 30%

profile of v5, /device:TPU:1, one launch (start us, length us, event | category | flops | bytes accessed | tf_op | source)
XLA Modules:
  0.0 172.2 jit_solution(7942075537588841981)
XLA Ops:
  6.6 4.0 %copy.27.transfer = bf16[128,64,64]{2,1,0:T(8,128)(2,1)S(1)} copy(bf16[128,64,64]{0,2,1:T(8,128)(2,1)} %param.16) | data formatting | bytes 2097152 | tf_op args[4]
  10.6 0.7 iota_compare_fusion
  11.3 0.2 copy.26.leaf_skel
  11.5 0.9 broadcast_select_fusion.values
  12.4 2.2 %copy-done = bf16[128,64,256]{2,1,0:T(8,128)(2,1)S(1)} copy-done((bf16[128,64,256]{2,1,0:T(8,128)(2,1)S(1)}, bf16[128,64,256]{2,1,0:T(8,128)(2,1)}, u32[]{:S(2)}) %copy-start) | copy-done | bytes 4194328
  14.6 4.8 %coef.1 = bf16[96,16,128]{2,1,0:T(8,128)(2,1)} custom-call(bf16[128,8,256]{2,1,0:T(8,128)(2,1)S(1)} %broadcast_select_fusion.values, bf16[128,64,256]{2,1,0:T(8,128)(2,1)S(1)} %copy-done, bf16[128,64,64]{2,1,0:T(8,128)(2,1)S(1)} %copy.27.transfer, bf16[128,8,64]{2,1,0:T(8,128)(2,1)S(1)} %copy.26.leaf_skel, bf16[64,8,64]{2,1,0:T(8,128)(2,1)S(1)} %copy-done.9), custom_call_target="tpu_custom_call" | custom-call | flops 100000000 | bytes 6291456 | tf_op jit(solution)/shard_map/coef/pallas_call | solution.py:430
  19.5 1.0 slice.39.refs_5_
  20.5 4.7 %collective-permute-start.6 = (bf16[96,8,128]{2,1,0:T(8,128)(2,1)S(1)}, bf16[96,8,128]{2,1,0:T(8,128)(2,1)}, u32[]{:S(2)}, u32[]{:S(2)}) collective-permute-start(bf16[96,8,128]{2,1,0:T(8,128)(2,1)S(1)} %slice.39.refs_5_), channel_id=1, source_target_pairs={{2,0},{4,2},{6,4},{0,6},{10,8},{12,10},{14,12},{8,14},{18,16},{20,... | collective-permute-start | bytes 589832 | tf_op jit(solution)/shard_map/ppermute | solution.py:322
  25.1 0.7 collective-permute-start.8
  25.8 1.4 pad_maximum_fusion.5
  27.2 1.3 collective-permute-start.1
  28.5 4.5 %collective-permute-start = (bf16[4,16,256]{2,1,0:T(8,128)(2,1)S(1)}, bf16[4,16,256]{2,1,0:T(8,128)(2,1)S(1)}, u32[]{:S(2)}, u32[]{:S(2)}) collective-permute-start(bf16[4,16,256]{2,1,0:T(8,128)(2,1)S(1)} %get-tuple-element.15), channel_id=1, source_target_pairs={{0,2},{2,4},{4,6},{6,8},{8,10},{10,12},{12,14},{14,16},{16,18},{18... | collective-permute-start | bytes 98312 | tf_op jit(solution)/shard_map/ppermute | solution.py:132
  33.0 0.5 iota_compare_fusion.1
  33.6 0.5 compare_select_fusion
  34.1 0.1 copy.24
  34.2 0.1 broadcast_in_dim.45
  34.4 0.1 pad_maximum_fusion
  34.6 2.0 %collective-permute-start.2 = (bf16[136,8,256]{2,1,0:T(8,128)(2,1)S(1)}, bf16[136,8,256]{2,1,0:T(8,128)(2,1)}, u32[]{:S(2)}, u32[]{:S(2)}) collective-permute-start(bf16[136,8,256]{2,1,0:T(8,128)(2,1)S(1)} %get-tuple-element.13), channel_id=1, source_target_pairs={{0,1},{1,0},{2,3},{3,2},{4,5},{5,4},{6,7},{7,6},{8,9},{9,8},{10,11... | collective-permute-start | bytes 1671176 | tf_op jit(solution)/shard_map/ppermute | solution.py:449
  36.6 0.1 broadcast_select_fusion.1.codes
  36.7 1.3 lists.1
  38.1 3.7 %collective-permute-start.3 = (s32[896]{0:T(1024)S(1)}, s32[896]{0:T(1024)S(1)}, u32[]{:S(2)}, u32[]{:S(2)}) collective-permute-start(s32[896]{0:T(1024)S(1)} %get-tuple-element.11), channel_id=1, source_target_pairs={{2,0},{4,2},{6,4},{0,6},{10,8},{12,10},{14,12},{8,14},{18,16},{20,... | collective-permute-start | bytes 10760 | tf_op jit(solution)/shard_map/ppermute | solution.py:322
  41.8 0.1 constant_dynamic-slice_fusion
  41.8 0.1 copy.22
  41.9 0.1 reshape.23
  42.0 0.1 pad_add_fusion.2.ids
  42.1 0.6 collective-permute-start.4
  42.7 1.1 pad_maximum_fusion.1.cols
  43.9 0.9 collective-permute-start.5
  44.7 30.6 %near.2 = f32[40,16,256]{2,1,0:T(8,128)S(1)} custom-call(s32[241]{0:T(256)S(1)} %pad_add_fusion.2.ids, bf16[136,8,256]{2,1,0:T(8,128)(2,1)S(1)} %get-tuple-element.14.pts, bf16[136,16,256]{2,1,0:T(8,128)(2,1)S(1)} %pad_maximum_fusion.1.cols), custom_call_target="tpu_custom_call" | custom-call | flops 1006632960 | bytes 4194304 | tf_op jit(solution)/shard_map/near/pallas_call | solution.py:105
  75.3 1.0 copy-done.6
  76.3 7.8 %all-gather.2.cloned.1.call-done.refs_4_ = bf16[1536,16,128]{2,1,0:T(8,128)(2,1)} async-done(((bf16[96,16,128]{2,1,0:T(8,128)(2,1)}), bf16[1536,16,128]{2,1,0:T(8,128)(2,1)}) %all-gather.2.cloned.1.call-update) | async-done | bytes 6291472 | tf_op jit(solution)/shard_map/all_gather | solution.py:315
  84.1 2.8 %copy-done.10 = bf16[1536,16,128]{2,1,0:T(8,128)(2,1)S(1)} copy-done((bf16[1536,16,128]{2,1,0:T(8,128)(2,1)S(1)}, bf16[1536,16,128]{2,1,0:T(8,128)(2,1)}, u32[]{:S(2)}) %copy-start.10) | copy-done | bytes 6291480
  86.9 38.8 %far.1 = f32[4,96,8,128]{3,2,1,0:T(8,128)S(1)} custom-call(s32[896]{0:T(1024)S(1)} %get-tuple-element.12.refs_0_, s32[896]{0:T(1024)S(1)} %collective-permute-done.3.refs_1_, s32[896]{0:T(1024)S(1)} %collective-permute-done.4.refs_2_, s32[896]{0:T(1024)S(1)} %collective-permute-done.5.refs_3_, bf16[1536,16,128]{2,1,0:T(8,128)(2,1)S(1)} %copy-done.10, ...), custom_call_target="tpu_custom_call" | custom-call | flops 30000001024 | bytes 10485760 | tf_op jit(solution)/shard_map/far/pallas_call | solution.py:464
  125.7 1.2 copy-done.3
  127.0 0.1 copy.23
  127.1 0.1 reshape.24
  127.2 0.9 collective-permute-start.9
  128.2 0.1 pad_add_fusion.3.ids
  128.2 1.2 copy-done.7
  129.5 20.3 %near.3 = f32[24,16,256]{2,1,0:T(8,128)S(1)} custom-call(s32[145]{0:T(256)S(1)} %pad_add_fusion.3.ids, bf16[136,8,256]{2,1,0:T(8,128)(2,1)S(1)} %get-tuple-element.14.pts, bf16[136,16,256]{2,1,0:T(8,128)(2,1)S(1)} %copy-done.7), custom_call_target="tpu_custom_call" | custom-call | flops 603979776 | bytes 4194304 | tf_op jit(solution)/shard_map/near/pallas_call | solution.py:105
  149.9 0.1 collective-permute-start.10
  150.1 1.3 collective-permute-done.10
  151.4 0.8 pad_maximum_fusion.3.near_theirs
  152.2 3.1 %reduce-scatter.2.cloned.1.call-done = f32[1,96,8,128]{3,2,1,0:T(8,128)} async-done(((f32[4,96,8,128]{3,2,1,0:T(8,128)}), f32[1,96,8,128]{3,2,1,0:T(8,128)}) %reduce-scatter.2.cloned.1.call-update) | async-done | bytes 393232 | tf_op jit(solution)/shard_map/reduce_scatter | solution.py:480
  155.3 2.2 %copy-done.1 = bf16[128,64,256]{2,1,0:T(8,128)(2,1)S(1)} copy-done((bf16[128,64,256]{2,1,0:T(8,128)(2,1)S(1)}, bf16[128,64,256]{2,1,0:T(8,128)(2,1)}, u32[]{:S(2)}) %copy-start.1) | copy-done | bytes 4194328
  157.5 1.0 copy-done.2
  158.5 1.0 copy-done.8
  159.5 5.9 %final.1 = f32[128,8,256]{2,1,0:T(8,128)} custom-call(s32[129]{0:T(256)S(1)} %pad_add_fusion.1.counts, bf16[128,64,64]{2,1,0:T(8,128)(2,1)S(1)} %copy.27.transfer, bf16[128,64,256]{2,1,0:T(8,128)(2,1)S(1)} %copy-done.1, f32[64,16,256]{2,1,0:T(8,128)S(1)} %pad_maximum_fusion.2.near_mine, f32[64,8,256]{2,1,0:T(8,128)S(1)} %copy-done.2, f32[96,8,128]{2,1,0:T(8,128)S(1)} %bitcast.5), custom_call_target="tpu_custom_call" | custom-call | tf_op jit(solution)/shard_map/final/pallas_call | solution.py:491
  (64 shorter events, 0.6 us)
Async XLA Ops:
  6.5 4.1 %copy-start.19 = (s32[128]{0:T(128)S(1)}, s32[128]{0:T(128)}, u32[]{:S(2)}) copy-start(s32[128]{0:T(128)} %param.14) | copy-start | bytes 1540
  6.5 4.8 %copy-start.13 = (bf16[128,8,64]{0,2,1:T(8,128)(2,1)S(1)}, bf16[128,8,64]{0,2,1:T(8,128)(2,1)}, u32[]{:S(2)}) copy-start(bf16[128,8,64]{0,2,1:T(8,128)(2,1)} %param.17) | copy-start | bytes 393220
  6.5 5.0 %copy-start.12 = (bf16[128,8,256]{2,1,0:T(8,128)(2,1)S(1)}, bf16[128,8,256]{2,1,0:T(8,128)(2,1)}, u32[]{:S(2)}) copy-start(bf16[128,8,256]{2,1,0:T(8,128)(2,1)} %param.13) | copy-start | bytes 1572868
  6.5 5.9 %copy-start.9 = (bf16[64,8,64]{2,1,0:T(8,128)(2,1)S(1)}, bf16[64,8,64]{2,1,0:T(8,128)(2,1)}, u32[]{:S(2)}) copy-start(bf16[64,8,64]{2,1,0:T(8,128)(2,1)} %upper_skel.1) | copy-start | bytes 196612
  6.5 77.5 %all-gather.2.cloned.1.call-start = ((), (), s32[]{:S(2)}) async-start(), calls=%async_computation.1 | async-start | bytes 6684672 | tf_op jit(solution)/shard_map/all_gather | solution.py:315
  12.4 2.2 %copy-start = (bf16[128,64,256]{2,1,0:T(8,128)(2,1)S(1)}, bf16[128,64,256]{2,1,0:T(8,128)(2,1)}, u32[]{:S(2)}) copy-start(bf16[128,64,256]{2,1,0:T(8,128)(2,1)} %basis.3) | copy-start | bytes 12582916
  14.6 18.9 %copy-start.14 = (s32[64,8]{0,1:T(8,128)S(1)}, s32[64,8]{0,1:T(8,128)}, u32[]{:S(2)}) copy-start(s32[64,8]{0,1:T(8,128)} %param.23) | copy-start | bytes 6148
  14.6 18.9 %copy-start.15 = (s32[64,8]{0,1:T(8,128)S(1)}, s32[64,8]{0,1:T(8,128)}, u32[]{:S(2)}) copy-start(s32[64,8]{0,1:T(8,128)} %param.22) | copy-start | bytes 6148
  14.6 18.9 %copy-start.16 = (s32[128,8]{0,1:T(8,128)S(1)}, s32[128,8]{0,1:T(8,128)}, u32[]{:S(2)}) copy-start(s32[128,8]{0,1:T(8,128)} %param.21) | copy-start | bytes 12292
  14.6 18.9 %copy-start.17 = (s32[128,8]{0,1:T(8,128)S(1)}, s32[128,8]{0,1:T(8,128)}, u32[]{:S(2)}) copy-start(s32[128,8]{0,1:T(8,128)} %param.20) | copy-start | bytes 12292
  19.4 15.0 %copy-start.11 = (bf16[128,8,256]{2,1,0:T(8,128)(2,1)S(1)}, bf16[128,8,256]{2,1,0:T(8,128)(2,1)}, u32[]{:S(2)}) copy-start(bf16[128,8,256]{2,1,0:T(8,128)(2,1)} %param.12) | copy-start | bytes 1572868
  19.4 135.8 %reduce-scatter.2.cloned.1.call-start = ((), (), s32[]{:S(2)}) async-start(), calls=%async_computation.2 | async-start | bytes 1966080 | tf_op jit(solution)/shard_map/reduce_scatter | solution.py:480
  20.5 63.6 %collective-permute-start.6 = (bf16[96,8,128]{2,1,0:T(8,128)(2,1)S(1)}, bf16[96,8,128]{2,1,0:T(8,128)(2,1)}, u32[]{:S(2)}, u32[]{:S(2)}) collective-permute-start(bf16[96,8,128]{2,1,0:T(8,128)(2,1)S(1)} %slice.39.refs_5_), channel_id=1, source_target_pairs={{2,0},{4,2},{6,4},{0,6},{10,8},{12,10},{14,12},{8,14},{18,16},{20,... | collective-permute-start | bytes 589832 | tf_op jit(solution)/shard_map/ppermute | solution.py:322
  25.1 58.9 %collective-permute-start.7 = (bf16[96,8,128]{2,1,0:T(8,128)(2,1)S(1)}, bf16[96,8,128]{2,1,0:T(8,128)(2,1)}, u32[]{:S(2)}, u32[]{:S(2)}) collective-permute-start(bf16[96,8,128]{2,1,0:T(8,128)(2,1)S(1)} %slice.39.refs_5_), channel_id=1, source_target_pairs={{4,0},{6,2},{0,4},{2,6},{12,8},{14,10},{8,12},{10,14},{20,16},{22,... | collective-permute-start | bytes 589832 | tf_op jit(solution)/shard_map/ppermute | solution.py:322
  25.1 58.9 %collective-permute-start.8 = (bf16[96,8,128]{2,1,0:T(8,128)(2,1)S(1)}, bf16[96,8,128]{2,1,0:T(8,128)(2,1)}, u32[]{:S(2)}, u32[]{:S(2)}) collective-permute-start(bf16[96,8,128]{2,1,0:T(8,128)(2,1)S(1)} %slice.39.refs_5_), channel_id=1, source_target_pairs={{6,0},{0,2},{2,4},{4,6},{14,8},{8,10},{10,12},{12,14},{22,16},{16,... | collective-permute-start | bytes 589832 | tf_op jit(solution)/shard_map/ppermute | solution.py:322
  27.2 7.2 %collective-permute-start.1 = (bf16[4,16,256]{2,1,0:T(8,128)(2,1)}, bf16[4,16,256]{2,1,0:T(8,128)(2,1)S(1)}, u32[]{:S(2)}, u32[]{:S(2)}) collective-permute-start(bf16[4,16,256]{2,1,0:T(8,128)(2,1)} %get-tuple-element.16), channel_id=1, source_target_pairs={{2,0},{4,2},{6,4},{8,6},{10,8},{12,10},{14,12},{16,14},{18,16},{20... | collective-permute-start | bytes 98312 | tf_op jit(solution)/shard_map/ppermute | solution.py:134
  28.5 5.9 %collective-permute-start = (bf16[4,16,256]{2,1,0:T(8,128)(2,1)S(1)}, bf16[4,16,256]{2,1,0:T(8,128)(2,1)S(1)}, u32[]{:S(2)}, u32[]{:S(2)}) collective-permute-start(bf16[4,16,256]{2,1,0:T(8,128)(2,1)S(1)} %get-tuple-element.15), channel_id=1, source_target_pairs={{0,2},{2,4},{4,6},{6,8},{8,10},{10,12},{12,14},{14,16},{16,18},{18... | collective-permute-start | bytes 98312 | tf_op jit(solution)/shard_map/ppermute | solution.py:132
  34.3 2.3 %copy-start.20 = (pred[8]{0:T(512)(128)(4,1)S(1)}, pred[8]{0:T(512)(128)(4,1)}, u32[]{:S(2)}) copy-start(pred[8]{0:T(512)(128)(4,1)} %iota_compare_fusion.1) | copy-start | bytes 28
  34.3 2.3 %copy-start.21 = (s32[8]{0:T(128)S(1)}, s32[8]{0:T(128)}, u32[]{:S(2)}) copy-start(s32[8]{0:T(128)} %compare_select_fusion) | copy-start | bytes 100
  34.3 7.4 %copy-start.18 = (s32[128,6]{0,1:T(8,128)S(1)}, s32[128,6]{0,1:T(8,128)}, u32[]{:S(2)}) copy-start(s32[128,6]{0,1:T(8,128)} %param.19) | copy-start | bytes 9220
  34.6 7.6 %collective-permute-start.2 = (bf16[136,8,256]{2,1,0:T(8,128)(2,1)S(1)}, bf16[136,8,256]{2,1,0:T(8,128)(2,1)}, u32[]{:S(2)}, u32[]{:S(2)}) collective-permute-start(bf16[136,8,256]{2,1,0:T(8,128)(2,1)S(1)} %get-tuple-element.13), channel_id=1, source_target_pairs={{0,1},{1,0},{2,3},{3,2},{4,5},{5,4},{6,7},{7,6},{8,9},{9,8},{10,11... | collective-permute-start | bytes 1671176 | tf_op jit(solution)/shard_map/ppermute | solution.py:449
  38.1 5.8 %collective-permute-start.3 = (s32[896]{0:T(1024)S(1)}, s32[896]{0:T(1024)S(1)}, u32[]{:S(2)}, u32[]{:S(2)}) collective-permute-start(s32[896]{0:T(1024)S(1)} %get-tuple-element.11), channel_id=1, source_target_pairs={{2,0},{4,2},{6,4},{0,6},{10,8},{12,10},{14,12},{8,14},{18,16},{20,... | collective-permute-start | bytes 10760 | tf_op jit(solution)/shard_map/ppermute | solution.py:322
  42.1 41.9 %collective-permute-start.4 = (s32[896]{0:T(1024)S(1)}, s32[896]{0:T(1024)S(1)}, u32[]{:S(2)}, u32[]{:S(2)}) collective-permute-start(s32[896]{0:T(1024)S(1)} %get-tuple-element.10), channel_id=1, source_target_pairs={{4,0},{6,2},{0,4},{2,6},{12,8},{14,10},{8,12},{10,14},{20,16},{22,... | collective-permute-start | bytes 10760 | tf_op jit(solution)/shard_map/ppermute | solution.py:322
  43.9 40.2 %collective-permute-start.5 = (s32[896]{0:T(1024)S(1)}, s32[896]{0:T(1024)S(1)}, u32[]{:S(2)}, u32[]{:S(2)}) collective-permute-start(s32[896]{0:T(1024)S(1)} %get-tuple-element.9), channel_id=1, source_target_pairs={{6,0},{0,2},{2,4},{4,6},{14,8},{8,10},{10,12},{12,14},{22,16},{16,... | collective-permute-start | bytes 10760 | tf_op jit(solution)/shard_map/ppermute | solution.py:322
  75.3 1.0 copy-start.6
  76.3 50.9 %copy-start.4 = (f32[40,16,256]{2,1,0:T(8,128)}, f32[40,16,256]{2,1,0:T(8,128)S(1)}, u32[]{:S(2)}) copy-start(f32[40,16,256]{2,1,0:T(8,128)S(1)} %near.2) | copy-start | bytes 1966084
  84.1 2.8 %copy-start.10 = (bf16[1536,16,128]{2,1,0:T(8,128)(2,1)S(1)}, bf16[1536,16,128]{2,1,0:T(8,128)(2,1)}, u32[]{:S(2)}) copy-start(bf16[1536,16,128]{2,1,0:T(8,128)(2,1)} %all-gather.2.cloned.1.call-done.refs_4_) | copy-start | bytes 18874372
  125.7 1.2 copy-start.3
  127.2 22.8 %copy-start.5 = (f32[40,16,256]{2,1,0:T(8,128)S(1)}, f32[40,16,256]{2,1,0:T(8,128)}, u32[]{:S(2)}) copy-start(f32[40,16,256]{2,1,0:T(8,128)} %copy-done.4) | copy-start | bytes 1966084
  127.2 22.8 %collective-permute-start.9 = (f32[40,8,256]{2,1,0:T(8,128)S(1)}, f32[40,8,256]{2,1,0:T(8,128)S(1)}, u32[]{:S(2)}, u32[]{:S(2)}) collective-permute-start(f32[40,8,256]{2,1,0:T(8,128)S(1)} %slice.40), channel_id=1, source_target_pairs={{0,1},{1,0},{2,3},{3,2},{4,5},{5,4},{6,7},{7,6},{8,9},{9,8},{10,11... | collective-permute-start | bytes 983048 | tf_op jit(solution)/shard_map/ppermute | solution.py:461
  128.2 1.2 copy-start.7
  149.9 1.5 collective-permute-start.10
  155.3 2.2 %copy-start.1 = (bf16[128,64,256]{2,1,0:T(8,128)(2,1)S(1)}, bf16[128,64,256]{2,1,0:T(8,128)(2,1)}, u32[]{:S(2)}) copy-start(bf16[128,64,256]{2,1,0:T(8,128)(2,1)} %basis.3) | copy-start | bytes 12582916
  157.5 1.0 copy-start.2
  158.5 1.0 copy-start.8
Sparse Core Ops, SparseCore 0:
  19.6 64.4 all-gather.1
  127.0 28.2 reduce-scatter.1

commit v6 on v5

--- a/solution.py
+++ b/solution.py
@@ -181,14 +181,18 @@
 
 
 def far_kernel(units, *refs):
-    lists, gathered, skels = refs[:4], refs[4], refs[5:9]
-    outs, table, sums, sem = refs[9:]
-    copy = pltpu.make_async_copy(gathered, table, sem)
-    copy.start()
+    lists, table, skels = refs[:4], refs[4], refs[5:9]
+    outs, sums = refs[9:]
     targets = 2 * skels[0].shape[0]
     rank = skels[0].shape[2] // 2
     lane = lax.broadcasted_iota(jnp.int32, (DIM, 2 * rank), 1)
     low = lane < rank
+    wide = lax.broadcasted_iota(jnp.int32, (2 * DIM, 2 * rank), 1)
+    low_wide = wide < rank
+    keep_low = jnp.where(low_wide, 1.0, 0.0).astype(BF16)
+    keep_high = jnp.where(low_wide, 0.0, 1.0).astype(BF16)
+    blank = jnp.zeros((2 * DIM, 2 * rank), BF16)
+    empty = jnp.zeros((DIM, 2 * rank), F32)
 
     def clear(i, carry):
         for n in range(4):
@@ -196,7 +200,6 @@
         return carry
 
     lax.fori_loop(0, sums.shape[0] // 4, clear, 0)
-    copy.wait()
 
     def turned(array):
         return jnp.concatenate([array[:, rank:], array[:, :rank]], axis=1)
@@ -208,30 +211,31 @@
             where, squares, weights = [], [], []
             for quad in range(units // 4):
                 left, right, coefs = [], [], []
-                for n in range(4):
-                    entry = listed[i * units + quad * 4 + n]
-                    target = entry >> 12
-                    row = (entry >> 1) & 2047
-                    source = table[row].astype(F32)
-                    swap = (entry & 1) != (n % 2)
-                    source = jnp.where(swap, turned(source), source)
-                    keep = low if n % 2 == 0 else jnp.logical_not(low)
-                    form = jnp.where(
-                        jnp.concatenate([keep, keep], axis=0), source_form(source[:DIM]), 0.0
-                    )
-                    coef = jnp.where(keep, source[DIM:], 0.0)
-                    blank = jnp.zeros_like(form)
-                    empty = jnp.zeros_like(coef)
-                    wide = [form, blank] if n < 2 else [blank, form]
-                    right.append(jnp.concatenate(wide, axis=1))
-                    wide = [coef, empty] if n < 2 else [empty, coef]
-                    coefs.append(jnp.concatenate(wide, axis=1))
-                    pair = skel[jnp.minimum(target, targets - 1) >> 1].astype(F32)
-                    pair = jnp.where((target & 1) == 1, turned(pair), pair)
-                    left.append(target_form(pair))
-                    where.append(first + target)
+                for m in range(2):
+                    sources, goals = [], []
+                    for n in range(2):
+                        entry = listed[i * units + quad * 4 + m * 2 + n]
+                        target = entry >> 12
+                        source = table[(entry >> 1) & 2047].astype(F32)
+                        swap = (entry & 1) != n
+                        sources.append(jnp.where(swap, turned(source), source))
+                        goal = skel[jnp.minimum(target, targets - 1) >> 1].astype(F32)
+                        swap = (target & 1) != n
+                        goals.append(jnp.where(swap, turned(goal), goal))
+                        where.append(first + target)
+                    source = jnp.where(low_wide, sources[0], sources[1])
+                    form = source_form(source[:DIM]).astype(BF16)
+                    coef = source[DIM:]
+                    for keep in (keep_low, keep_high):
+                        pieces = [form * keep, blank] if m == 0 else [blank, form * keep]
+                        right.append(jnp.concatenate(pieces, axis=1))
+                    for piece in (jnp.where(low, coef, 0.0), jnp.where(low, 0.0, coef)):
+                        pieces = [piece, empty] if m == 0 else [empty, piece]
+                        coefs.append(jnp.concatenate(pieces, axis=1))
+                    form = target_form(jnp.where(low, goals[0], goals[1]))
+                    left += [form, turned(form)]
                 left = jnp.concatenate(left, axis=0)[:, :rank].astype(BF16)
-                right = jnp.concatenate(right, axis=0).astype(BF16)
+                right = jnp.concatenate(right, axis=0)
                 weights.append(jnp.concatenate(coefs, axis=0).astype(BF16))
                 squares.append(
                     lax.dot_general(
@@ -422,7 +426,6 @@
     swap = [(0, 1), (1, 0)]
     vmem = pl.BlockSpec(memory_space=pltpu.VMEM)
     smem = pl.BlockSpec(memory_space=pltpu.SMEM)
-    anywhere = pl.BlockSpec(memory_space=pl.ANY)
     params = pltpu.CompilerParams(vmem_limit_bytes=40 * 2**20)
 
     point_live = lax.broadcasted_iota(jnp.int32, (leaf_dev, leaf_size), 1) < counts[:, None]
@@ -464,12 +467,10 @@
     parts = pl.pallas_call(
         functools.partial(far_kernel, 32),
         out_shape=jax.ShapeDtypeStruct((SIDE, pairs, columns, 2 * rank), F32),
-        in_specs=[smem] * 4 + [anywhere] + [vmem] * 4,
+        in_specs=[smem] * 4 + [vmem] * 5,
         out_specs=vmem,
         scratch_shapes=[
-            pltpu.VMEM((SIDE * SIDE * pairs, 2 * DIM, 2 * rank), BF16),
             pltpu.VMEM((SIDE * (2 * pairs + 1), columns, rank), F32),
-            pltpu.SemaphoreType.DMA,
         ],
         compiler_params=params,
         cost_estimate=pl.CostEstimate(

time: 173 us -> 177 us (1.023)
  Pallas kernels: 102 us -> 109 us
  waiting for transfers between devices: 12.2 us -> 9.12 us
    pallas_call x1, Pallas kernels: 38.8 us -> 46.6 us  [body(): pl.pallas_call(functools.partial(far_kernel, 32), out_shape=jax.ShapeDtyp...]
    reduce_scatter x1, waiting for transfers between devices: 3.09 us -> 0.01 us  [body(): lax.psum_scatter(parts, 'leaf', scatter_dimension=0, axis_index_groups=li...]
  transfers between devices with their start and end apart: 13 -> 13, of which waited for: 3 -> 2; matrix products, arithmetic and copies ran while one was open for 4% -> 4% of each run, Pallas kernels for 30% -> 30%
where the time goes in v6:
time: 177 us
  Pallas kernels  109 us (62%)
  starting transfers between devices  19.4 us (11%)
  local copies, waits for them, and re-layouts  18.7 us (11%)
  between operations  13.8 us (8%)
  waiting for transfers between devices  9.12 us (5%)
  other arithmetic  6.36 us (4%)
    pallas_call x2, Pallas kernels, near_field(): pl.pallas_call(functools.partial(near_kernel, near, leaves), out_shape=ja...  50.9 us
    pallas_call x1, Pallas kernels, body(): pl.pallas_call(functools.partial(far_kernel, 32), out_shape=jax.ShapeDtyp...  46.6 us
    unnamed x46, local copies, waits for them, and re-layouts  16.8 us
    ppermute x6, starting transfers between devices, line_shift(): return lax.ppermute(block, 'leaf', pairs)  10.5 us
    all_gather x1, waiting for transfers between devices, plane_gather(): return lax.all_gather(block, 'leaf', axis_index_groups=groups, tiled=True)  7.75 us
    pallas_call x1, Pallas kernels, body(): pl.pallas_call(final_kernel, out_shape=jax.ShapeDtypeStruct((leaf_dev, co...  5.86 us
    pallas_call x1, Pallas kernels, body(): pl.pallas_call(coef_kernel, out_shape=jax.ShapeDtypeStruct((pairs, 2 * DI...  4.78 us
    ppermute x1, starting transfers between devices, with_halo(): lax.ppermute(tail, axis, [(i, (i + 1) % count) for i in range(ends)])  4.48 us
  transfers between devices with their start and end apart: 13, of which 2 were waited for; matrix products, arithmetic and copies ran while one was open for 4% of the time, Pallas kernels for 30%

profile of v6, /device:TPU:1, one launch (start us, length us, event | category | flops | bytes accessed | tf_op | source)
XLA Modules:
  0.0 176.9 jit_solution(18243519114218090617)
XLA Ops:
  6.6 4.0 %copy.27.transfer = bf16[128,64,64]{2,1,0:T(8,128)(2,1)S(1)} copy(bf16[128,64,64]{0,2,1:T(8,128)(2,1)} %param.16) | data formatting | bytes 2097152 | tf_op args[4]
  10.6 0.7 iota_compare_fusion
  11.3 0.2 copy.26.leaf_skel
  11.5 0.9 broadcast_select_fusion.values
  12.4 2.2 %copy-done = bf16[128,64,256]{2,1,0:T(8,128)(2,1)S(1)} copy-done((bf16[128,64,256]{2,1,0:T(8,128)(2,1)S(1)}, bf16[128,64,256]{2,1,0:T(8,128)(2,1)}, u32[]{:S(2)}) %copy-start) | copy-done | bytes 4194328
  14.6 4.8 %coef.1 = bf16[96,16,128]{2,1,0:T(8,128)(2,1)} custom-call(bf16[128,8,256]{2,1,0:T(8,128)(2,1)S(1)} %broadcast_select_fusion.values, bf16[128,64,256]{2,1,0:T(8,128)(2,1)S(1)} %copy-done, bf16[128,64,64]{2,1,0:T(8,128)(2,1)S(1)} %copy.27.transfer, bf16[128,8,64]{2,1,0:T(8,128)(2,1)S(1)} %copy.26.leaf_skel, bf16[64,8,64]{2,1,0:T(8,128)(2,1)S(1)} %copy-done.9), custom_call_target="tpu_custom_call" | custom-call | flops 100000000 | bytes 6291456 | tf_op jit(solution)/shard_map/coef/pallas_call | solution.py:433
  19.5 1.0 slice.39.refs_5_
  20.5 4.7 %collective-permute-start.6 = (bf16[96,8,128]{2,1,0:T(8,128)(2,1)S(1)}, bf16[96,8,128]{2,1,0:T(8,128)(2,1)}, u32[]{:S(2)}, u32[]{:S(2)}) collective-permute-start(bf16[96,8,128]{2,1,0:T(8,128)(2,1)S(1)} %slice.39.refs_5_), channel_id=1, source_target_pairs={{2,0},{4,2},{6,4},{0,6},{10,8},{12,10},{14,12},{8,14},{18,16},{20,... | collective-permute-start | bytes 589832 | tf_op jit(solution)/shard_map/ppermute | solution.py:326
  25.1 0.7 collective-permute-start.8
  25.8 1.4 pad_maximum_fusion.5
  27.2 1.3 collective-permute-start.1
  28.5 4.5 %collective-permute-start = (bf16[4,16,256]{2,1,0:T(8,128)(2,1)S(1)}, bf16[4,16,256]{2,1,0:T(8,128)(2,1)S(1)}, u32[]{:S(2)}, u32[]{:S(2)}) collective-permute-start(bf16[4,16,256]{2,1,0:T(8,128)(2,1)S(1)} %get-tuple-element.15), channel_id=1, source_target_pairs={{0,2},{2,4},{4,6},{6,8},{8,10},{10,12},{12,14},{14,16},{16,18},{18... | collective-permute-start | bytes 98312 | tf_op jit(solution)/shard_map/ppermute | solution.py:132
  33.0 0.5 iota_compare_fusion.1
  33.6 0.5 compare_select_fusion
  34.1 0.1 copy.24
  34.2 0.1 broadcast_in_dim.45
  34.4 0.1 pad_maximum_fusion
  34.5 0.1 fusion.27
  34.6 2.0 %collective-permute-start.2 = (bf16[136,8,256]{2,1,0:T(8,128)(2,1)S(1)}, bf16[136,8,256]{2,1,0:T(8,128)(2,1)}, u32[]{:S(2)}, u32[]{:S(2)}) collective-permute-start(bf16[136,8,256]{2,1,0:T(8,128)(2,1)S(1)} %get-tuple-element.13), channel_id=1, source_target_pairs={{0,1},{1,0},{2,3},{3,2},{4,5},{5,4},{6,7},{7,6},{8,9},{9,8},{10,11... | collective-permute-start | bytes 1671176 | tf_op jit(solution)/shard_map/ppermute | solution.py:452
  36.6 0.1 broadcast_select_fusion.1.codes
  36.7 1.3 lists.1
  38.1 3.7 %collective-permute-start.3 = (s32[896]{0:T(1024)S(1)}, s32[896]{0:T(1024)S(1)}, u32[]{:S(2)}, u32[]{:S(2)}) collective-permute-start(s32[896]{0:T(1024)S(1)} %get-tuple-element.11), channel_id=1, source_target_pairs={{2,0},{4,2},{6,4},{0,6},{10,8},{12,10},{14,12},{8,14},{18,16},{20,... | collective-permute-start | bytes 10760 | tf_op jit(solution)/shard_map/ppermute | solution.py:326
  41.8 0.1 constant_dynamic-slice_fusion
  41.8 0.1 copy.22
  41.9 0.1 reshape.23
  42.0 0.1 pad_add_fusion.2.ids
  42.1 0.6 collective-permute-start.4
  42.7 1.1 pad_maximum_fusion.1.cols
  43.9 0.9 collective-permute-start.5
  44.7 30.6 %near.2 = f32[40,16,256]{2,1,0:T(8,128)S(1)} custom-call(s32[241]{0:T(256)S(1)} %pad_add_fusion.2.ids, bf16[136,8,256]{2,1,0:T(8,128)(2,1)S(1)} %get-tuple-element.14.pts, bf16[136,16,256]{2,1,0:T(8,128)(2,1)S(1)} %pad_maximum_fusion.1.cols), custom_call_target="tpu_custom_call" | custom-call | flops 1006632960 | bytes 4194304 | tf_op jit(solution)/shard_map/near/pallas_call | solution.py:105
  75.3 1.0 copy-done.6
  76.3 7.8 %all-gather.2.cloned.1.call-done.refs_4_ = bf16[1536,16,128]{2,1,0:T(8,128)(2,1)} async-done(((bf16[96,16,128]{2,1,0:T(8,128)(2,1)}), bf16[1536,16,128]{2,1,0:T(8,128)(2,1)}) %all-gather.2.cloned.1.call-update) | async-done | bytes 6291472 | tf_op jit(solution)/shard_map/all_gather | solution.py:319
  84.1 2.8 %copy-done.10 = bf16[1536,16,128]{2,1,0:T(8,128)(2,1)S(1)} copy-done((bf16[1536,16,128]{2,1,0:T(8,128)(2,1)S(1)}, bf16[1536,16,128]{2,1,0:T(8,128)(2,1)}, u32[]{:S(2)}) %copy-start.10) | copy-done | bytes 6291480
  86.9 46.6 %far.1 = f32[4,96,8,128]{3,2,1,0:T(8,128)S(1)} custom-call(s32[896]{0:T(1024)S(1)} %get-tuple-element.12.refs_0_, s32[896]{0:T(1024)S(1)} %collective-permute-done.3.refs_1_, s32[896]{0:T(1024)S(1)} %collective-permute-done.4.refs_2_, s32[896]{0:T(1024)S(1)} %collective-permute-done.5.refs_3_, bf16[1536,16,128]{2,1,0:T(8,128)(2,1)S(1)} %copy-done.10, ...), custom_call_target="tpu_custom_call" | custom-call | flops 30000001024 | bytes 10485760 | tf_op jit(solution)/shard_map/far/pallas_call | solution.py:467
  133.5 1.2 copy-done.3
  134.7 0.1 copy.23
  134.8 0.1 reshape.24
  135.0 0.9 collective-permute-start.9
  135.9 0.1 pad_add_fusion.3.ids
  136.0 1.2 copy-done.7
  137.2 20.3 %near.3 = f32[24,16,256]{2,1,0:T(8,128)S(1)} custom-call(s32[145]{0:T(256)S(1)} %pad_add_fusion.3.ids, bf16[136,8,256]{2,1,0:T(8,128)(2,1)S(1)} %get-tuple-element.14.pts, bf16[136,16,256]{2,1,0:T(8,128)(2,1)S(1)} %copy-done.7), custom_call_target="tpu_custom_call" | custom-call | flops 603979776 | bytes 4194304 | tf_op jit(solution)/shard_map/near/pallas_call | solution.py:105
  157.6 0.1 collective-permute-start.10
  157.8 1.3 collective-permute-done.10
  159.1 0.8 pad_maximum_fusion.3.near_theirs
  159.9 2.2 %copy-done.1 = bf16[128,64,256]{2,1,0:T(8,128)(2,1)S(1)} copy-done((bf16[128,64,256]{2,1,0:T(8,128)(2,1)S(1)}, bf16[128,64,256]{2,1,0:T(8,128)(2,1)}, u32[]{:S(2)}) %copy-start.1) | copy-done | bytes 4194328
  162.1 1.0 copy-done.2
  163.2 1.0 copy-done.8
  164.2 5.9 %final.1 = f32[128,8,256]{2,1,0:T(8,128)} custom-call(s32[129]{0:T(256)S(1)} %pad_add_fusion.1.counts, bf16[128,64,64]{2,1,0:T(8,128)(2,1)S(1)} %copy.27.transfer, bf16[128,64,256]{2,1,0:T(8,128)(2,1)S(1)} %copy-done.1, f32[64,16,256]{2,1,0:T(8,128)S(1)} %pad_maximum_fusion.2.near_mine, f32[64,8,256]{2,1,0:T(8,128)S(1)} %copy-done.2, f32[96,8,128]{2,1,0:T(8,128)S(1)} %bitcast.5), custom_call_target="tpu_custom_call" | custom-call | tf_op jit(solution)/shard_map/final/pallas_call | solution.py:492
  (64 shorter events, 0.5 us)
Async XLA Ops:
  6.5 4.1 %copy-start.19 = (s32[128]{0:T(128)S(1)}, s32[128]{0:T(128)}, u32[]{:S(2)}) copy-start(s32[128]{0:T(128)} %param.14) | copy-start | bytes 1540
  6.5 4.8 %copy-start.13 = (bf16[128,8,64]{0,2,1:T(8,128)(2,1)S(1)}, bf16[128,8,64]{0,2,1:T(8,128)(2,1)}, u32[]{:S(2)}) copy-start(bf16[128,8,64]{0,2,1:T(8,128)(2,1)} %param.17) | copy-start | bytes 393220
  6.5 5.0 %copy-start.12 = (bf16[128,8,256]{2,1,0:T(8,128)(2,1)S(1)}, bf16[128,8,256]{2,1,0:T(8,128)(2,1)}, u32[]{:S(2)}) copy-start(bf16[128,8,256]{2,1,0:T(8,128)(2,1)} %param.13) | copy-start | bytes 1572868
  6.5 5.9 %copy-start.9 = (bf16[64,8,64]{2,1,0:T(8,128)(2,1)S(1)}, bf16[64,8,64]{2,1,0:T(8,128)(2,1)}, u32[]{:S(2)}) copy-start(bf16[64,8,64]{2,1,0:T(8,128)(2,1)} %upper_skel.1) | copy-start | bytes 196612
  6.5 77.5 %all-gather.2.cloned.1.call-start = ((), (), s32[]{:S(2)}) async-start(), calls=%async_computation.1 | async-start | bytes 6684672 | tf_op jit(solution)/shard_map/all_gather | solution.py:319
  12.4 2.2 %copy-start = (bf16[128,64,256]{2,1,0:T(8,128)(2,1)S(1)}, bf16[128,64,256]{2,1,0:T(8,128)(2,1)}, u32[]{:S(2)}) copy-start(bf16[128,64,256]{2,1,0:T(8,128)(2,1)} %basis.3) | copy-start | bytes 12582916
  14.6 18.9 %copy-start.14 = (s32[64,8]{0,1:T(8,128)S(1)}, s32[64,8]{0,1:T(8,128)}, u32[]{:S(2)}) copy-start(s32[64,8]{0,1:T(8,128)} %param.23) | copy-start | bytes 6148
  14.6 18.9 %copy-start.15 = (s32[64,8]{0,1:T(8,128)S(1)}, s32[64,8]{0,1:T(8,128)}, u32[]{:S(2)}) copy-start(s32[64,8]{0,1:T(8,128)} %param.22) | copy-start | bytes 6148
  14.6 18.9 %copy-start.16 = (s32[128,8]{0,1:T(8,128)S(1)}, s32[128,8]{0,1:T(8,128)}, u32[]{:S(2)}) copy-start(s32[128,8]{0,1:T(8,128)} %param.21) | copy-start | bytes 12292
  14.6 18.9 %copy-start.17 = (s32[128,8]{0,1:T(8,128)S(1)}, s32[128,8]{0,1:T(8,128)}, u32[]{:S(2)}) copy-start(s32[128,8]{0,1:T(8,128)} %param.20) | copy-start | bytes 12292
  19.4 15.0 %copy-start.11 = (bf16[128,8,256]{2,1,0:T(8,128)(2,1)S(1)}, bf16[128,8,256]{2,1,0:T(8,128)(2,1)}, u32[]{:S(2)}) copy-start(bf16[128,8,256]{2,1,0:T(8,128)(2,1)} %param.12) | copy-start | bytes 1572868
  19.4 140.5 %reduce-scatter.2.cloned.1.call-start = ((), (), s32[]{:S(2)}) async-start(), calls=%async_computation.2 | async-start | bytes 1966080 | tf_op jit(solution)/shard_map/reduce_scatter | solution.py:481
  20.5 63.6 %collective-permute-start.6 = (bf16[96,8,128]{2,1,0:T(8,128)(2,1)S(1)}, bf16[96,8,128]{2,1,0:T(8,128)(2,1)}, u32[]{:S(2)}, u32[]{:S(2)}) collective-permute-start(bf16[96,8,128]{2,1,0:T(8,128)(2,1)S(1)} %slice.39.refs_5_), channel_id=1, source_target_pairs={{2,0},{4,2},{6,4},{0,6},{10,8},{12,10},{14,12},{8,14},{18,16},{20,... | collective-permute-start | bytes 589832 | tf_op jit(solution)/shard_map/ppermute | solution.py:326
  25.1 58.9 %collective-permute-start.7 = (bf16[96,8,128]{2,1,0:T(8,128)(2,1)S(1)}, bf16[96,8,128]{2,1,0:T(8,128)(2,1)}, u32[]{:S(2)}, u32[]{:S(2)}) collective-permute-start(bf16[96,8,128]{2,1,0:T(8,128)(2,1)S(1)} %slice.39.refs_5_), channel_id=1, source_target_pairs={{4,0},{6,2},{0,4},{2,6},{12,8},{14,10},{8,12},{10,14},{20,16},{22,... | collective-permute-start | bytes 589832 | tf_op jit(solution)/shard_map/ppermute | solution.py:326
  25.1 58.9 %collective-permute-start.8 = (bf16[96,8,128]{2,1,0:T(8,128)(2,1)S(1)}, bf16[96,8,128]{2,1,0:T(8,128)(2,1)}, u32[]{:S(2)}, u32[]{:S(2)}) collective-permute-start(bf16[96,8,128]{2,1,0:T(8,128)(2,1)S(1)} %slice.39.refs_5_), channel_id=1, source_target_pairs={{6,0},{0,2},{2,4},{4,6},{14,8},{8,10},{10,12},{12,14},{22,16},{16,... | collective-permute-start | bytes 589832 | tf_op jit(solution)/shard_map/ppermute | solution.py:326
  27.2 7.2 %collective-permute-start.1 = (bf16[4,16,256]{2,1,0:T(8,128)(2,1)}, bf16[4,16,256]{2,1,0:T(8,128)(2,1)S(1)}, u32[]{:S(2)}, u32[]{:S(2)}) collective-permute-start(bf16[4,16,256]{2,1,0:T(8,128)(2,1)} %get-tuple-element.16), channel_id=1, source_target_pairs={{2,0},{4,2},{6,4},{8,6},{10,8},{12,10},{14,12},{16,14},{18,16},{20... | collective-permute-start | bytes 98312 | tf_op jit(solution)/shard_map/ppermute | solution.py:134
  28.5 5.9 %collective-permute-start = (bf16[4,16,256]{2,1,0:T(8,128)(2,1)S(1)}, bf16[4,16,256]{2,1,0:T(8,128)(2,1)S(1)}, u32[]{:S(2)}, u32[]{:S(2)}) collective-permute-start(bf16[4,16,256]{2,1,0:T(8,128)(2,1)S(1)} %get-tuple-element.15), channel_id=1, source_target_pairs={{0,2},{2,4},{4,6},{6,8},{8,10},{10,12},{12,14},{14,16},{16,18},{18... | collective-permute-start | bytes 98312 | tf_op jit(solution)/shard_map/ppermute | solution.py:132
  34.3 2.3 %copy-start.20 = (pred[8]{0:T(512)(128)(4,1)S(1)}, pred[8]{0:T(512)(128)(4,1)}, u32[]{:S(2)}) copy-start(pred[8]{0:T(512)(128)(4,1)} %iota_compare_fusion.1) | copy-start | bytes 28
  34.3 2.3 %copy-start.21 = (s32[8]{0:T(128)S(1)}, s32[8]{0:T(128)}, u32[]{:S(2)}) copy-start(s32[8]{0:T(128)} %compare_select_fusion) | copy-start | bytes 100
  34.3 7.4 %copy-start.18 = (s32[128,6]{0,1:T(8,128)S(1)}, s32[128,6]{0,1:T(8,128)}, u32[]{:S(2)}) copy-start(s32[128,6]{0,1:T(8,128)} %param.19) | copy-start | bytes 9220
  34.6 7.6 %collective-permute-start.2 = (bf16[136,8,256]{2,1,0:T(8,128)(2,1)S(1)}, bf16[136,8,256]{2,1,0:T(8,128)(2,1)}, u32[]{:S(2)}, u32[]{:S(2)}) collective-permute-start(bf16[136,8,256]{2,1,0:T(8,128)(2,1)S(1)} %get-tuple-element.13), channel_id=1, source_target_pairs={{0,1},{1,0},{2,3},{3,2},{4,5},{5,4},{6,7},{7,6},{8,9},{9,8},{10,11... | collective-permute-start | bytes 1671176 | tf_op jit(solution)/shard_map/ppermute | solution.py:452
  38.1 5.8 %collective-permute-start.3 = (s32[896]{0:T(1024)S(1)}, s32[896]{0:T(1024)S(1)}, u32[]{:S(2)}, u32[]{:S(2)}) collective-permute-start(s32[896]{0:T(1024)S(1)} %get-tuple-element.11), channel_id=1, source_target_pairs={{2,0},{4,2},{6,4},{0,6},{10,8},{12,10},{14,12},{8,14},{18,16},{20,... | collective-permute-start | bytes 10760 | tf_op jit(solution)/shard_map/ppermute | solution.py:326
  42.1 41.9 %collective-permute-start.4 = (s32[896]{0:T(1024)S(1)}, s32[896]{0:T(1024)S(1)}, u32[]{:S(2)}, u32[]{:S(2)}) collective-permute-start(s32[896]{0:T(1024)S(1)} %get-tuple-element.10), channel_id=1, source_target_pairs={{4,0},{6,2},{0,4},{2,6},{12,8},{14,10},{8,12},{10,14},{20,16},{22,... | collective-permute-start | bytes 10760 | tf_op jit(solution)/shard_map/ppermute | solution.py:326
  43.9 40.2 %collective-permute-start.5 = (s32[896]{0:T(1024)S(1)}, s32[896]{0:T(1024)S(1)}, u32[]{:S(2)}, u32[]{:S(2)}) collective-permute-start(s32[896]{0:T(1024)S(1)} %get-tuple-element.9), channel_id=1, source_target_pairs={{6,0},{0,2},{2,4},{4,6},{14,8},{8,10},{10,12},{12,14},{22,16},{16,... | collective-permute-start | bytes 10760 | tf_op jit(solution)/shard_map/ppermute | solution.py:326
  75.3 1.0 copy-start.6
  76.3 58.6 %copy-start.4 = (f32[40,16,256]{2,1,0:T(8,128)}, f32[40,16,256]{2,1,0:T(8,128)S(1)}, u32[]{:S(2)}) copy-start(f32[40,16,256]{2,1,0:T(8,128)S(1)} %near.2) | copy-start | bytes 1966084
  84.1 2.8 %copy-start.10 = (bf16[1536,16,128]{2,1,0:T(8,128)(2,1)S(1)}, bf16[1536,16,128]{2,1,0:T(8,128)(2,1)}, u32[]{:S(2)}) copy-start(bf16[1536,16,128]{2,1,0:T(8,128)(2,1)} %all-gather.2.cloned.1.call-done.refs_4_) | copy-start | bytes 18874372
  133.5 1.2 copy-start.3
  135.0 22.8 %copy-start.5 = (f32[40,16,256]{2,1,0:T(8,128)S(1)}, f32[40,16,256]{2,1,0:T(8,128)}, u32[]{:S(2)}) copy-start(f32[40,16,256]{2,1,0:T(8,128)} %copy-done.4) | copy-start | bytes 1966084
  135.0 22.8 %collective-permute-start.9 = (f32[40,8,256]{2,1,0:T(8,128)S(1)}, f32[40,8,256]{2,1,0:T(8,128)S(1)}, u32[]{:S(2)}, u32[]{:S(2)}) collective-permute-start(f32[40,8,256]{2,1,0:T(8,128)S(1)} %slice.40), channel_id=1, source_target_pairs={{0,1},{1,0},{2,3},{3,2},{4,5},{5,4},{6,7},{7,6},{8,9},{9,8},{10,11... | collective-permute-start | bytes 983048 | tf_op jit(solution)/shard_map/ppermute | solution.py:464
  136.0 1.2 copy-start.7
  157.6 1.5 collective-permute-start.10
  159.9 2.2 %copy-start.1 = (bf16[128,64,256]{2,1,0:T(8,128)(2,1)S(1)}, bf16[128,64,256]{2,1,0:T(8,128)(2,1)}, u32[]{:S(2)}) copy-start(bf16[128,64,256]{2,1,0:T(8,128)(2,1)} %basis.3) | copy-start | bytes 12582916
  162.1 1.0 copy-start.2
  163.2 1.0 copy-start.8
Sparse Core Ops, SparseCore 0:
  19.6 64.4 all-gather.1
  134.8 22.5 reduce-scatter.1

commit v7 on v5

--- a/solution.py
+++ b/solution.py
@@ -181,10 +181,8 @@
 
 
 def far_kernel(units, *refs):
-    lists, gathered, skels = refs[:4], refs[4], refs[5:9]
-    outs, table, sums, sem = refs[9:]
-    copy = pltpu.make_async_copy(gathered, table, sem)
-    copy.start()
+    lists, table, skels = refs[:4], refs[4], refs[5:9]
+    outs, *sums = refs[9:]
     targets = 2 * skels[0].shape[0]
     rank = skels[0].shape[2] // 2
     lane = lax.broadcasted_iota(jnp.int32, (DIM, 2 * rank), 1)
@@ -192,11 +190,11 @@
 
     def clear(i, carry):
         for n in range(4):
-            sums[i * 4 + n] = jnp.zeros(sums.shape[1:], F32)
+            for one in sums:
+                one[i * 4 + n] = jnp.zeros(one.shape[1:], F32)
         return carry
 
-    lax.fori_loop(0, sums.shape[0] // 4, clear, 0)
-    copy.wait()
+    lax.fori_loop(0, sums[0].shape[0] // 4, clear, 0)
 
     def turned(array):
         return jnp.concatenate([array[:, rank:], array[:, :rank]], axis=1)
@@ -247,7 +245,7 @@
             ]
             for n in range(units):
                 at = DIM * (n % 4)
-                sums[where[n]] += fields[n // 4][at : at + DIM]
+                sums[n % len(sums)][where[n]] += fields[n // 4][at : at + DIM]
             return carry
 
         count = listed[listed.shape[0] - 128]
@@ -257,7 +255,8 @@
         def pack(k, carry):
             for n in range(8):
                 p = k * 8 + n
-                both = [sums[first + 2 * p], sums[first + 2 * p + 1]]
+                spots = [first + 2 * p, first + 2 * p + 1]
+                both = [(sums[0][q] + sums[1][q]) + (sums[2][q] + sums[3][q]) for q in spots]
                 outs[origin, p] = jnp.concatenate(both, axis=1)
             return carry
 
@@ -422,7 +421,6 @@
     swap = [(0, 1), (1, 0)]
     vmem = pl.BlockSpec(memory_space=pltpu.VMEM)
     smem = pl.BlockSpec(memory_space=pltpu.SMEM)
-    anywhere = pl.BlockSpec(memory_space=pl.ANY)
     params = pltpu.CompilerParams(vmem_limit_bytes=40 * 2**20)
 
     point_live = lax.broadcasted_iota(jnp.int32, (leaf_dev, leaf_size), 1) < counts[:, None]
@@ -462,14 +460,12 @@
     gathered, _ = lax.optimization_barrier((gathered, near_first))
 
     parts = pl.pallas_call(
-        functools.partial(far_kernel, 32),
+        functools.partial(far_kernel, 64),
         out_shape=jax.ShapeDtypeStruct((SIDE, pairs, columns, 2 * rank), F32),
-        in_specs=[smem] * 4 + [anywhere] + [vmem] * 4,
+        in_specs=[smem] * 4 + [vmem] * 5,
         out_specs=vmem,
         scratch_shapes=[
-            pltpu.VMEM((SIDE * SIDE * pairs, 2 * DIM, 2 * rank), BF16),
-            pltpu.VMEM((SIDE * (2 * pairs + 1), columns, rank), F32),
-            pltpu.SemaphoreType.DMA,
+            pltpu.VMEM((SIDE * (2 * pairs + 1), columns, rank), F32) for _ in range(4)
         ],
         compiler_params=params,
         cost_estimate=pl.CostEstimate(

time: 173 us -> 169 us (0.977)
  waiting for transfers between devices: 12.2 us -> 9.11 us
    reduce_scatter x1, waiting for transfers between devices: 3.09 us -> 0.01 us  [body(): lax.psum_scatter(parts, 'leaf', scatter_dimension=0, axis_index_groups=li...]
  transfers between devices with their start and end apart: 13 -> 13, of which waited for: 3 -> 2; matrix products, arithmetic and copies ran while one was open for 4% -> 4% of each run, Pallas kernels for 30% -> 31%
where the time goes in v7:
time: 169 us
  Pallas kernels  101 us (60%)
  starting transfers between devices  19.2 us (11%)
  local copies, waits for them, and re-layouts  18.7 us (11%)
  between operations  13.8 us (8%)
  waiting for transfers between devices  9.11 us (5%)
  other arithmetic  6.36 us (4%)
    pallas_call x2, Pallas kernels, near_field(): pl.pallas_call(functools.partial(near_kernel, near, leaves), out_shape=ja...  50.9 us
    pallas_call x1, Pallas kernels, body(): pl.pallas_call(functools.partial(far_kernel, 64), out_shape=jax.ShapeDtyp...  38.5 us
    unnamed x46, local copies, waits for them, and re-layouts  16.8 us
    ppermute x6, starting transfers between devices, line_shift(): return lax.ppermute(block, 'leaf', pairs)  10.5 us
    all_gather x1, waiting for transfers between devices, plane_gather(): return lax.all_gather(block, 'leaf', axis_index_groups=groups, tiled=True)  7.75 us
    pallas_call x1, Pallas kernels, body(): pl.pallas_call(final_kernel, out_shape=jax.ShapeDtypeStruct((leaf_dev, co...  5.86 us
    pallas_call x1, Pallas kernels, body(): pl.pallas_call(coef_kernel, out_shape=jax.ShapeDtypeStruct((pairs, 2 * DI...  4.78 us
    ppermute x1, starting transfers between devices, with_halo(): lax.ppermute(tail, axis, [(i, (i + 1) % count) for i in range(ends)])  4.48 us
  transfers between devices with their start and end apart: 13, of which 2 were waited for; matrix products, arithmetic and copies ran while one was open for 4% of the time, Pallas kernels for 31%

profile of v7, /device:TPU:1, one launch (start us, length us, event | category | flops | bytes accessed | tf_op | source)
XLA Modules:
  0.0 168.6 jit_solution(17063757543370243919)
XLA Ops:
  6.6 4.0 %copy.27.transfer = bf16[128,64,64]{2,1,0:T(8,128)(2,1)S(1)} copy(bf16[128,64,64]{0,2,1:T(8,128)(2,1)} %param.16) | data formatting | bytes 2097152 | tf_op args[4]
  10.6 0.7 iota_compare_fusion
  11.3 0.2 copy.26.leaf_skel
  11.5 0.9 broadcast_select_fusion.values
  12.4 2.2 %copy-done = bf16[128,64,256]{2,1,0:T(8,128)(2,1)S(1)} copy-done((bf16[128,64,256]{2,1,0:T(8,128)(2,1)S(1)}, bf16[128,64,256]{2,1,0:T(8,128)(2,1)}, u32[]{:S(2)}) %copy-start) | copy-done | bytes 4194328
  14.6 4.8 %coef.1 = bf16[96,16,128]{2,1,0:T(8,128)(2,1)} custom-call(bf16[128,8,256]{2,1,0:T(8,128)(2,1)S(1)} %broadcast_select_fusion.values, bf16[128,64,256]{2,1,0:T(8,128)(2,1)S(1)} %copy-done, bf16[128,64,64]{2,1,0:T(8,128)(2,1)S(1)} %copy.27.transfer, bf16[128,8,64]{2,1,0:T(8,128)(2,1)S(1)} %copy.26.leaf_skel, bf16[64,8,64]{2,1,0:T(8,128)(2,1)S(1)} %copy-done.9), custom_call_target="tpu_custom_call" | custom-call | flops 100000000 | bytes 6291456 | tf_op jit(solution)/shard_map/coef/pallas_call | solution.py:428
  19.5 1.0 slice.39.refs_5_
  20.5 4.7 %collective-permute-start.6 = (bf16[96,8,128]{2,1,0:T(8,128)(2,1)S(1)}, bf16[96,8,128]{2,1,0:T(8,128)(2,1)}, u32[]{:S(2)}, u32[]{:S(2)}) collective-permute-start(bf16[96,8,128]{2,1,0:T(8,128)(2,1)S(1)} %slice.39.refs_5_), channel_id=1, source_target_pairs={{2,0},{4,2},{6,4},{0,6},{10,8},{12,10},{14,12},{8,14},{18,16},{20,... | collective-permute-start | bytes 589832 | tf_op jit(solution)/shard_map/ppermute | solution.py:321
  25.1 0.7 collective-permute-start.8
  25.8 1.4 pad_maximum_fusion.5
  27.2 1.3 collective-permute-start.1
  28.5 4.5 %collective-permute-start = (bf16[4,16,256]{2,1,0:T(8,128)(2,1)S(1)}, bf16[4,16,256]{2,1,0:T(8,128)(2,1)S(1)}, u32[]{:S(2)}, u32[]{:S(2)}) collective-permute-start(bf16[4,16,256]{2,1,0:T(8,128)(2,1)S(1)} %get-tuple-element.15), channel_id=1, source_target_pairs={{0,2},{2,4},{4,6},{6,8},{8,10},{10,12},{12,14},{14,16},{16,18},{18... | collective-permute-start | bytes 98312 | tf_op jit(solution)/shard_map/ppermute | solution.py:132
  33.0 0.5 iota_compare_fusion.1
  33.6 0.5 compare_select_fusion
  34.1 0.1 copy.24
  34.2 0.1 broadcast_in_dim.45
  34.4 0.1 pad_maximum_fusion
  34.5 0.1 fusion.27
  34.6 2.0 %collective-permute-start.2 = (bf16[136,8,256]{2,1,0:T(8,128)(2,1)S(1)}, bf16[136,8,256]{2,1,0:T(8,128)(2,1)}, u32[]{:S(2)}, u32[]{:S(2)}) collective-permute-start(bf16[136,8,256]{2,1,0:T(8,128)(2,1)S(1)} %get-tuple-element.13), channel_id=1, source_target_pairs={{0,1},{1,0},{2,3},{3,2},{4,5},{5,4},{6,7},{7,6},{8,9},{9,8},{10,11... | collective-permute-start | bytes 1671176 | tf_op jit(solution)/shard_map/ppermute | solution.py:447
  36.6 0.1 broadcast_select_fusion.1.codes
  36.7 1.3 lists.1
  38.1 3.7 %collective-permute-start.3 = (s32[896]{0:T(1024)S(1)}, s32[896]{0:T(1024)S(1)}, u32[]{:S(2)}, u32[]{:S(2)}) collective-permute-start(s32[896]{0:T(1024)S(1)} %get-tuple-element.11), channel_id=1, source_target_pairs={{2,0},{4,2},{6,4},{0,6},{10,8},{12,10},{14,12},{8,14},{18,16},{20,... | collective-permute-start | bytes 10760 | tf_op jit(solution)/shard_map/ppermute | solution.py:321
  41.8 0.1 constant_dynamic-slice_fusion
  41.8 0.1 copy.22
  41.9 0.1 reshape.23
  42.0 0.1 pad_add_fusion.2.ids
  42.1 0.6 collective-permute-start.4
  42.7 1.1 pad_maximum_fusion.1.cols
  43.9 0.9 collective-permute-start.5
  44.7 30.6 %near.2 = f32[40,16,256]{2,1,0:T(8,128)S(1)} custom-call(s32[241]{0:T(256)S(1)} %pad_add_fusion.2.ids, bf16[136,8,256]{2,1,0:T(8,128)(2,1)S(1)} %get-tuple-element.14.pts, bf16[136,16,256]{2,1,0:T(8,128)(2,1)S(1)} %pad_maximum_fusion.1.cols), custom_call_target="tpu_custom_call" | custom-call | flops 1006632960 | bytes 4194304 | tf_op jit(solution)/shard_map/near/pallas_call | solution.py:105
  75.3 1.0 copy-done.6
  76.3 7.8 %all-gather.2.cloned.1.call-done.refs_4_ = bf16[1536,16,128]{2,1,0:T(8,128)(2,1)} async-done(((bf16[96,16,128]{2,1,0:T(8,128)(2,1)}), bf16[1536,16,128]{2,1,0:T(8,128)(2,1)}) %all-gather.2.cloned.1.call-update) | async-done | bytes 6291472 | tf_op jit(solution)/shard_map/all_gather | solution.py:314
  84.1 2.8 %copy-done.10 = bf16[1536,16,128]{2,1,0:T(8,128)(2,1)S(1)} copy-done((bf16[1536,16,128]{2,1,0:T(8,128)(2,1)S(1)}, bf16[1536,16,128]{2,1,0:T(8,128)(2,1)}, u32[]{:S(2)}) %copy-start.10) | copy-done | bytes 6291480
  86.9 38.5 %far.1 = f32[4,96,8,128]{3,2,1,0:T(8,128)S(1)} custom-call(s32[896]{0:T(1024)S(1)} %get-tuple-element.12.refs_0_, s32[896]{0:T(1024)S(1)} %collective-permute-done.3.refs_1_, s32[896]{0:T(1024)S(1)} %collective-permute-done.4.refs_2_, s32[896]{0:T(1024)S(1)} %collective-permute-done.5.refs_3_, bf16[1536,16,128]{2,1,0:T(8,128)(2,1)S(1)} %copy-done.10, ...), custom_call_target="tpu_custom_call" | custom-call | flops 30000001024 | bytes 10485760 | tf_op jit(solution)/shard_map/far/pallas_call | solution.py:462
  125.4 1.2 copy-done.3
  126.7 0.1 copy.23
  126.8 0.1 reshape.24
  126.9 0.8 collective-permute-start.9
  127.7 0.1 pad_add_fusion.3.ids
  127.7 1.2 copy-done.7
  129.0 20.3 %near.3 = f32[24,16,256]{2,1,0:T(8,128)S(1)} custom-call(s32[145]{0:T(256)S(1)} %pad_add_fusion.3.ids, bf16[136,8,256]{2,1,0:T(8,128)(2,1)S(1)} %get-tuple-element.14.pts, bf16[136,16,256]{2,1,0:T(8,128)(2,1)S(1)} %copy-done.7), custom_call_target="tpu_custom_call" | custom-call | flops 603979776 | bytes 4194304 | tf_op jit(solution)/shard_map/near/pallas_call | solution.py:105
  149.4 0.1 collective-permute-start.10
  149.6 1.3 collective-permute-done.10
  150.9 0.8 pad_maximum_fusion.3.near_theirs
  151.7 2.2 %copy-done.1 = bf16[128,64,256]{2,1,0:T(8,128)(2,1)S(1)} copy-done((bf16[128,64,256]{2,1,0:T(8,128)(2,1)S(1)}, bf16[128,64,256]{2,1,0:T(8,128)(2,1)}, u32[]{:S(2)}) %copy-start.1) | copy-done | bytes 4194328
  153.9 1.0 copy-done.2
  155.0 1.0 copy-done.8
  156.0 5.9 %final.1 = f32[128,8,256]{2,1,0:T(8,128)} custom-call(s32[129]{0:T(256)S(1)} %pad_add_fusion.1.counts, bf16[128,64,64]{2,1,0:T(8,128)(2,1)S(1)} %copy.27.transfer, bf16[128,64,256]{2,1,0:T(8,128)(2,1)S(1)} %copy-done.1, f32[64,16,256]{2,1,0:T(8,128)S(1)} %pad_maximum_fusion.2.near_mine, f32[64,8,256]{2,1,0:T(8,128)S(1)} %copy-done.2, f32[96,8,128]{2,1,0:T(8,128)S(1)} %bitcast.5), custom_call_target="tpu_custom_call" | custom-call | tf_op jit(solution)/shard_map/final/pallas_call | solution.py:487
  (64 shorter events, 0.5 us)
Async XLA Ops:
  6.5 4.1 %copy-start.19 = (s32[128]{0:T(128)S(1)}, s32[128]{0:T(128)}, u32[]{:S(2)}) copy-start(s32[128]{0:T(128)} %param.14) | copy-start | bytes 1540
  6.5 4.8 %copy-start.13 = (bf16[128,8,64]{0,2,1:T(8,128)(2,1)S(1)}, bf16[128,8,64]{0,2,1:T(8,128)(2,1)}, u32[]{:S(2)}) copy-start(bf16[128,8,64]{0,2,1:T(8,128)(2,1)} %param.17) | copy-start | bytes 393220
  6.5 5.0 %copy-start.12 = (bf16[128,8,256]{2,1,0:T(8,128)(2,1)S(1)}, bf16[128,8,256]{2,1,0:T(8,128)(2,1)}, u32[]{:S(2)}) copy-start(bf16[128,8,256]{2,1,0:T(8,128)(2,1)} %param.13) | copy-start | bytes 1572868
  6.5 5.9 %copy-start.9 = (bf16[64,8,64]{2,1,0:T(8,128)(2,1)S(1)}, bf16[64,8,64]{2,1,0:T(8,128)(2,1)}, u32[]{:S(2)}) copy-start(bf16[64,8,64]{2,1,0:T(8,128)(2,1)} %upper_skel.1) | copy-start | bytes 196612
  6.5 77.5 %all-gather.2.cloned.1.call-start = ((), (), s32[]{:S(2)}) async-start(), calls=%async_computation.1 | async-start | bytes 6684672 | tf_op jit(solution)/shard_map/all_gather | solution.py:314
  12.4 2.2 %copy-start = (bf16[128,64,256]{2,1,0:T(8,128)(2,1)S(1)}, bf16[128,64,256]{2,1,0:T(8,128)(2,1)}, u32[]{:S(2)}) copy-start(bf16[128,64,256]{2,1,0:T(8,128)(2,1)} %basis.3) | copy-start | bytes 12582916
  14.6 18.9 %copy-start.14 = (s32[64,8]{0,1:T(8,128)S(1)}, s32[64,8]{0,1:T(8,128)}, u32[]{:S(2)}) copy-start(s32[64,8]{0,1:T(8,128)} %param.23) | copy-start | bytes 6148
  14.6 18.9 %copy-start.15 = (s32[64,8]{0,1:T(8,128)S(1)}, s32[64,8]{0,1:T(8,128)}, u32[]{:S(2)}) copy-start(s32[64,8]{0,1:T(8,128)} %param.22) | copy-start | bytes 6148
  14.6 18.9 %copy-start.16 = (s32[128,8]{0,1:T(8,128)S(1)}, s32[128,8]{0,1:T(8,128)}, u32[]{:S(2)}) copy-start(s32[128,8]{0,1:T(8,128)} %param.21) | copy-start | bytes 12292
  14.6 18.9 %copy-start.17 = (s32[128,8]{0,1:T(8,128)S(1)}, s32[128,8]{0,1:T(8,128)}, u32[]{:S(2)}) copy-start(s32[128,8]{0,1:T(8,128)} %param.20) | copy-start | bytes 12292
  19.4 15.0 %copy-start.11 = (bf16[128,8,256]{2,1,0:T(8,128)(2,1)S(1)}, bf16[128,8,256]{2,1,0:T(8,128)(2,1)}, u32[]{:S(2)}) copy-start(bf16[128,8,256]{2,1,0:T(8,128)(2,1)} %param.12) | copy-start | bytes 1572868
  19.4 132.3 %reduce-scatter.2.cloned.1.call-start = ((), (), s32[]{:S(2)}) async-start(), calls=%async_computation.2 | async-start | bytes 1966080 | tf_op jit(solution)/shard_map/reduce_scatter | solution.py:476
  20.5 63.6 %collective-permute-start.6 = (bf16[96,8,128]{2,1,0:T(8,128)(2,1)S(1)}, bf16[96,8,128]{2,1,0:T(8,128)(2,1)}, u32[]{:S(2)}, u32[]{:S(2)}) collective-permute-start(bf16[96,8,128]{2,1,0:T(8,128)(2,1)S(1)} %slice.39.refs_5_), channel_id=1, source_target_pairs={{2,0},{4,2},{6,4},{0,6},{10,8},{12,10},{14,12},{8,14},{18,16},{20,... | collective-permute-start | bytes 589832 | tf_op jit(solution)/shard_map/ppermute | solution.py:321
  25.1 58.9 %collective-permute-start.7 = (bf16[96,8,128]{2,1,0:T(8,128)(2,1)S(1)}, bf16[96,8,128]{2,1,0:T(8,128)(2,1)}, u32[]{:S(2)}, u32[]{:S(2)}) collective-permute-start(bf16[96,8,128]{2,1,0:T(8,128)(2,1)S(1)} %slice.39.refs_5_), channel_id=1, source_target_pairs={{4,0},{6,2},{0,4},{2,6},{12,8},{14,10},{8,12},{10,14},{20,16},{22,... | collective-permute-start | bytes 589832 | tf_op jit(solution)/shard_map/ppermute | solution.py:321
  25.1 58.9 %collective-permute-start.8 = (bf16[96,8,128]{2,1,0:T(8,128)(2,1)S(1)}, bf16[96,8,128]{2,1,0:T(8,128)(2,1)}, u32[]{:S(2)}, u32[]{:S(2)}) collective-permute-start(bf16[96,8,128]{2,1,0:T(8,128)(2,1)S(1)} %slice.39.refs_5_), channel_id=1, source_target_pairs={{6,0},{0,2},{2,4},{4,6},{14,8},{8,10},{10,12},{12,14},{22,16},{16,... | collective-permute-start | bytes 589832 | tf_op jit(solution)/shard_map/ppermute | solution.py:321
  27.2 7.2 %collective-permute-start.1 = (bf16[4,16,256]{2,1,0:T(8,128)(2,1)}, bf16[4,16,256]{2,1,0:T(8,128)(2,1)S(1)}, u32[]{:S(2)}, u32[]{:S(2)}) collective-permute-start(bf16[4,16,256]{2,1,0:T(8,128)(2,1)} %get-tuple-element.16), channel_id=1, source_target_pairs={{2,0},{4,2},{6,4},{8,6},{10,8},{12,10},{14,12},{16,14},{18,16},{20... | collective-permute-start | bytes 98312 | tf_op jit(solution)/shard_map/ppermute | solution.py:134
  28.5 5.9 %collective-permute-start = (bf16[4,16,256]{2,1,0:T(8,128)(2,1)S(1)}, bf16[4,16,256]{2,1,0:T(8,128)(2,1)S(1)}, u32[]{:S(2)}, u32[]{:S(2)}) collective-permute-start(bf16[4,16,256]{2,1,0:T(8,128)(2,1)S(1)} %get-tuple-element.15), channel_id=1, source_target_pairs={{0,2},{2,4},{4,6},{6,8},{8,10},{10,12},{12,14},{14,16},{16,18},{18... | collective-permute-start | bytes 98312 | tf_op jit(solution)/shard_map/ppermute | solution.py:132
  34.3 2.3 %copy-start.20 = (pred[8]{0:T(512)(128)(4,1)S(1)}, pred[8]{0:T(512)(128)(4,1)}, u32[]{:S(2)}) copy-start(pred[8]{0:T(512)(128)(4,1)} %iota_compare_fusion.1) | copy-start | bytes 28
  34.3 2.3 %copy-start.21 = (s32[8]{0:T(128)S(1)}, s32[8]{0:T(128)}, u32[]{:S(2)}) copy-start(s32[8]{0:T(128)} %compare_select_fusion) | copy-start | bytes 100
  34.3 7.4 %copy-start.18 = (s32[128,6]{0,1:T(8,128)S(1)}, s32[128,6]{0,1:T(8,128)}, u32[]{:S(2)}) copy-start(s32[128,6]{0,1:T(8,128)} %param.19) | copy-start | bytes 9220
  34.6 7.6 %collective-permute-start.2 = (bf16[136,8,256]{2,1,0:T(8,128)(2,1)S(1)}, bf16[136,8,256]{2,1,0:T(8,128)(2,1)}, u32[]{:S(2)}, u32[]{:S(2)}) collective-permute-start(bf16[136,8,256]{2,1,0:T(8,128)(2,1)S(1)} %get-tuple-element.13), channel_id=1, source_target_pairs={{0,1},{1,0},{2,3},{3,2},{4,5},{5,4},{6,7},{7,6},{8,9},{9,8},{10,11... | collective-permute-start | bytes 1671176 | tf_op jit(solution)/shard_map/ppermute | solution.py:447
  38.1 5.8 %collective-permute-start.3 = (s32[896]{0:T(1024)S(1)}, s32[896]{0:T(1024)S(1)}, u32[]{:S(2)}, u32[]{:S(2)}) collective-permute-start(s32[896]{0:T(1024)S(1)} %get-tuple-element.11), channel_id=1, source_target_pairs={{2,0},{4,2},{6,4},{0,6},{10,8},{12,10},{14,12},{8,14},{18,16},{20,... | collective-permute-start | bytes 10760 | tf_op jit(solution)/shard_map/ppermute | solution.py:321
  42.1 41.9 %collective-permute-start.4 = (s32[896]{0:T(1024)S(1)}, s32[896]{0:T(1024)S(1)}, u32[]{:S(2)}, u32[]{:S(2)}) collective-permute-start(s32[896]{0:T(1024)S(1)} %get-tuple-element.10), channel_id=1, source_target_pairs={{4,0},{6,2},{0,4},{2,6},{12,8},{14,10},{8,12},{10,14},{20,16},{22,... | collective-permute-start | bytes 10760 | tf_op jit(solution)/shard_map/ppermute | solution.py:321
  43.9 40.2 %collective-permute-start.5 = (s32[896]{0:T(1024)S(1)}, s32[896]{0:T(1024)S(1)}, u32[]{:S(2)}, u32[]{:S(2)}) collective-permute-start(s32[896]{0:T(1024)S(1)} %get-tuple-element.9), channel_id=1, source_target_pairs={{6,0},{0,2},{2,4},{4,6},{14,8},{8,10},{10,12},{12,14},{22,16},{16,... | collective-permute-start | bytes 10760 | tf_op jit(solution)/shard_map/ppermute | solution.py:321
  75.3 1.0 copy-start.6
  76.3 50.6 %copy-start.4 = (f32[40,16,256]{2,1,0:T(8,128)}, f32[40,16,256]{2,1,0:T(8,128)S(1)}, u32[]{:S(2)}) copy-start(f32[40,16,256]{2,1,0:T(8,128)S(1)} %near.2) | copy-start | bytes 1966084
  84.1 2.8 %copy-start.10 = (bf16[1536,16,128]{2,1,0:T(8,128)(2,1)S(1)}, bf16[1536,16,128]{2,1,0:T(8,128)(2,1)}, u32[]{:S(2)}) copy-start(bf16[1536,16,128]{2,1,0:T(8,128)(2,1)} %all-gather.2.cloned.1.call-done.refs_4_) | copy-start | bytes 18874372
  125.4 1.2 copy-start.3
  126.9 22.6 %copy-start.5 = (f32[40,16,256]{2,1,0:T(8,128)S(1)}, f32[40,16,256]{2,1,0:T(8,128)}, u32[]{:S(2)}) copy-start(f32[40,16,256]{2,1,0:T(8,128)} %copy-done.4) | copy-start | bytes 1966084
  126.9 22.7 %collective-permute-start.9 = (f32[40,8,256]{2,1,0:T(8,128)S(1)}, f32[40,8,256]{2,1,0:T(8,128)S(1)}, u32[]{:S(2)}, u32[]{:S(2)}) collective-permute-start(f32[40,8,256]{2,1,0:T(8,128)S(1)} %slice.40), channel_id=1, source_target_pairs={{0,1},{1,0},{2,3},{3,2},{4,5},{5,4},{6,7},{7,6},{8,9},{9,8},{10,11... | collective-permute-start | bytes 983048 | tf_op jit(solution)/shard_map/ppermute | solution.py:459
  127.7 1.2 copy-start.7
  149.4 1.5 collective-permute-start.10
  151.7 2.2 %copy-start.1 = (bf16[128,64,256]{2,1,0:T(8,128)(2,1)S(1)}, bf16[128,64,256]{2,1,0:T(8,128)(2,1)}, u32[]{:S(2)}) copy-start(bf16[128,64,256]{2,1,0:T(8,128)(2,1)} %basis.3) | copy-start | bytes 12582916
  153.9 1.0 copy-start.2
  155.0 1.0 copy-start.8
Sparse Core Ops, SparseCore 0:
  19.6 64.4 all-gather.1
  126.7 24.5 reduce-scatter.1
